TPU v7x, 32 devices: a whole 2x2x4 slice. The times are simulated.
32 devices in a mesh: space: 8 (over y, x, core), chaos: 4 (over z).
Axes of the slice: x: 2, y: 2, z: 4, core: 2. Of those that a mesh axis runs over, the one named last changes fastest.
Arguments:
- forcing: float32 [288, 128, 128], P('chaos', 'space'), may hold values from -12 to 12, as said below
- start_guess: float32 [288, 128, 128], P('chaos', 'space'), may hold values from -2 to 2, as said below
- mean_field: float32 [128, 128], P('space'), may hold values from 1 to 2
- mode_fields: float32 [10, 128, 128], P(None, 'space'), may hold values from -0.04 to 0.04
- multi_index: int32 [288, 10], P('chaos'), may hold values from -1 to 3, as said below
- coupled_slot: int32 [288, 20], P('chaos'), may hold values from 0 to 288, as said below
Outputs:
- approximation: float32 [288, 128, 128], P('chaos', 'space')
- recursive_residual: float32 [288, 128, 128], P('chaos', 'space')
Inputs may be any that keep to these rules, and one draw needn't show every extreme that they name: `multi_index`: row s is the multi-index of the chaos term placed in slot s: 10 nonnegative entries summing to at most 3, each such multi-index in exactly one slot; the slots without a term hold -1 in every entry. `coupled_slot`: entry (s, k) for k < 10 is the slot whose multi-index is that of slot s with one more in mode k, entry (s, 10 + k) the slot with one less in mode k; 288 where no such term exists or slot s holds no term. `forcing`: zero in the slots that hold no term. `start_guess`: zero in the slots that hold no term.
All inputs are finite; a program needn't handle non-finite values.
Results may differ from a plain program's by a relative error of at most 0.0003.
Values sent between devices are 32-bit elements; how exact they have to be, the bound alone decides.
No kernel may reach another device: no remote copies, remote signals or barrier semaphores. Data moves between devices by JAX's collectives and lax.ppermute only.
A program may use at most 128 MiB of HBM per device.

v0:
```python
import jax
import jax.numpy as jnp
from jax import lax
from jax.sharding import PartitionSpec as P

ITERS = 2


def with_halo(value, sides, width):
    for axis, dim in sides:
        size, length = (lax.axis_size(axis), value.shape[dim])
        up = [(i, (i + 1) % size) for i in range(size - 1)]
        down = [(j, i) for i, j in up]
        last = lax.slice_in_dim(value, length - width, length, axis=dim)
        first = lax.slice_in_dim(value, 0, width, axis=dim)
        before = lax.ppermute(last, axis, up)
        after = lax.ppermute(first, axis, down)
        value = jnp.concatenate([before, value, after], axis=dim)
    return value


def stencil(values, coeffs):
    col_faces = 0.5 * (coeffs[1:] + coeffs[:-1])
    col_flux = col_faces * (values[:, 1:] - values[:, :-1])
    across = col_flux[:, :-1] - col_flux[:, 1:]
    inner_coef = jnp.pad(coeffs[1:-1], ((0, 0), (1, 1)))
    inner_vals = jnp.pad(values[:, 1:-1], ((0, 0), (0, 0), (1, 1)))
    row_faces = 0.5 * (inner_coef[:, 1:] + inner_coef[:, :-1])
    row_flux = row_faces * (inner_vals[:, :, 1:] - inner_vals[:, :, :-1])
    return across + row_flux[:, :, :-1] - row_flux[:, :, 1:]


def weights_of(multi_index, coupled_slot, slot_count):
    mode_count = multi_index.shape[1]
    degrees = multi_index.astype(jnp.float32)
    raise_weight = jnp.where(
        coupled_slot[:, :mode_count] < slot_count, jnp.sqrt(degrees + 1.0), 0.0
    )
    lower_weight = jnp.sqrt(jnp.maximum(degrees, 0.0))
    return (raise_weight, lower_weight)


def operate_gathered(term_field, coeff_ext, multi_index, coupled_slot):
    mode_count = multi_index.shape[1]
    slot_count = lax.axis_size("chaos") * term_field.shape[0]
    raise_weight, lower_weight = weights_of(multi_index, coupled_slot, slot_count)
    raise_index = jnp.minimum(coupled_slot[:, :mode_count], slot_count - 1)
    lower_index = jnp.minimum(coupled_slot[:, mode_count:], slot_count - 1)
    extended = with_halo(term_field, (("space", 1),), 1)
    result = stencil(extended, coeff_ext[0])
    everything = lax.all_gather(extended, "chaos", axis=0, tiled=True)
    for kl_mode in range(mode_count):
        mixture = raise_weight[:, kl_mode, None, None] * everything[raise_index[:, kl_mode]]
        mixture = (
            mixture + lower_weight[:, kl_mode, None, None] * everything[lower_index[:, kl_mode]]
        )
        result = result + stencil(mixture, coeff_ext[kl_mode + 1])
    return result


def squares(residual):
    return lax.psum(jnp.sum(residual * residual), ("space", "chaos"))


def curving(direction, applied):
    return lax.psum(jnp.sum(direction * applied), ("space", "chaos"))


def solve_steps(apply_op, forcing, start_guess):
    approximation = start_guess
    residual = forcing - apply_op(start_guess)
    direction = residual
    norm_now = squares(residual)
    for number in range(ITERS):
        applied = apply_op(direction)
        step_length = norm_now / curving(direction, applied)
        approximation = approximation + step_length * direction
        residual = residual - step_length * applied
        if number + 1 < ITERS:
            norm_next = squares(residual)
            direction = residual + norm_next / norm_now * direction
            norm_now = norm_next
    return (approximation, residual)


def per_device(forcing, start_guess, mean_field, mode_fields, multi_index, coupled_slot):
    stacked = jnp.concatenate([mean_field[None], mode_fields], axis=0)
    coeff_ext = with_halo(stacked, (("space", 1),), 1)

    def apply_op(term_field):
        return operate_gathered(term_field, coeff_ext, multi_index, coupled_slot)

    return solve_steps(apply_op, forcing, start_guess)


def solution(mesh):
    placed = (
        P("chaos", "space", None),
        P("chaos", "space", None),
        P("space", None),
        P(None, "space", None),
        P("chaos", None),
        P("chaos", None),
    )
    return jax.shard_map(
        per_device,
        mesh=mesh,
        in_specs=placed,
        out_specs=(P("chaos", "space", None), P("chaos", "space", None)),
        check_vma=False,
    )
```

profile of v0, /device:TPU:0, one launch (start us, length us, event | category | flops | bytes accessed | tf_op | source)
XLA Modules:
  0.0 695.0 jit_solution(84687090150263485)
XLA Ops:
  14.8 5.1 collective-permute-start.1
  37.7 44.2 %all-gather.4.cloned.1.call-done = f32[288,18,128]{2,0,1:T(8,128)} async-done(((f32[72,18,128]{2,0,1:T(8,128)}), f32[288,18,128]{2,0,1:T(8,128)}) %all-gather.4.cloned.1.call-update) | async-done | bytes 2654224 | tf_op jit(solution)/shard_map/all_gather | solution.py:51
  165.8 4.6 fusion.120
  178.4 55.6 %all-gather.6.cloned.1.call-done = f32[288,18,128]{2,0,1:T(8,128)} async-done(((f32[72,18,128]{2,0,1:T(8,128)}), f32[288,18,128]{2,0,1:T(8,128)}) %all-gather.6.cloned.1.call-update) | async-done | bytes 2654224 | tf_op jit(solution)/shard_map/all_gather | solution.py:51
  234.1 5.2 copy.32
  242.0 3.7 gather_fusion.38
  247.9 3.7 gather_fusion.37
  251.6 3.7 gather_fusion.36
  284.2 3.7 gather_fusion.30
  291.4 3.7 gather_fusion.29
  295.1 3.7 gather_fusion.28
  302.4 3.7 gather_fusion.27
  328.0 3.7 gather_fusion.22
  358.3 17.4 %multiply_reduce_fusion.2 = (f32[]{:T(128)}, f32[]{:T(128)}, f32[72,16,128]{2,1,0:T(8,128)S(1)}) fusion(f32[72,16,128]{2,1,0:T(8,128)S(1)} %fusion.120, f32[72,16,129]{2,1,0:T(8,128)S(1)} %fusion.43, f32[72,17,128]{2,1,0:T(8,128)S(1)} %fusion.76, f32[72,16,129]{2,1,0:T(8,128)S(1)} %fusion.41, f32[72,17,128]{2,1,0:T(8,128)S(1)} %copy-done.21, ...), kind=kLoop, calls=%fused_computation.427 | loop fusion | flops 6930430 | bytes 27131912 | tf_op jit(solution)/shard_map/reduce_sum | solution.py:66
  375.6 39.3 %all-reduce.44 = (f32[]{:T(128)}, f32[]{:T(128)}) all-reduce(f32[]{:T(128)} %get-tuple-element.3, f32[]{:T(128)} %get-tuple-element.2), channel_id=1, replica_groups=mesh['space'=8,'chaos'=4] {'space','chaos'}, use_global_device_ids=true, to_apply=%region_1.2 | all-reduce | flops 2 | bytes 16 | tf_op jit(solution)/shard_map/psum | solution.py:62
  417.0 40.5 %psum.30 = f32[]{:T(128)} all-reduce(f32[]{:T(128)} %multiply_reduce_fusion.1), channel_id=1, replica_groups=mesh['space'=8,'chaos'=4] {'space','chaos'}, use_global_device_ids=true, to_apply=%region_5.6 | all-reduce | flops 1 | bytes 8 | tf_op jit(solution)/shard_map/psum | solution.py:62
  466.9 56.1 %all-gather.8.cloned.1.call-done = f32[288,18,128]{2,0,1:T(8,128)} async-done(((f32[72,18,128]{2,0,1:T(8,128)}), f32[288,18,128]{2,0,1:T(8,128)}) %all-gather.8.cloned.1.call-update) | async-done | bytes 2654224 | tf_op jit(solution)/shard_map/all_gather | solution.py:51
  523.0 5.2 copy.53
  531.0 3.7 gather_fusion.58
  550.4 3.7 gather_fusion.54
  569.9 3.7 gather_fusion.50
  608.8 3.7 gather_fusion.42
  638.7 6.7 multiply_reduce_fusion
  645.4 39.2 %psum.31 = f32[]{:T(128)} all-reduce(f32[]{:T(128)} %get-tuple-element.6), channel_id=1, replica_groups=mesh['space'=8,'chaos'=4] {'space','chaos'}, use_global_device_ids=true, to_apply=%region_7.8 | all-reduce | flops 1 | bytes 8 | tf_op jit(solution)/shard_map/psum | solution.py:66
  (491 shorter events, 312.3 us)
Async XLA Ops:
  7.2 74.7 %all-gather.4.cloned.1.call-start = ((), (), s32[]{:S(2)}) async-start(), calls=%async_computation | async-start | bytes 3317760 | tf_op jit(solution)/shard_map/all_gather | solution.py:51
  8.3 13.6 %collective-permute-start.2 = (f32[72,1,128]{2,1,0:T(1,128)S(1)}, f32[72,1,128]{2,1,0:T(1,128)S(1)}, u32[]{:S(2)}, u32[]{:S(2)}) collective-permute-start(f32[72,1,128]{2,1,0:T(1,128)S(1)} %get-tuple-element.16), channel_id=1, source_target_pairs={{4,0},{8,4},{12,8},{16,12},{20,16},{24,20},{28,24},{5,1},{9,5},{13... | collective-permute-start | bytes 110600 | tf_op jit(solution)/shard_map/ppermute | solution.py:17
  9.6 12.3 %collective-permute-start.3 = (f32[72,1,128]{2,1,0:T(1,128)S(1)}, f32[72,1,128]{2,1,0:T(1,128)S(1)}, u32[]{:S(2)}, u32[]{:S(2)}) collective-permute-start(f32[72,1,128]{2,1,0:T(1,128)S(1)} %get-tuple-element.15), channel_id=1, source_target_pairs={{0,4},{4,8},{8,12},{12,16},{16,20},{20,24},{24,28},{1,5},{5,9},{9,... | collective-permute-start | bytes 110600 | tf_op jit(solution)/shard_map/ppermute | solution.py:16
  13.5 21.8 %collective-permute-start = (f32[11,1,128]{2,1,0:T(1,128)S(1)}, f32[11,1,128]{2,1,0:T(1,128)S(1)}, u32[]{:S(2)}, u32[]{:S(2)}) collective-permute-start(f32[11,1,128]{2,1,0:T(1,128)S(1)} %get-tuple-element.30), channel_id=1, source_target_pairs={{4,0},{8,4},{12,8},{16,12},{20,16},{24,20},{28,24},{5,1},{9,5},{13... | collective-permute-start | bytes 16904 | tf_op jit(solution)/shard_map/ppermute | solution.py:17
  14.8 20.5 %collective-permute-start.1 = (f32[11,1,128]{2,1,0:T(1,128)S(1)}, f32[11,1,128]{2,1,0:T(1,128)S(1)}, u32[]{:S(2)}, u32[]{:S(2)}) collective-permute-start(f32[11,1,128]{2,1,0:T(1,128)S(1)} %get-tuple-element.31), channel_id=1, source_target_pairs={{0,4},{4,8},{8,12},{12,16},{16,20},{20,24},{24,28},{1,5},{5,9},{9,... | collective-permute-start | bytes 16904 | tf_op jit(solution)/shard_map/ppermute | solution.py:16
  21.9 6.6 copy-start.57
  22.0 10.0 %copy-start.122 = (s32[72,20]{0,1:T(8,128)S(1)}, s32[72,20]{0,1:T(8,128)}, u32[]{:S(2)}) copy-start(s32[72,20]{0,1:T(8,128)} %param.11) | copy-start | bytes 17284
  22.0 10.0 %copy-start.127 = (s32[72,10]{0,1:T(8,128)S(1)}, s32[72,10]{0,1:T(8,128)}, u32[]{:S(2)}) copy-start(s32[72,10]{0,1:T(8,128)} %param.10) | copy-start | bytes 8644
  22.0 11.3 %copy-start = (f32[72,16,128]{2,1,0:T(8,128)S(1)}, f32[72,16,128]{2,1,0:T(8,128)}, u32[]{:S(2)}) copy-start(f32[72,16,128]{2,1,0:T(8,128)} %param.7) | copy-start | bytes 1769476
  23.0 211.1 %all-gather.6.cloned.1.call-start = ((), (), s32[]{:S(2)}) async-start(), calls=%async_computation.1 | async-start | bytes 3317760 | tf_op jit(solution)/shard_map/all_gather | solution.py:51
  28.6 6.7 copy-start.85
  158.2 7.1 %copy-start.30 = (f32[72,16,129]{2,1,0:T(8,128)S(1)}, f32[72,16,129]{2,1,0:T(8,128)}, u32[]{:S(2)}) copy-start(f32[72,16,129]{2,1,0:T(8,128)} %fusion.1) | copy-start | bytes 1783300
  158.8 6.6 copy-start.19
  158.8 6.6 copy-start.20
  170.5 4.3 collective-permute-start.4
  171.8 3.9 collective-permute-start.5
  176.8 346.2 %all-gather.8.cloned.1.call-start = ((), (), s32[]{:S(2)}) async-start(), calls=%async_computation.2 | async-start | bytes 3317760 | tf_op jit(solution)/shard_map/all_gather | solution.py:51
  350.6 7.2 %copy-start.31 = (f32[72,16,129]{2,1,0:T(8,128)S(1)}, f32[72,16,129]{2,1,0:T(8,128)}, u32[]{:S(2)}) copy-start(f32[72,16,129]{2,1,0:T(8,128)} %fusion.23) | copy-start | bytes 1783300
  459.0 4.3 collective-permute-start.6
  460.3 3.9 collective-permute-start.7
  628.6 6.9 copy-start.52
  629.7 8.7 %copy-start.29 = (f32[72,16,129]{2,1,0:T(8,128)S(1)}, f32[72,16,129]{2,1,0:T(8,128)}, u32[]{:S(2)}) copy-start(f32[72,16,129]{2,1,0:T(8,128)} %fusion.45) | copy-start | bytes 1783300
  631.1 7.2 %copy-start.18 = (f32[72,17,128]{2,1,0:T(8,128)S(1)}, f32[72,17,128]{2,1,0:T(8,128)}, u32[]{:S(2)}) copy-start(f32[72,17,128]{2,1,0:T(8,128)} %fusion.74) | copy-start | bytes 1880068
  638.7 47.2 %copy-start.1 = (f32[72,16,128]{2,1,0:T(8,128)S(1)}, f32[72,16,128]{2,1,0:T(8,128)}, u32[]{:S(2)}) copy-start(f32[72,16,128]{2,1,0:T(8,128)} %param.7) | copy-start | bytes 1769476
  (115 other events, 220.8 us)
Sparse Core Ops, SparseCore 0:
  23.1 58.7 all-gather.3
  176.9 57.0 all-gather.5
  465.4 57.5 all-gather.7
where the time goes:
time: 703 us; the launch traced here: 695 us
  local copies, waits for them, and re-layouts  226 us (32%)
  waiting for transfers between devices  158 us (22%)
  other arithmetic  153 us (22%)
  blocking collectives  119 us (17%)
  starting transfers between devices  19.5 us (3%)
  between operations  19.4 us (3%)
    all_gather x3, waiting for transfers between devices, operate_gathered(): everything = lax.all_gather(extended, 'chaos', axis=0, tiled=True)  156 us
    gather x30, local copies, waits for them, and re-layouts, operate_gathered(): everything[raise_index[:, kl_mode]]  90.3 us
    gather x30, local copies, waits for them, and re-layouts, operate_gathered(): everything[lower_index[:, kl_mode]]  80 us
    psum x2, blocking collectives, squares(): return lax.psum(jnp.sum(residual * residual), ('space', 'chaos'))  79.8 us
    add x30, other arithmetic, operate_gathered(): mixture + lower_weight[:, kl_mode, None, None] * everything[lower_index[:...  46.7 us
    psum x1, blocking collectives, curving(): return lax.psum(jnp.sum(direction * applied), ('space', 'chaos'))  39.2 us
    mul x33, other arithmetic, stencil(): row_flux = row_faces * (inner_vals[:, :, 1:] - inner_vals[:, :, :-1])  31.5 us
    mul x35, other arithmetic, stencil(): col_flux = col_faces * (values[:, 1:] - values[:, :-1])  30.7 us
  transfers between devices with their start and end apart: 11, of which 5 were waited for; matrix products, arithmetic and copies ran while one was open for 3% of the time, Pallas kernels for 0%

commit v1 on v0

v1 whole, which is shorter than its diff:
```python
import functools
import math

import jax
import jax.numpy as jnp
import numpy as np
from jax import lax
from jax.experimental import pallas as pl
from jax.experimental.pallas import tpu as pltpu
from jax.sharding import PartitionSpec as P

DEGREE = 3
SUB = 8
LANES = 128
VMEM = pltpu.CompilerParams(vmem_limit_bytes=48 * 1024 * 1024)


def term_list(modes):
    triples = [
        (a, b, c) for a in range(modes + 1) for b in range(a + 1) for c in range(b + 1)
    ]
    place = {t: i for i, t in enumerate(triples)}
    edges = []
    for t in triples:
        used = [x for x in t if x]
        mine = []
        for k in range(1, modes + 1):
            power = used.count(k)
            if len(used) < DEGREE:
                up = tuple(sorted(used + [k], reverse=True))
                mine.append((place[up + (0,) * (DEGREE - len(up))], k - 1, power + 1))
            if power:
                left = list(used)
                left.remove(k)
                mine.append((place[tuple(left) + (0,) * (DEGREE - len(left))], k - 1, power))
        edges.append(mine)
    return edges


def rank_of(multi_index):
    modes = multi_index.shape[1]
    from_top = jnp.asarray(np.tril(np.ones((modes, modes), np.int32)))
    above = jnp.sum(jnp.maximum(multi_index, 0)[:, :, None] * from_top[None], axis=1)
    a, b, c = (jnp.sum((above >= n).astype(jnp.int32), axis=1) for n in (1, 2, 3))
    rank = a * (a + 1) * (a + 2) // 6 + b * (b + 1) // 2 + c
    return jnp.where(multi_index[:, 0] < 0, math.comb(modes + DEGREE, DEGREE), rank)


def columns_at(value, start, width):
    return lax.dynamic_slice_in_dim(value, start, width, axis=1)


def lane_next(u):
    lane = lax.broadcasted_iota(jnp.int32, u.shape, u.ndim - 1)
    return jnp.where(lane == LANES - 1, 0.0, pltpu.roll(u, LANES - 1, u.ndim - 1))


def lane_before(u):
    lane = lax.broadcasted_iota(jnp.int32, u.shape, u.ndim - 1)
    return jnp.where(lane == 0, 0.0, pltpu.roll(u, 1, u.ndim - 1))


def face_coefficients(coef_ref):
    east, right, left = [], [], []
    for k in range(coef_ref.shape[0]):
        c = coef_ref[k]
        east.append(0.5 * (c + pltpu.roll(c, SUB - 1, 0)))
        right.append(0.5 * (c + lane_next(c)))
        left.append(0.5 * (c + lane_before(c)))
    return east, right, left


def apply_operator(u_ref, coef_ref, edges, store, diff_ref):
    terms = len(edges)

    def differences(s, carry):
        u = u_ref[s]
        diff_ref[0, s] = pltpu.roll(u, SUB - 1, 0) - u
        diff_ref[1, s] = u - lane_next(u)
        diff_ref[2, s] = u - lane_before(u)
        return carry

    lax.fori_loop(0, terms, differences, 0, unroll=2)
    east, right, left = face_coefficients(coef_ref)
    for s in range(terms):
        groups = {1: [(s, 0)]}
        for t, k, weight in edges[s]:
            groups.setdefault(weight, []).append((t, k + 1))
        across = along = None
        for weight, members in groups.items():
            e = a = None
            for t, k in members:
                de = east[k] * diff_ref[0, t]
                da = right[k] * diff_ref[1, t] + left[k] * diff_ref[2, t]
                e = de if e is None else e + de
                a = da if a is None else a + da
            if weight > 1:
                e, a = e * math.sqrt(weight), a * math.sqrt(weight)
            across = e if across is None else across + e
            along = a if along is None else along + a
        store(s, pltpu.roll(across, 1, 0) - across + along)


def pack_rows(ranks_ref, packed_refs, field_ref, columns):
    per = SUB // columns
    rows = packed_refs[0].shape[0]
    sub = lax.broadcasted_iota(jnp.int32, (SUB, LANES), 0)
    for d, out in enumerate(packed_refs):

        def one(q, carry, d=d, out=out):
            row = field_ref[ranks_ref[(d * rows + q) * per]]
            for g in range(1, per):
                other = field_ref[ranks_ref[(d * rows + q) * per + g]]
                row = jnp.where(sub < g * columns, row, pltpu.roll(other, g * columns, 0))
            out[q] = row
            return carry

        lax.fori_loop(0, rows, one, 0, unroll=4)


def scatter_row(ranks_ref, at, row, field_ref, columns):
    per = SUB // columns
    for g in range(per):
        part = row if g == 0 else pltpu.roll(row, SUB - g * columns, 0)
        field_ref[ranks_ref[at * per + g], 0:columns] = part[0:columns]


def take_column(flat_ref, j, rows):
    return flat_ref[pl.ds(j, rows, stride=SUB), :]


def enter_kernel(n, columns, ranks_ref, *refs):
    parts, (field_ref, first_ref, last_ref) = refs[:n], refs[n:]
    rows = parts[0].shape[0]
    slots = field_ref.shape[0]
    field_ref[...] = jnp.zeros_like(field_ref)
    for d, part in enumerate(parts):

        def one(q, carry, d=d, part=part):
            scatter_row(ranks_ref, d * rows + q, part[q], field_ref, columns)
            return carry

        lax.fori_loop(0, rows, one, 0, unroll=4)
    flat = field_ref.reshape(slots * SUB, LANES)
    first_ref[...] = take_column(flat, 0, slots)
    last_ref[...] = take_column(flat, columns - 1, slots)


def start_kernel(n, columns, edges, ranks_ref, x_ref, before_ref, after_ref, coef_ref, *refs):
    packed, (u_ref, y_ref, diff_ref) = refs[:n], refs[n:]
    slots = x_ref.shape[0]
    u_ref[...] = x_ref[...]
    flat = u_ref.reshape(slots * SUB, LANES)
    flat[pl.ds(SUB - 1, slots, stride=SUB), :] = before_ref[...]
    flat[pl.ds(columns, slots, stride=SUB), :] = after_ref[...]
    y_ref[len(edges) :] = jnp.zeros((slots - len(edges), SUB, LANES), jnp.float32)

    def store(s, value):
        y_ref[s] = value

    apply_operator(u_ref, coef_ref, edges, store, diff_ref)
    pack_rows(ranks_ref, packed, y_ref, columns)


def residual_kernel(n, columns, ranks_ref, *refs):
    forcing, image = refs[:n], refs[n : 2 * n]
    packed = refs[2 * n : 3 * n]
    field_ref, first_ref, last_ref, sum_ref = refs[3 * n :]
    rows = forcing[0].shape[0]
    slots = field_ref.shape[0]
    field_ref[...] = jnp.zeros_like(field_ref)
    total = jnp.zeros((SUB, LANES), jnp.float32)
    for d in range(n):

        def one(q, total, d=d):
            v = forcing[d][q] - image[d][q]
            packed[d][q] = v
            scatter_row(ranks_ref, d * rows + q, v, field_ref, columns)
            return total + v * v

        total = lax.fori_loop(0, rows, one, total, unroll=4)
    sum_ref[...] = total
    flat = field_ref.reshape(slots * SUB, LANES)
    for j in range(2):
        first_ref[j] = take_column(flat, j, slots)
        last_ref[j] = take_column(flat, columns - 2 + j, slots)


def first_kernel(n, columns, edges, ranks_ref, v_ref, before_ref, after_ref, coef_ref, inside_ref, *refs):
    packed, (out_ref, sum_ref), (u_ref, diff_ref) = refs[:n], refs[n : n + 2], refs[n + 2 :]
    slots = v_ref.shape[0]
    u_ref[...] = v_ref[...]
    flat = u_ref.reshape(slots * SUB, LANES)
    for j in range(2):
        flat[pl.ds(SUB - 2 + j, slots, stride=SUB), :] = before_ref[j]
        flat[pl.ds(columns + j, slots, stride=SUB), :] = after_ref[j]
    out_ref[len(edges) :] = jnp.zeros((slots - len(edges), SUB, LANES), jnp.float32)
    inside = inside_ref[...] > 0.0

    def store(s, value):
        out_ref[s] = jnp.where(inside, value, 0.0)

    apply_operator(u_ref, coef_ref, edges, store, diff_ref)
    own = lax.broadcasted_iota(jnp.int32, (SUB, LANES), 0) < columns

    def dot(s, total):
        return total + jnp.where(own, u_ref[s] * out_ref[s], 0.0)

    sum_ref[...] = lax.fori_loop(0, len(edges), dot, jnp.zeros((SUB, LANES), jnp.float32), unroll=4)
    pack_rows(ranks_ref, packed, out_ref, columns)


def second_kernel(n, columns, edges, ranks_ref, v_ref, coef_ref, *refs):
    packed, (y_ref, diff_ref) = refs[:n], refs[n:]
    slots = v_ref.shape[0]
    y_ref[len(edges) :] = jnp.zeros((slots - len(edges), SUB, LANES), jnp.float32)

    def store(s, value):
        y_ref[s] = value

    apply_operator(v_ref, coef_ref, edges, store, diff_ref)
    pack_rows(ranks_ref, packed, y_ref, columns)


def lines_of(sums_ref, count):
    full = jnp.sum(sums_ref[...], axis=1, keepdims=True)
    return [full[i : i + 1] for i in range(count)]


def dots_kernel(n, sums_ref, *refs):
    v0, v1, v2, out_ref = refs[:n], refs[n : 2 * n], refs[2 * n : 3 * n], refs[3 * n]
    rows = v0[0].shape[0]
    s00, s01 = lines_of(sums_ref, 2)
    step = s00 / s01
    totals = (jnp.zeros((SUB, LANES), jnp.float32),) * 4
    for d in range(n):

        def one(q, totals, d=d):
            a, b, c = v0[d][q], v1[d][q], v2[d][q]
            r = a - step * b
            image = b - step * c
            return tuple(t + x for t, x in zip(totals, (r * r, r * image, r * b, a * image)))

        totals = lax.fori_loop(0, rows, one, totals, unroll=4)
    out_ref[...] = jnp.zeros_like(out_ref)
    for i, t in enumerate(totals):
        out_ref[i : i + 1] = jnp.sum(t, axis=0, keepdims=True)


def finish_kernel(n, columns, offsets_ref, first_ref, second_ref, x_ref, f_ref, *refs):
    image, v1, v2 = refs[:n], refs[n : 2 * n], refs[2 * n : 3 * n]
    approx_ref, residual_ref = refs[3 * n :]
    per = SUB // columns
    rows = image[0].shape[0]
    s00, s01 = lines_of(first_ref, 2)
    rr, r_ar, r_v1, v0_ar = lines_of(second_ref, 4)
    step = s00 / s01
    beta = rr / s00
    last = rr / (r_ar + beta * (r_v1 + v0_ar) + beta * beta * s01)
    whole = step + last * beta
    for d in range(n):
        at = pl.ds(pl.multiple_of(offsets_ref[d], columns), columns)

        def one(q, carry, d=d, at=at):
            y, b, c = image[d][q], v1[d][q], v2[d][q]
            for g in range(per):
                part = slice(g * columns, (g + 1) * columns)
                s = q * per + g
                yg, bg, cg = y[part], b[part], c[part]
                v0 = f_ref[s, at] - yg
                r1 = v0 - step * bg
                approx_ref[s, at] = x_ref[s, at] + whole * v0 + last * r1
                residual_ref[s, at] = r1 - last * ((1.0 + beta) * bg - step * cg)
            return carry

        lax.fori_loop(0, rows, one, 0, unroll=2)


def call(kernel, scalars, arrays, outs, scratch=()):
    whole = pl.BlockSpec(memory_space=pltpu.VMEM)
    return pl.pallas_call(
        kernel,
        in_specs=[pl.BlockSpec(memory_space=pltpu.SMEM)] * len(scalars) + [whole] * len(arrays),
        out_specs=[whole] * len(outs),
        out_shape=[jax.ShapeDtypeStruct(s, jnp.float32) for s in outs],
        scratch_shapes=[pltpu.VMEM(s, jnp.float32) for s in scratch],
        compiler_params=VMEM,
    )(*scalars, *arrays)


def butterfly(value, sizes):
    count = math.prod(sizes)
    bit = 1
    while bit < count:
        value = value + lax.ppermute(value, ("space", "chaos"), [(i, i ^ bit) for i in range(count)])
        bit *= 2
    return value


def per_device(forcing, start_guess, mean_field, mode_fields, multi_index, coupled_slot):
    spaces, n = lax.axis_size("space"), lax.axis_size("chaos")
    i, z = lax.axis_index("space"), lax.axis_index("chaos")
    here, width, lanes = forcing.shape
    modes = mode_fields.shape[0]
    columns = width // n
    rows = here * columns // SUB
    slots = n * here
    edges = term_list(modes)

    def chunk(space, chaos):
        return jnp.where(space % 2 == 0, chaos, n - 1 - chaos)

    def device_at(p):
        tile, c = divmod(p, n)
        return tile * n + (c if tile % 2 == 0 else n - 1 - c)

    line = [(device_at(p), device_at(p + 1)) for p in range(spaces * n - 1)]
    back_line = [(b, a) for a, b in line]
    both = ("space", "chaos")

    def outward(d):
        return [(j, (j + d) % n) for j in range(n)]

    def homeward(d):
        return [(j, (j - d) % n) for j in range(n)]

    offsets = [columns * chunk(i, (z + d) % n) for d in range(n)]

    def cut(value, d):
        return columns_at(value, offsets[d], columns).reshape(rows, SUB, lanes)

    def sent(parts, way):
        return parts[:1] + [lax.ppermute(parts[d], "chaos", way(d)) for d in range(1, n)]

    rank = rank_of(multi_index)
    tag = jnp.pad(rank.astype(jnp.float32)[None, None], ((0, 0), (0, SUB - 1), (0, lanes - here)))
    x_parts = sent([jnp.concatenate([cut(start_guess, d), tag], axis=0) for d in range(n)], outward)
    ranks = jnp.concatenate([p[rows, 0, :here] for p in x_parts]).astype(jnp.int32)
    x_parts = [p[:rows] for p in x_parts]
    f_parts = sent([cut(forcing, d) for d in range(n)], outward)

    stacked = jnp.concatenate([mean_field[None], mode_fields], axis=0)
    up = [(j, j + 1) for j in range(spaces - 1)]
    down = [(j + 1, j) for j in range(spaces - 1)]
    coef = jnp.concatenate(
        [
            lax.ppermute(stacked[:, width - 2 :], "space", up),
            stacked,
            lax.ppermute(stacked[:, :2], "space", down),
        ],
        axis=1,
    )
    coef = columns_at(coef, offsets[0], columns + 4)
    gap = jnp.zeros((modes + 1, SUB - columns - 4, lanes), jnp.float32)
    coef = jnp.concatenate([coef[:, 2:], gap, coef[:, :2]], axis=1)
    sub = lax.broadcasted_iota(jnp.int32, (SUB, lanes), 0)
    position = i * n + chunk(i, z)
    outside = ((position == 0) & (sub >= SUB - 2)) | (
        (position == spaces * n - 1) & (sub >= columns) & (sub < columns + 2)
    )
    inside = jnp.where(outside, 0.0, 1.0)

    field, part, small = (slots, SUB, lanes), (rows, SUB, lanes), (SUB, lanes)
    diff = (3,) + field

    x, x_first, x_last = call(
        functools.partial(enter_kernel, n, columns),
        [ranks],
        x_parts,
        [field, (slots, lanes), (slots, lanes)],
    )
    x_before = lax.ppermute(x_last, both, line)
    x_after = lax.ppermute(x_first, both, back_line)
    image = call(
        functools.partial(start_kernel, n, columns, edges),
        [ranks],
        [x, x_before, x_after, coef],
        [part] * n,
        [field, field, diff],
    )
    *v0_parts, v0, v0_first, v0_last, sum00 = call(
        functools.partial(residual_kernel, n, columns),
        [ranks],
        f_parts + list(image),
        [part] * n + [field, (2, slots, lanes), (2, slots, lanes), small],
    )
    v0_before = lax.ppermute(v0_last, both, line)
    v0_after = lax.ppermute(v0_first, both, back_line)
    image_home = sent(list(image), homeward)
    *v1_parts, v1, sum01 = call(
        functools.partial(first_kernel, n, columns, edges),
        [ranks],
        [v0, v0_before, v0_after, coef, inside],
        [part] * n + [field, small],
        [field, diff],
    )
    v1_home = sent(v1_parts, homeward)
    sums = jnp.stack([jnp.sum(sum00, axis=0), jnp.sum(sum01, axis=0)])
    sums = butterfly(jnp.pad(sums, ((0, SUB - 2), (0, 0))), (spaces, n))
    v2_parts = call(
        functools.partial(second_kernel, n, columns, edges),
        [ranks],
        [v1, coef],
        [part] * n,
        [field, diff],
    )
    v2_home = sent(list(v2_parts), homeward)
    (dots,) = call(
        functools.partial(dots_kernel, n),
        [],
        [sums] + v0_parts + v1_parts + list(v2_parts),
        [small],
    )
    dots = butterfly(dots, (spaces, n))
    return call(
        functools.partial(finish_kernel, n, columns),
        [jnp.stack(offsets).astype(jnp.int32)],
        [sums, dots, start_guess, forcing] + image_home + v1_home + v2_home,
        [forcing.shape] * 2,
    )


def solution(mesh):
    placed = (
        P("chaos", "space", None),
        P("chaos", "space", None),
        P("space", None),
        P(None, "space", None),
        P("chaos", None),
        P("chaos", None),
    )
    return jax.shard_map(
        lambda *a: tuple(per_device(*a)),
        mesh=mesh,
        in_specs=placed,
        out_specs=(P("chaos", "space", None), P("chaos", "space", None)),
        check_vma=False,
    )
```

time: 703 us -> 173 us (0.25); the launches traced: 695 us -> 173 us
  local copies, waits for them, and re-layouts: 226 us -> 6.58 us
  other arithmetic: 153 us -> 1.32 us
  blocking collectives: 119 us -> 0 us
  waiting for transfers between devices: 158 us -> 71.9 us
  Pallas kernels: 0 us -> 48.5 us
  starting transfers between devices: 19.5 us -> 43.2 us
  between operations: 19.4 us -> 1.22 us
    gather x60 -> x0, local copies, waits for them, and re-layouts: 170 us -> none  [the longest x30 90.3 us: operate_gathered(): everything[raise_index[:, kl_mode]]]
    all_gather x3 -> x0, waiting for transfers between devices: 156 us -> none  [operate_gathered(): everything = lax.all_gather(extended, 'chaos', axis=0, tiled=True)]
    psum x3 -> x0, blocking collectives: 119 us -> none  [the longest x2 79.8 us: squares(): return lax.psum(jnp.sum(residual * residual), ('space', 'chaos'))]
    ppermute x8 -> x31, waiting for transfers between devices: 1.69 us -> 71.9 us  [the longest x15 41.4 us: sent(): lax.ppermute(parts[d], 'chaos', way(d))]
    mul x74 -> x0, other arithmetic: 65.6 us -> none  [the longest x33 31.5 us: stencil(): row_flux = row_faces * (inner_vals[:, :, 1:] - inner_vals[:, :, :-1])]
    pallas_call x0 -> x7, Pallas kernels: none -> 48.5 us  [call(): pl.pallas_call(kernel, in_specs=[pl.BlockSpec(memory_space=pltpu.SMEM)] *...]
    add x31 -> x10, other arithmetic: 46.8 us -> 0.05 us  [butterfly(): value + lax.ppermute(value, ('space', 'chaos'), [(i, i ^ bit) for i in ra...]
    reduce_sum x3 -> x4, other arithmetic: 24.8 us -> 0.15 us  [the longest x1 0.09 us: rank_of(): jnp.sum(jnp.maximum(multi_index, 0)[:, :, None] * from_top[None], axis=1)]
  transfers between devices with their start and end apart: 11 -> 31, of which waited for: 5 -> 16; matrix products, arithmetic and copies ran while one was open for 3% -> 1% of each run, Pallas kernels for 0% -> 17%
where the time goes in v1:
time: 173 us
  waiting for transfers between devices  71.9 us (42%)
  Pallas kernels  48.5 us (28%)
  starting transfers between devices  43.2 us (25%)
  local copies, waits for them, and re-layouts  6.58 us (4%)
    pallas_call x7, Pallas kernels, call(): pl.pallas_call(kernel, in_specs=[pl.BlockSpec(memory_space=pltpu.SMEM)] *...  48.5 us
    ppermute x15, waiting for transfers between devices, sent(): lax.ppermute(parts[d], 'chaos', way(d))  41.4 us
    ppermute x15, starting transfers between devices, sent(): lax.ppermute(parts[d], 'chaos', way(d))  24.7 us
    ppermute x10, waiting for transfers between devices, butterfly(): lax.ppermute(value, ('space', 'chaos'), [(i, i ^ bit) for i in range(coun...  16.3 us
    ppermute x10, starting transfers between devices, butterfly(): lax.ppermute(value, ('space', 'chaos'), [(i, i ^ bit) for i in range(coun...  7.77 us
    ppermute x1, waiting for transfers between devices, per_device(): v0_after = lax.ppermute(v0_first, both, back_line)  5.7 us
    unnamed x44, local copies, waits for them, and re-layouts  4.66 us
    ppermute x1, waiting for transfers between devices, per_device(): x_after = lax.ppermute(x_first, both, back_line)  4.4 us
  transfers between devices with their start and end apart: 31, of which 16 were waited for; matrix products, arithmetic and copies ran while one was open for 1% of the time, Pallas kernels for 17%

profile of v1, /device:TPU:0, one launch (start us, length us, event | category | flops | bytes accessed | tf_op | source)
XLA Modules:
  0.0 172.7 jit_solution(6561494322010805745)
XLA Ops:
  2.7 3.0 %collective-permute-start.8 = (f32[11,2,128]{2,1,0:T(2,128)S(1)}, f32[11,2,128]{2,1,0:T(2,128)S(1)}, u32[]{:S(2)}, u32[]{:S(2)}) collective-permute-start(f32[11,2,128]{2,1,0:T(2,128)S(1)} %get-tuple-element.64), channel_id=1, source_target_pairs={{0,4},{4,8},{8,12},{12,16},{16,20},{20,24},{24,28},{1,5},{5,9},{9,... | collective-permute-start | bytes 33800 | tf_op jit(solution)/shard_map/ppermute | solution.py:347
  7.7 3.1 %collective-permute-start.3 = (f32[36,8,128]{2,1,0:T(8,128)S(1)}, f32[36,8,128]{2,1,0:T(8,128)S(1)}, u32[]{:S(2)}, u32[]{:S(2)}) collective-permute-start(f32[36,8,128]{2,1,0:T(8,128)S(1)} %bitcast.51), channel_id=1, source_target_pairs={{0,1},{1,2},{2,3},{3,0},{4,5},{5,6},{6,7},{7,4},{8,9},{9,10},{10,1... | collective-permute-start | bytes 442376 | tf_op jit(solution)/shard_map/ppermute | solution.py:333
  10.8 2.6 %collective-permute-start.4 = (f32[36,8,128]{2,1,0:T(8,128)S(1)}, f32[36,8,128]{2,1,0:T(8,128)S(1)}, u32[]{:S(2)}, u32[]{:S(2)}) collective-permute-start(f32[36,8,128]{2,1,0:T(8,128)S(1)} %bitcast.50), channel_id=1, source_target_pairs={{0,2},{1,3},{2,0},{3,1},{4,6},{5,7},{6,4},{7,5},{8,10},{9,11},{10,... | collective-permute-start | bytes 442376 | tf_op jit(solution)/shard_map/ppermute | solution.py:333
  13.7 9.9 %collective-permute-done = f32[37,8,128]{2,1,0:T(8,128)S(1)} collective-permute-done((f32[37,8,128]{2,1,0:T(8,128)S(1)}, f32[37,8,128]{2,1,0:T(8,128)S(1)}, u32[]{:S(2)}, u32[]{:S(2)}) %collective-permute-start) | collective-permute-done | bytes 151584 | tf_op jit(solution)/shard_map/ppermute | solution.py:333
  23.7 4.3 %collective-permute-start.1 = (f32[37,8,128]{2,1,0:T(8,128)S(1)}, f32[37,8,128]{2,1,0:T(8,128)S(1)}, u32[]{:S(2)}, u32[]{:S(2)}) collective-permute-start(f32[37,8,128]{2,1,0:T(8,128)S(1)} %get-tuple-element.66), channel_id=1, source_target_pairs={{0,2},{1,3},{2,0},{3,1},{4,6},{5,7},{6,4},{7,5},{8,10},{9,11},{10,... | collective-permute-start | bytes 454664 | tf_op jit(solution)/shard_map/ppermute | solution.py:333
  28.0 7.5 %collective-permute-done.1 = f32[37,8,128]{2,1,0:T(8,128)S(1)} collective-permute-done((f32[37,8,128]{2,1,0:T(8,128)S(1)}, f32[37,8,128]{2,1,0:T(8,128)S(1)}, u32[]{:S(2)}, u32[]{:S(2)}) %collective-permute-start.1) | collective-permute-done | bytes 151584 | tf_op jit(solution)/shard_map/ppermute | solution.py:333
  36.1 5.0 %collective-permute-done.2 = f32[37,8,128]{2,1,0:T(8,128)S(1)} collective-permute-done((f32[37,8,128]{2,1,0:T(8,128)S(1)}, f32[37,8,128]{2,1,0:T(8,128)S(1)}, u32[]{:S(2)}, u32[]{:S(2)}) %collective-permute-start.2) | collective-permute-done | bytes 151584 | tf_op jit(solution)/shard_map/ppermute | solution.py:333
  41.0 2.1 %collective-permute-start.5 = (f32[36,8,128]{2,1,0:T(8,128)S(1)}, f32[36,8,128]{2,1,0:T(8,128)S(1)}, u32[]{:S(2)}, u32[]{:S(2)}) collective-permute-start(f32[36,8,128]{2,1,0:T(8,128)S(1)} %bitcast.49), channel_id=1, source_target_pairs={{0,3},{1,0},{2,1},{3,2},{4,7},{5,4},{6,5},{7,6},{8,11},{9,8},{10,9... | collective-permute-start | bytes 442376 | tf_op jit(solution)/shard_map/ppermute | solution.py:333
  49.0 4.4 %collective-permute-done.7.after_ref = f32[288,128]{1,0:T(8,128)S(1)} collective-permute-done((f32[288,128]{1,0:T(8,128)S(1)}, f32[288,128]{1,0:T(8,128)S(1)}, u32[]{:S(2)}, u32[]{:S(2)}) %collective-permute-start.7) | collective-permute-done | bytes 147488 | tf_op jit(solution)/shard_map/ppermute | solution.py:373
  53.4 13.9 %shard_map.78 = (f32[36,8,128]{2,1,0:T(8,128)S(1)}, f32[36,8,128]{2,1,0:T(8,128)S(1)}, f32[36,8,128]{2,1,0:T(8,128)S(1)}, f32[36,8,128]{2,1,0:T(8,128)S(1)}) custom-call(s32[288]{0:T(512)S(1)} %maximum_convert_fusion.ranks_ref, f32[288,8,128]{2,1,0:T(8,128)S(1)} %get-tuple-element.27.x_ref, f32[288,128]{1,0:T(8,128)S(1)} %collective-permute-done.6.before_ref, ...), custom_call_target="tpu_custom_call" | custom-call | tf_op jit(solution)/shard_map/pallas_call | solution.py:281
  74.6 2.8 %collective-permute-done.10.before_ref = f32[2,288,128]{2,1,0:T(8,128)S(1)} collective-permute-done((f32[2,288,128]{2,1,0:T(8,128)S(1)}, f32[2,288,128]{2,1,0:T(8,128)S(1)}, u32[]{:S(2)}, u32[]{:S(2)}) %collective-permute-start.10) | collective-permute-done | bytes 294944 | tf_op jit(solution)/shard_map/ppermute | solution.py:387
  77.5 5.7 %collective-permute-done.11.after_ref = f32[2,288,128]{2,1,0:T(8,128)S(1)} collective-permute-done((f32[2,288,128]{2,1,0:T(8,128)S(1)}, f32[2,288,128]{2,1,0:T(8,128)S(1)}, u32[]{:S(2)}, u32[]{:S(2)}) %collective-permute-start.11) | collective-permute-done | bytes 294944 | tf_op jit(solution)/shard_map/ppermute | solution.py:388
  83.3 14.7 %shard_map.80 = (f32[36,8,128]{2,1,0:T(8,128)S(1)}, f32[36,8,128]{2,1,0:T(8,128)S(1)}, f32[36,8,128]{2,1,0:T(8,128)S(1)}, f32[36,8,128]{2,1,0:T(8,128)S(1)}, f32...) custom-call(s32[288]{0:T(512)S(1)} %maximum_convert_fusion.ranks_ref, f32[288,8,128]{2,1,0:T(8,128)S(1)} %get-tuple-element.35.v_ref, ...), custom_call_target="tpu_custom_call" | custom-call | tf_op jit(solution)/shard_map/pallas_call | solution.py:281
  100.1 3.6 %collective-permute-done.12 = f32[8,128]{1,0:T(8,128)S(1)} collective-permute-done((f32[8,128]{1,0:T(8,128)S(1)}, f32[8,128]{1,0:T(8,128)S(1)}, u32[]{:S(2)}, u32[]{:S(2)}) %collective-permute-start.12) | collective-permute-done | bytes 4128 | tf_op jit(solution)/shard_map/ppermute | solution.py:295
  103.8 2.4 %collective-permute-start.22 = (f32[36,8,128]{2,1,0:T(8,128)}, f32[36,8,128]{2,1,0:T(8,128)S(1)}, u32[]{:S(2)}, u32[]{:S(2)}) collective-permute-start(f32[36,8,128]{2,1,0:T(8,128)} %copy-done.3), channel_id=1, source_target_pairs={{0,3},{1,0},{2,1},{3,2},{4,7},{5,4},{6,5},{7,6},{8,11},{9,8},{10,9... | collective-permute-start | bytes 442376 | tf_op jit(solution)/shard_map/ppermute | solution.py:333
  106.7 2.0 %collective-permute-start.24 = (f32[36,8,128]{2,1,0:T(8,128)S(1)}, f32[36,8,128]{2,1,0:T(8,128)S(1)}, u32[]{:S(2)}, u32[]{:S(2)}) collective-permute-start(f32[36,8,128]{2,1,0:T(8,128)S(1)} %get-tuple-element.33.refs_7_), channel_id=1, source_target_pairs={{0,1},{1,2},{2,3},{3,0},{4,5},{5,6},{6,7},{7,4},{8,9},{9,10},{10,1... | collective-permute-start | bytes 442376 | tf_op jit(solution)/shard_map/ppermute | solution.py:333
  111.8 2.6 %collective-permute-start.15 = (f32[8,128]{1,0:T(8,128)S(1)}, f32[8,128]{1,0:T(8,128)S(1)}, u32[]{:S(2)}, u32[]{:S(2)}) collective-permute-start(f32[8,128]{1,0:T(8,128)S(1)} %add.201), channel_id=1, source_target_pairs={{0,8},{1,9},{2,10},{3,11},{4,12},{5,13},{6,14},{7,15},{8,0},{9,1},... | collective-permute-start | bytes 12296 | tf_op jit(solution)/shard_map/ppermute | solution.py:295
  116.4 13.5 %shard_map.81 = (f32[36,8,128]{2,1,0:T(8,128)S(1)}, f32[36,8,128]{2,1,0:T(8,128)S(1)}, f32[36,8,128]{2,1,0:T(8,128)S(1)}, f32[36,8,128]{2,1,0:T(8,128)S(1)}) custom-call(s32[288]{0:T(512)S(1)} %maximum_convert_fusion.ranks_ref, f32[288,8,128]{2,1,0:T(8,128)S(1)} %get-tuple-element.47.v_ref, f32[11,8,128]{2,1,0:T(8,128)S(1)} %pad_maximum_fusion.coef_ref), custom_call_target="tpu_custom_call" | custom-call | tf_op jit(solution)/shard_map/pallas_call | solution.py:281
  131.0 3.4 %collective-permute-done.17 = f32[8,128]{1,0:T(8,128)S(1)} collective-permute-done((f32[8,128]{1,0:T(8,128)S(1)}, f32[8,128]{1,0:T(8,128)S(1)}, u32[]{:S(2)}, u32[]{:S(2)}) %collective-permute-start.17) | collective-permute-done | bytes 4128 | tf_op jit(solution)/shard_map/ppermute | solution.py:295
  135.6 3.4 %collective-permute-done.18 = f32[8,128]{1,0:T(8,128)S(1)} collective-permute-done((f32[8,128]{1,0:T(8,128)S(1)}, f32[8,128]{1,0:T(8,128)S(1)}, u32[]{:S(2)}, u32[]{:S(2)}) %collective-permute-start.18) | collective-permute-done | bytes 4128 | tf_op jit(solution)/shard_map/ppermute | solution.py:295
  146.0 3.8 %collective-permute-start.28 = (f32[36,8,128]{2,1,0:T(8,128)S(1)}, f32[36,8,128]{2,1,0:T(8,128)S(1)}, u32[]{:S(2)}, u32[]{:S(2)}) collective-permute-start(f32[36,8,128]{2,1,0:T(8,128)S(1)} %get-tuple-element.49.refs_9_), channel_id=1, source_target_pairs={{0,3},{1,0},{2,1},{3,2},{4,7},{5,4},{6,5},{7,6},{8,11},{9,8},{10,9... | collective-permute-start | bytes 442376 | tf_op jit(solution)/shard_map/ppermute | solution.py:333
  150.7 12.8 %collective-permute-done.26.refs_6_ = f32[36,8,128]{2,1,0:T(8,128)S(1)} collective-permute-done((f32[36,8,128]{2,1,0:T(8,128)S(1)}, f32[36,8,128]{2,1,0:T(8,128)S(1)}, u32[]{:S(2)}, u32[]{:S(2)}) %collective-permute-start.26) | collective-permute-done | bytes 147488 | tf_op jit(solution)/shard_map/ppermute | solution.py:333
  163.5 6.2 %collective-permute-done.29.refs_10_ = f32[36,8,128]{2,1,0:T(8,128)S(1)} collective-permute-done((f32[36,8,128]{2,1,0:T(8,128)S(1)}, f32[36,8,128]{2,1,0:T(8,128)S(1)}, u32[]{:S(2)}, u32[]{:S(2)}) %collective-permute-start.29) | collective-permute-done | bytes 147488 | tf_op jit(solution)/shard_map/ppermute | solution.py:333
  169.7 3.0 %shard_map.83 = (f32[72,16,128]{2,1,0:T(8,128)}, f32[72,16,128]{2,1,0:T(8,128)}) custom-call(s32[4]{0:T(128)S(1)} %pad_add_fusion.offsets_ref, f32[8,128]{1,0:T(8,128)S(1)} %add.203.sums_ref.first_ref, f32[8,128]{1,0:T(8,128)S(1)} %add.208.second_ref, f32[72,16,128]{2,1,0:T(8,128)S(1)} %copy-done, f32[72,16,128]{2,1,0:T(8,128)S(1)} %copy-done.1, ...), custom_call_target="tpu_custom_call" | custom-call | tf_op jit(solution)/shard_map/pallas_call | solution.py:281
  (124 shorter events, 35.7 us)
Async XLA Ops:
  1.4 43.0 %collective-permute-start.9 = (f32[11,2,128]{2,1,0:T(2,128)S(1)}, f32[11,2,128]{2,1,0:T(2,128)S(1)}, u32[]{:S(2)}, u32[]{:S(2)}) collective-permute-start(f32[11,2,128]{2,1,0:T(2,128)S(1)} %get-tuple-element.63), channel_id=1, source_target_pairs={{4,0},{8,4},{12,8},{16,12},{20,16},{24,20},{28,24},{5,1},{9,5},{13... | collective-permute-start | bytes 33800 | tf_op jit(solution)/shard_map/ppermute | solution.py:349
  2.7 43.6 %collective-permute-start.8 = (f32[11,2,128]{2,1,0:T(2,128)S(1)}, f32[11,2,128]{2,1,0:T(2,128)S(1)}, u32[]{:S(2)}, u32[]{:S(2)}) collective-permute-start(f32[11,2,128]{2,1,0:T(2,128)S(1)} %get-tuple-element.64), channel_id=1, source_target_pairs={{0,4},{4,8},{8,12},{12,16},{16,20},{20,24},{24,28},{1,5},{5,9},{9,... | collective-permute-start | bytes 33800 | tf_op jit(solution)/shard_map/ppermute | solution.py:347
  7.7 59.6 %collective-permute-start.3 = (f32[36,8,128]{2,1,0:T(8,128)S(1)}, f32[36,8,128]{2,1,0:T(8,128)S(1)}, u32[]{:S(2)}, u32[]{:S(2)}) collective-permute-start(f32[36,8,128]{2,1,0:T(8,128)S(1)} %bitcast.51), channel_id=1, source_target_pairs={{0,1},{1,2},{2,3},{3,0},{4,5},{5,6},{6,7},{7,4},{8,9},{9,10},{10,1... | collective-permute-start | bytes 442376 | tf_op jit(solution)/shard_map/ppermute | solution.py:333
  10.8 56.6 %collective-permute-start.4 = (f32[36,8,128]{2,1,0:T(8,128)S(1)}, f32[36,8,128]{2,1,0:T(8,128)S(1)}, u32[]{:S(2)}, u32[]{:S(2)}) collective-permute-start(f32[36,8,128]{2,1,0:T(8,128)S(1)} %bitcast.50), channel_id=1, source_target_pairs={{0,2},{1,3},{2,0},{3,1},{4,6},{5,7},{6,4},{7,5},{8,10},{9,11},{10,... | collective-permute-start | bytes 442376 | tf_op jit(solution)/shard_map/ppermute | solution.py:333
  13.6 10.1 %collective-permute-start = (f32[37,8,128]{2,1,0:T(8,128)S(1)}, f32[37,8,128]{2,1,0:T(8,128)S(1)}, u32[]{:S(2)}, u32[]{:S(2)}) collective-permute-start(f32[37,8,128]{2,1,0:T(8,128)S(1)} %get-tuple-element.65), channel_id=1, source_target_pairs={{0,1},{1,2},{2,3},{3,0},{4,5},{5,6},{6,7},{7,4},{8,9},{9,10},{10,1... | collective-permute-start | bytes 454664 | tf_op jit(solution)/shard_map/ppermute | solution.py:333
  23.7 11.8 %collective-permute-start.1 = (f32[37,8,128]{2,1,0:T(8,128)S(1)}, f32[37,8,128]{2,1,0:T(8,128)S(1)}, u32[]{:S(2)}, u32[]{:S(2)}) collective-permute-start(f32[37,8,128]{2,1,0:T(8,128)S(1)} %get-tuple-element.66), channel_id=1, source_target_pairs={{0,2},{1,3},{2,0},{3,1},{4,6},{5,7},{6,4},{7,5},{8,10},{9,11},{10,... | collective-permute-start | bytes 454664 | tf_op jit(solution)/shard_map/ppermute | solution.py:333
  35.4 5.6 %collective-permute-start.2 = (f32[37,8,128]{2,1,0:T(8,128)S(1)}, f32[37,8,128]{2,1,0:T(8,128)S(1)}, u32[]{:S(2)}, u32[]{:S(2)}) collective-permute-start(f32[37,8,128]{2,1,0:T(8,128)S(1)} %get-tuple-element.67), channel_id=1, source_target_pairs={{0,3},{1,0},{2,1},{3,2},{4,7},{5,4},{6,5},{7,6},{8,11},{9,8},{10,9... | collective-permute-start | bytes 454664 | tf_op jit(solution)/shard_map/ppermute | solution.py:333
  41.0 26.3 %collective-permute-start.5 = (f32[36,8,128]{2,1,0:T(8,128)S(1)}, f32[36,8,128]{2,1,0:T(8,128)S(1)}, u32[]{:S(2)}, u32[]{:S(2)}) collective-permute-start(f32[36,8,128]{2,1,0:T(8,128)S(1)} %bitcast.49), channel_id=1, source_target_pairs={{0,3},{1,0},{2,1},{3,2},{4,7},{5,4},{6,5},{7,6},{8,11},{9,8},{10,9... | collective-permute-start | bytes 442376 | tf_op jit(solution)/shard_map/ppermute | solution.py:333
  44.5 4.5 %collective-permute-start.6 = (f32[288,128]{1,0:T(8,128)S(1)}, f32[288,128]{1,0:T(8,128)S(1)}, u32[]{:S(2)}, u32[]{:S(2)}) collective-permute-start(f32[288,128]{1,0:T(8,128)S(1)} %get-tuple-element.28), channel_id=1, source_target_pairs={{0,1},{1,2},{2,3},{3,7},{7,6},{6,5},{5,4},{4,8},{8,9},{9,10},{10,1... | collective-permute-start | bytes 442376 | tf_op jit(solution)/shard_map/ppermute | solution.py:372
  46.3 7.0 %collective-permute-start.7 = (f32[288,128]{1,0:T(8,128)S(1)}, f32[288,128]{1,0:T(8,128)S(1)}, u32[]{:S(2)}, u32[]{:S(2)}) collective-permute-start(f32[288,128]{1,0:T(8,128)S(1)} %get-tuple-element.29), channel_id=1, source_target_pairs={{1,0},{2,1},{3,2},{7,3},{6,7},{5,6},{4,5},{8,4},{9,8},{10,9},{11,1... | collective-permute-start | bytes 442376 | tf_op jit(solution)/shard_map/ppermute | solution.py:373
  71.4 6.1 %collective-permute-start.10 = (f32[2,288,128]{2,1,0:T(8,128)S(1)}, f32[2,288,128]{2,1,0:T(8,128)S(1)}, u32[]{:S(2)}, u32[]{:S(2)}) collective-permute-start(f32[2,288,128]{2,1,0:T(8,128)S(1)} %get-tuple-element.36), channel_id=1, source_target_pairs={{0,1},{1,2},{2,3},{3,7},{7,6},{6,5},{5,4},{4,8},{8,9},{9,10},{10,1... | collective-permute-start | bytes 884744 | tf_op jit(solution)/shard_map/ppermute | solution.py:387
  73.3 9.9 %collective-permute-start.11 = (f32[2,288,128]{2,1,0:T(8,128)S(1)}, f32[2,288,128]{2,1,0:T(8,128)S(1)}, u32[]{:S(2)}, u32[]{:S(2)}) collective-permute-start(f32[2,288,128]{2,1,0:T(8,128)S(1)} %get-tuple-element.37), channel_id=1, source_target_pairs={{1,0},{2,1},{3,2},{7,3},{6,7},{5,6},{4,5},{8,4},{9,8},{10,9},{11,1... | collective-permute-start | bytes 884744 | tf_op jit(solution)/shard_map/ppermute | solution.py:388
  103.7 6.8 %collective-permute-start.13 = (f32[8,128]{1,0:T(8,128)S(1)}, f32[8,128]{1,0:T(8,128)S(1)}, u32[]{:S(2)}, u32[]{:S(2)}) collective-permute-start(f32[8,128]{1,0:T(8,128)S(1)} %fusion.10), channel_id=1, source_target_pairs={{0,2},{1,3},{2,0},{3,1},{4,6},{5,7},{6,4},{7,5},{8,10},{9,11},{10,... | collective-permute-start | bytes 12296 | tf_op jit(solution)/shard_map/ppermute | solution.py:295
  103.8 41.6 %collective-permute-start.22 = (f32[36,8,128]{2,1,0:T(8,128)}, f32[36,8,128]{2,1,0:T(8,128)S(1)}, u32[]{:S(2)}, u32[]{:S(2)}) collective-permute-start(f32[36,8,128]{2,1,0:T(8,128)} %copy-done.3), channel_id=1, source_target_pairs={{0,3},{1,0},{2,1},{3,2},{4,7},{5,4},{6,5},{7,6},{8,11},{9,8},{10,9... | collective-permute-start | bytes 442376 | tf_op jit(solution)/shard_map/ppermute | solution.py:333
  106.1 39.8 %collective-permute-start.23 = (f32[36,8,128]{2,1,0:T(8,128)}, f32[36,8,128]{2,1,0:T(8,128)S(1)}, u32[]{:S(2)}, u32[]{:S(2)}) collective-permute-start(f32[36,8,128]{2,1,0:T(8,128)} %copy-done.2), channel_id=1, source_target_pairs={{0,2},{1,3},{2,0},{3,1},{4,6},{5,7},{6,4},{7,5},{8,10},{9,11},{10,... | collective-permute-start | bytes 442376 | tf_op jit(solution)/shard_map/ppermute | solution.py:333
  106.7 39.3 %collective-permute-start.24 = (f32[36,8,128]{2,1,0:T(8,128)S(1)}, f32[36,8,128]{2,1,0:T(8,128)S(1)}, u32[]{:S(2)}, u32[]{:S(2)}) collective-permute-start(f32[36,8,128]{2,1,0:T(8,128)S(1)} %get-tuple-element.33.refs_7_), channel_id=1, source_target_pairs={{0,1},{1,2},{2,3},{3,0},{4,5},{5,6},{6,7},{7,4},{8,9},{9,10},{10,1... | collective-permute-start | bytes 442376 | tf_op jit(solution)/shard_map/ppermute | solution.py:333
  108.7 41.6 %collective-permute-start.25 = (f32[36,8,128]{2,1,0:T(8,128)}, f32[36,8,128]{2,1,0:T(8,128)S(1)}, u32[]{:S(2)}, u32[]{:S(2)}) collective-permute-start(f32[36,8,128]{2,1,0:T(8,128)} %copy-done.8), channel_id=1, source_target_pairs={{0,3},{1,0},{2,1},{3,2},{4,7},{5,4},{6,5},{7,6},{8,11},{9,8},{10,9... | collective-permute-start | bytes 442376 | tf_op jit(solution)/shard_map/ppermute | solution.py:333
  115.9 14.0 %collective-permute-start.16 = (f32[8,128]{1,0:T(8,128)S(1)}, f32[8,128]{1,0:T(8,128)S(1)}, u32[]{:S(2)}, u32[]{:S(2)}) collective-permute-start(f32[8,128]{1,0:T(8,128)S(1)} %add.202), channel_id=1, source_target_pairs={{0,16},{1,17},{2,18},{3,19},{4,20},{5,21},{6,22},{7,23},{8,24},{9,... | collective-permute-start | bytes 12296 | tf_op jit(solution)/shard_map/ppermute | solution.py:295
  143.8 6.0 %collective-permute-start.21 = (f32[8,128]{1,0:T(8,128)S(1)}, f32[8,128]{1,0:T(8,128)S(1)}, u32[]{:S(2)}, u32[]{:S(2)}) collective-permute-start(f32[8,128]{1,0:T(8,128)S(1)} %add.207), channel_id=1, source_target_pairs={{0,16},{1,17},{2,18},{3,19},{4,20},{5,21},{6,22},{7,23},{8,24},{9,... | collective-permute-start | bytes 12296 | tf_op jit(solution)/shard_map/ppermute | solution.py:295
  145.4 18.1 %collective-permute-start.26 = (f32[36,8,128]{2,1,0:T(8,128)S(1)}, f32[36,8,128]{2,1,0:T(8,128)S(1)}, u32[]{:S(2)}, u32[]{:S(2)}) collective-permute-start(f32[36,8,128]{2,1,0:T(8,128)S(1)} %copy-done.7), channel_id=1, source_target_pairs={{0,2},{1,3},{2,0},{3,1},{4,6},{5,7},{6,4},{7,5},{8,10},{9,11},{10,... | collective-permute-start | bytes 442376 | tf_op jit(solution)/shard_map/ppermute | solution.py:333
  146.0 17.5 %collective-permute-start.27 = (f32[36,8,128]{2,1,0:T(8,128)S(1)}, f32[36,8,128]{2,1,0:T(8,128)S(1)}, u32[]{:S(2)}, u32[]{:S(2)}) collective-permute-start(f32[36,8,128]{2,1,0:T(8,128)S(1)} %copy-done.5), channel_id=1, source_target_pairs={{0,1},{1,2},{2,3},{3,0},{4,5},{5,6},{6,7},{7,4},{8,9},{9,10},{10,1... | collective-permute-start | bytes 442376 | tf_op jit(solution)/shard_map/ppermute | solution.py:333
  146.0 17.5 %collective-permute-start.28 = (f32[36,8,128]{2,1,0:T(8,128)S(1)}, f32[36,8,128]{2,1,0:T(8,128)S(1)}, u32[]{:S(2)}, u32[]{:S(2)}) collective-permute-start(f32[36,8,128]{2,1,0:T(8,128)S(1)} %get-tuple-element.49.refs_9_), channel_id=1, source_target_pairs={{0,3},{1,0},{2,1},{3,2},{4,7},{5,4},{6,5},{7,6},{8,11},{9,8},{10,9... | collective-permute-start | bytes 442376 | tf_op jit(solution)/shard_map/ppermute | solution.py:333
  149.8 19.9 %collective-permute-start.29 = (f32[36,8,128]{2,1,0:T(8,128)S(1)}, f32[36,8,128]{2,1,0:T(8,128)S(1)}, u32[]{:S(2)}, u32[]{:S(2)}) collective-permute-start(f32[36,8,128]{2,1,0:T(8,128)S(1)} %get-tuple-element.50.refs_10_), channel_id=1, source_target_pairs={{0,2},{1,3},{2,0},{3,1},{4,6},{5,7},{6,4},{7,5},{8,10},{9,11},{10,... | collective-permute-start | bytes 442376 | tf_op jit(solution)/shard_map/ppermute | solution.py:333
  150.3 19.3 %collective-permute-start.30 = (f32[36,8,128]{2,1,0:T(8,128)S(1)}, f32[36,8,128]{2,1,0:T(8,128)S(1)}, u32[]{:S(2)}, u32[]{:S(2)}) collective-permute-start(f32[36,8,128]{2,1,0:T(8,128)S(1)} %get-tuple-element.51.refs_11_), channel_id=1, source_target_pairs={{0,1},{1,2},{2,3},{3,0},{4,5},{5,6},{6,7},{7,4},{8,9},{9,10},{10,1... | collective-permute-start | bytes 442376 | tf_op jit(solution)/shard_map/ppermute | solution.py:333
  (29 other events, 411.7 us)

commit v2 on v1

--- a/solution.py
+++ b/solution.py
@@ -12,7 +12,7 @@
 DEGREE = 3
 SUB = 8
 LANES = 128
-VMEM = pltpu.CompilerParams(vmem_limit_bytes=48 * 1024 * 1024)
+PARAMS = pltpu.CompilerParams(vmem_limit_bytes=24 * 1024 * 1024)
 
 
 def term_list(modes):
@@ -73,14 +73,10 @@
 def apply_operator(u_ref, coef_ref, edges, store, diff_ref):
     terms = len(edges)
 
-    def differences(s, carry):
-        u = u_ref[s]
-        diff_ref[0, s] = pltpu.roll(u, SUB - 1, 0) - u
-        diff_ref[1, s] = u - lane_next(u)
-        diff_ref[2, s] = u - lane_before(u)
-        return carry
-
-    lax.fori_loop(0, terms, differences, 0, unroll=2)
+    u = u_ref[0:terms]
+    diff_ref[0, 0:terms] = pltpu.roll(u, SUB - 1, 1) - u
+    diff_ref[1, 0:terms] = u - lane_next(u)
+    diff_ref[2, 0:terms] = u - lane_before(u)
     east, right, left = face_coefficients(coef_ref)
     for s in range(terms):
         groups = {1: [(s, 0)]}
@@ -129,10 +125,10 @@
     return flat_ref[pl.ds(j, rows, stride=SUB), :]
 
 
-def enter_kernel(n, columns, ranks_ref, *refs):
+def enter_kernel(n, columns, rows, ranks_ref, coef_ref, *refs):
     parts, (field_ref, first_ref, last_ref) = refs[:n], refs[n:]
-    rows = parts[0].shape[0]
     slots = field_ref.shape[0]
+    fields = coef_ref.shape[0]
     field_ref[...] = jnp.zeros_like(field_ref)
     for d, part in enumerate(parts):
 
@@ -142,17 +138,30 @@
 
         lax.fori_loop(0, rows, one, 0, unroll=4)
     flat = field_ref.reshape(slots * SUB, LANES)
-    first_ref[...] = take_column(flat, 0, slots)
-    last_ref[...] = take_column(flat, columns - 1, slots)
-
-
-def start_kernel(n, columns, edges, ranks_ref, x_ref, before_ref, after_ref, coef_ref, *refs):
-    packed, (u_ref, y_ref, diff_ref) = refs[:n], refs[n:]
-    slots = x_ref.shape[0]
+    first_ref[slots:] = jnp.zeros_like(first_ref[slots:])
+    last_ref[slots:] = jnp.zeros_like(last_ref[slots:])
+    first_ref[0:slots] = take_column(flat, 0, slots)
+    last_ref[0:slots] = take_column(flat, columns - 1, slots)
+    flat = coef_ref.reshape(fields * SUB, LANES)
+    for j in range(2):
+        at = slots + j * fields
+        first_ref[at : at + fields] = take_column(flat, j, fields)
+        last_ref[at : at + fields] = take_column(flat, columns - 2 + j, fields)
+
+
+def start_kernel(n, columns, edges, ranks_ref, x_ref, before_ref, after_ref, own_ref, *refs):
+    packed, (coef_ref, u_ref, y_ref, diff_ref) = refs[:n], refs[n:]
+    slots, fields = x_ref.shape[0], own_ref.shape[0]
+    coef_ref[...] = own_ref[...]
+    flat = coef_ref.reshape(fields * SUB, LANES)
+    for j in range(2):
+        at = slots + j * fields
+        flat[pl.ds(SUB - 2 + j, fields, stride=SUB), :] = before_ref[at : at + fields]
+        flat[pl.ds(columns + j, fields, stride=SUB), :] = after_ref[at : at + fields]
     u_ref[...] = x_ref[...]
     flat = u_ref.reshape(slots * SUB, LANES)
-    flat[pl.ds(SUB - 1, slots, stride=SUB), :] = before_ref[...]
-    flat[pl.ds(columns, slots, stride=SUB), :] = after_ref[...]
+    flat[pl.ds(SUB - 1, slots, stride=SUB), :] = before_ref[0:slots]
+    flat[pl.ds(columns, slots, stride=SUB), :] = after_ref[0:slots]
     y_ref[len(edges) :] = jnp.zeros((slots - len(edges), SUB, LANES), jnp.float32)
 
     def store(s, value):
@@ -165,21 +174,19 @@
 def residual_kernel(n, columns, ranks_ref, *refs):
     forcing, image = refs[:n], refs[n : 2 * n]
     packed = refs[2 * n : 3 * n]
-    field_ref, first_ref, last_ref, sum_ref = refs[3 * n :]
+    field_ref, first_ref, last_ref = refs[3 * n :]
     rows = forcing[0].shape[0]
     slots = field_ref.shape[0]
     field_ref[...] = jnp.zeros_like(field_ref)
-    total = jnp.zeros((SUB, LANES), jnp.float32)
     for d in range(n):
 
-        def one(q, total, d=d):
+        def one(q, carry, d=d):
             v = forcing[d][q] - image[d][q]
             packed[d][q] = v
             scatter_row(ranks_ref, d * rows + q, v, field_ref, columns)
-            return total + v * v
-
-        total = lax.fori_loop(0, rows, one, total, unroll=4)
-    sum_ref[...] = total
+            return carry
+
+        lax.fori_loop(0, rows, one, 0, unroll=4)
     flat = field_ref.reshape(slots * SUB, LANES)
     for j in range(2):
         first_ref[j] = take_column(flat, j, slots)
@@ -187,7 +194,7 @@
 
 
 def first_kernel(n, columns, edges, ranks_ref, v_ref, before_ref, after_ref, coef_ref, inside_ref, *refs):
-    packed, (out_ref, sum_ref), (u_ref, diff_ref) = refs[:n], refs[n : n + 2], refs[n + 2 :]
+    packed, (out_ref, u_ref, diff_ref) = refs[:n], refs[n:]
     slots = v_ref.shape[0]
     u_ref[...] = v_ref[...]
     flat = u_ref.reshape(slots * SUB, LANES)
@@ -201,12 +208,6 @@
         out_ref[s] = jnp.where(inside, value, 0.0)
 
     apply_operator(u_ref, coef_ref, edges, store, diff_ref)
-    own = lax.broadcasted_iota(jnp.int32, (SUB, LANES), 0) < columns
-
-    def dot(s, total):
-        return total + jnp.where(own, u_ref[s] * out_ref[s], 0.0)
-
-    sum_ref[...] = lax.fori_loop(0, len(edges), dot, jnp.zeros((SUB, LANES), jnp.float32), unroll=4)
     pack_rows(ranks_ref, packed, out_ref, columns)
 
 
@@ -222,41 +223,63 @@
     pack_rows(ranks_ref, packed, y_ref, columns)
 
 
-def lines_of(sums_ref, count):
-    full = jnp.sum(sums_ref[...], axis=1, keepdims=True)
-    return [full[i : i + 1] for i in range(count)]
-
-
-def dots_kernel(n, sums_ref, *refs):
+def row_sums(n, rows, of_row, count):
+    totals = (jnp.zeros((SUB, LANES), jnp.float32),) * count
+    for d in range(n):
+
+        def one(q, totals, d=d):
+            return tuple(t + x for t, x in zip(totals, of_row(d, q)))
+
+        totals = lax.fori_loop(0, rows, one, totals, unroll=4)
+    return [jnp.sum(jnp.sum(t, axis=0, keepdims=True), axis=1, keepdims=True) for t in totals]
+
+
+def dots_kernel(n, place_ref, *refs):
     v0, v1, v2, out_ref = refs[:n], refs[n : 2 * n], refs[2 * n : 3 * n], refs[3 * n]
     rows = v0[0].shape[0]
-    s00, s01 = lines_of(sums_ref, 2)
-    step = s00 / s01
-    totals = (jnp.zeros((SUB, LANES), jnp.float32),) * 4
-    for d in range(n):
-
-        def one(q, totals, d=d):
-            a, b, c = v0[d][q], v1[d][q], v2[d][q]
-            r = a - step * b
-            image = b - step * c
-            return tuple(t + x for t, x in zip(totals, (r * r, r * image, r * b, a * image)))
-
-        totals = lax.fori_loop(0, rows, one, totals, unroll=4)
-    out_ref[...] = jnp.zeros_like(out_ref)
-    for i, t in enumerate(totals):
-        out_ref[i : i + 1] = jnp.sum(t, axis=0, keepdims=True)
-
-
-def finish_kernel(n, columns, offsets_ref, first_ref, second_ref, x_ref, f_ref, *refs):
+    aa, ab = row_sums(n, rows, lambda d, q: (v0[d][q] * v0[d][q], v0[d][q] * v1[d][q]), 2)
+    m = jnp.where(aa > 0.0, ab / jnp.where(aa > 0.0, aa, 1.0), 0.0)
+
+    def products(d, q):
+        a, b, c = v0[d][q], v1[d][q], v2[d][q]
+        w = b - m * a
+        e = c - m * b
+        return a * w, w * w, a * e, w * b, w * e
+
+    entries = [aa, ab, m] + row_sums(n, rows, products, 5)
+    lane = lax.broadcasted_iota(jnp.int32, out_ref.shape, 1)
+    row = lax.broadcasted_iota(jnp.int32, out_ref.shape, 0)
+    table = jnp.zeros(out_ref.shape, jnp.float32)
+    for k, value in enumerate(entries):
+        table = jnp.where(lane == k, value, table)
+    out_ref[...] = jnp.where(row == place_ref[0], table, 0.0)
+
+
+def step_lengths(table):
+    lane = lax.broadcasted_iota(jnp.int32, table.shape, 1)
+    aa, ab, m, aw, ww, ae, wb, we = (
+        jnp.sum(jnp.where(lane == k, table, 0.0), axis=1, keepdims=True) for k in range(8)
+    )
+
+    def total(x):
+        return jnp.sum(x, axis=0, keepdims=True)
+
+    norm, curve = total(aa), total(ab)
+    step = norm / curve
+    g = 1.0 - step * m
+    rr = total(g * g * aa - 2.0 * g * step * aw + step * step * ww)
+    r_ar = total(g * g * ab - g * step * (ae + wb) + step * step * we)
+    mixed = total(2.0 * g * ab - step * (wb + ae))
+    beta = rr / norm
+    return step, beta, rr / (r_ar + beta * mixed + beta * beta * curve)
+
+
+def finish_kernel(n, columns, offsets_ref, table_ref, x_ref, f_ref, *refs):
     image, v1, v2 = refs[:n], refs[n : 2 * n], refs[2 * n : 3 * n]
     approx_ref, residual_ref = refs[3 * n :]
     per = SUB // columns
     rows = image[0].shape[0]
-    s00, s01 = lines_of(first_ref, 2)
-    rr, r_ar, r_v1, v0_ar = lines_of(second_ref, 4)
-    step = s00 / s01
-    beta = rr / s00
-    last = rr / (r_ar + beta * (r_v1 + v0_ar) + beta * beta * s01)
+    step, beta, last = step_lengths(table_ref[...])
     whole = step + last * beta
     for d in range(n):
         at = pl.ds(pl.multiple_of(offsets_ref[d], columns), columns)
@@ -284,7 +307,7 @@
         out_specs=[whole] * len(outs),
         out_shape=[jax.ShapeDtypeStruct(s, jnp.float32) for s in outs],
         scratch_shapes=[pltpu.VMEM(s, jnp.float32) for s in scratch],
-        compiler_params=VMEM,
+        compiler_params=PARAMS,
     )(*scalars, *arrays)
 
 
@@ -336,23 +359,10 @@
     tag = jnp.pad(rank.astype(jnp.float32)[None, None], ((0, 0), (0, SUB - 1), (0, lanes - here)))
     x_parts = sent([jnp.concatenate([cut(start_guess, d), tag], axis=0) for d in range(n)], outward)
     ranks = jnp.concatenate([p[rows, 0, :here] for p in x_parts]).astype(jnp.int32)
-    x_parts = [p[:rows] for p in x_parts]
     f_parts = sent([cut(forcing, d) for d in range(n)], outward)
 
     stacked = jnp.concatenate([mean_field[None], mode_fields], axis=0)
-    up = [(j, j + 1) for j in range(spaces - 1)]
-    down = [(j + 1, j) for j in range(spaces - 1)]
-    coef = jnp.concatenate(
-        [
-            lax.ppermute(stacked[:, width - 2 :], "space", up),
-            stacked,
-            lax.ppermute(stacked[:, :2], "space", down),
-        ],
-        axis=1,
-    )
-    coef = columns_at(coef, offsets[0], columns + 4)
-    gap = jnp.zeros((modes + 1, SUB - columns - 4, lanes), jnp.float32)
-    coef = jnp.concatenate([coef[:, 2:], gap, coef[:, :2]], axis=1)
+    own_coef = jnp.pad(columns_at(stacked, offsets[0], columns), ((0, 0), (0, SUB - columns), (0, 0)))
     sub = lax.broadcasted_iota(jnp.int32, (SUB, lanes), 0)
     position = i * n + chunk(i, z)
     outside = ((position == 0) & (sub >= SUB - 2)) | (
@@ -360,43 +370,42 @@
     )
     inside = jnp.where(outside, 0.0, 1.0)
 
-    field, part, small = (slots, SUB, lanes), (rows, SUB, lanes), (SUB, lanes)
+    field, part, fields = (slots, SUB, lanes), (rows, SUB, lanes), (modes + 1, SUB, lanes)
     diff = (3,) + field
+    edge = (-(-(slots + 2 * (modes + 1)) // SUB) * SUB, lanes)
 
     x, x_first, x_last = call(
-        functools.partial(enter_kernel, n, columns),
+        functools.partial(enter_kernel, n, columns, rows),
         [ranks],
-        x_parts,
-        [field, (slots, lanes), (slots, lanes)],
+        [own_coef] + x_parts,
+        [field, edge, edge],
     )
     x_before = lax.ppermute(x_last, both, line)
     x_after = lax.ppermute(x_first, both, back_line)
-    image = call(
+    *image, coef = call(
         functools.partial(start_kernel, n, columns, edges),
         [ranks],
-        [x, x_before, x_after, coef],
-        [part] * n,
+        [x, x_before, x_after, own_coef],
+        [part] * n + [fields],
         [field, field, diff],
     )
-    *v0_parts, v0, v0_first, v0_last, sum00 = call(
+    *v0_parts, v0, v0_first, v0_last = call(
         functools.partial(residual_kernel, n, columns),
         [ranks],
-        f_parts + list(image),
-        [part] * n + [field, (2, slots, lanes), (2, slots, lanes), small],
+        f_parts + image,
+        [part] * n + [field, (2, slots, lanes), (2, slots, lanes)],
     )
     v0_before = lax.ppermute(v0_last, both, line)
     v0_after = lax.ppermute(v0_first, both, back_line)
-    image_home = sent(list(image), homeward)
-    *v1_parts, v1, sum01 = call(
+    image_home = sent(image, homeward)
+    *v1_parts, v1 = call(
         functools.partial(first_kernel, n, columns, edges),
         [ranks],
         [v0, v0_before, v0_after, coef, inside],
-        [part] * n + [field, small],
+        [part] * n + [field],
         [field, diff],
     )
     v1_home = sent(v1_parts, homeward)
-    sums = jnp.stack([jnp.sum(sum00, axis=0), jnp.sum(sum01, axis=0)])
-    sums = butterfly(jnp.pad(sums, ((0, SUB - 2), (0, 0))), (spaces, n))
     v2_parts = call(
         functools.partial(second_kernel, n, columns, edges),
         [ranks],
@@ -405,17 +414,17 @@
         [field, diff],
     )
     v2_home = sent(list(v2_parts), homeward)
-    (dots,) = call(
+    (table,) = call(
         functools.partial(dots_kernel, n),
-        [],
-        [sums] + v0_parts + v1_parts + list(v2_parts),
-        [small],
-    )
-    dots = butterfly(dots, (spaces, n))
+        [(i * n + z).astype(jnp.int32)[None]],
+        v0_parts + v1_parts + list(v2_parts),
+        [(-(-spaces * n // SUB) * SUB, lanes)],
+    )
+    table = butterfly(table, (spaces, n))
     return call(
         functools.partial(finish_kernel, n, columns),
         [jnp.stack(offsets).astype(jnp.int32)],
-        [sums, dots, start_guess, forcing] + image_home + v1_home + v2_home,
+        [table, start_guess, forcing] + image_home + v1_home + v2_home,
         [forcing.shape] * 2,
     )
 

time: 173 us -> 124 us (0.72)
  waiting for transfers between devices: 71.9 us -> 41.1 us
  Pallas kernels: 48.5 us -> 19.6 us
  starting transfers between devices: 43.2 us -> 50.2 us
  other arithmetic: 1.32 us -> 3.16 us
    pallas_call x7, Pallas kernels: 48.5 us -> 19.6 us  [call(): pl.pallas_call(kernel, in_specs=[pl.BlockSpec(memory_space=pltpu.SMEM)] *...]
    ppermute x15, waiting for transfers between devices: 41.4 us -> 26.3 us  [sent(): lax.ppermute(parts[d], 'chaos', way(d))]
    ppermute x10 -> x5, waiting for transfers between devices: 16.3 us -> 6.52 us  [butterfly(): lax.ppermute(value, ('space', 'chaos'), [(i, i ^ bit) for i in range(coun...]
    ppermute x1, waiting for transfers between devices: 5.7 us -> 1.25 us  [per_device(): v0_after = lax.ppermute(v0_first, both, back_line)]
    ppermute x2 -> x0, starting transfers between devices: 4.32 us -> none  [the longest x1 3.03 us: per_device(): lax.ppermute(stacked[:, width - 2:], 'space', up)]
    ppermute x1, starting transfers between devices: 1.86 us -> 5.63 us  [per_device(): x_before = lax.ppermute(x_last, both, line)]
    ppermute x1, starting transfers between devices: 1.92 us -> 5.13 us  [per_device(): v0_before = lax.ppermute(v0_last, both, line)]
    ppermute x15, starting transfers between devices: 24.7 us -> 27.2 us  [sent(): lax.ppermute(parts[d], 'chaos', way(d))]
  transfers between devices with their start and end apart: 31 -> 24, of which waited for: 16 -> 12; matrix products, arithmetic and copies ran while one was open for 1% -> 1% of each run, Pallas kernels for 17% -> 11%
where the time goes in v2:
time: 124 us; the launch traced here: 123 us
  starting transfers between devices  50.2 us (40%)
  waiting for transfers between devices  41.1 us (33%)
  Pallas kernels  19.6 us (16%)
  local copies, waits for them, and re-layouts  8.23 us (7%)
  other arithmetic  3.16 us (3%)
    ppermute x15, starting transfers between devices, sent(): lax.ppermute(parts[d], 'chaos', way(d))  27.2 us
    ppermute x15, waiting for transfers between devices, sent(): lax.ppermute(parts[d], 'chaos', way(d))  26.3 us
    pallas_call x7, Pallas kernels, call(): pl.pallas_call(kernel, in_specs=[pl.BlockSpec(memory_space=pltpu.SMEM)] *...  19.6 us
    ppermute x5, starting transfers between devices, butterfly(): lax.ppermute(value, ('space', 'chaos'), [(i, i ^ bit) for i in range(coun...  9.64 us
    ppermute x5, waiting for transfers between devices, butterfly(): lax.ppermute(value, ('space', 'chaos'), [(i, i ^ bit) for i in range(coun...  6.52 us
    unnamed x24, local copies, waits for them, and re-layouts  6.29 us
    ppermute x1, starting transfers between devices, per_device(): x_before = lax.ppermute(x_last, both, line)  5.63 us
    ppermute x1, starting transfers between devices, per_device(): v0_before = lax.ppermute(v0_last, both, line)  5.13 us
  transfers between devices with their start and end apart: 24, of which 12 were waited for; matrix products, arithmetic and copies ran while one was open for 1% of the time, Pallas kernels for 11%

profile of v2, /device:TPU:0, one launch (start us, length us, event | category | flops | bytes accessed | tf_op | source)
XLA Modules:
  0.0 123.2 jit_solution(6647785219188023456)
XLA Ops:
  2.9 1.9 %constant_dynamic-slice_fusion = (f32[72,4,128]{2,1,0:T(4,128)S(1)}, f32[72,4,128]{2,1,0:T(4,128)S(1)}, f32[72,4,128]{2,1,0:T(4,128)S(1)}, f32[72,4,128]{2,1,0:T...) fusion(f32[72,16,128]{2,1,0:T(8,128)} %x_ref.1, ...), kind=kLoop, calls=%fused_computation.14 | loop fusion | bytes 2359312 | tf_op jit(solution)/shard_map/dynamic_slice | solution.py:50
  4.9 3.1 %collective-permute-start = (f32[37,8,128]{2,1,0:T(8,128)S(1)}, f32[37,8,128]{2,1,0:T(8,128)S(1)}, u32[]{:S(2)}, u32[]{:S(2)}) collective-permute-start(f32[37,8,128]{2,1,0:T(8,128)S(1)} %get-tuple-element.62), channel_id=1, source_target_pairs={{0,1},{1,2},{2,3},{3,0},{4,5},{5,6},{6,7},{7,4},{8,9},{9,10},{10,1... | collective-permute-start | bytes 454664 | tf_op jit(solution)/shard_map/ppermute | solution.py:356
  8.0 2.6 %collective-permute-start.1 = (f32[37,8,128]{2,1,0:T(8,128)S(1)}, f32[37,8,128]{2,1,0:T(8,128)S(1)}, u32[]{:S(2)}, u32[]{:S(2)}) collective-permute-start(f32[37,8,128]{2,1,0:T(8,128)S(1)} %get-tuple-element.63), channel_id=1, source_target_pairs={{0,2},{1,3},{2,0},{3,1},{4,6},{5,7},{6,4},{7,5},{8,10},{9,11},{10,... | collective-permute-start | bytes 454664 | tf_op jit(solution)/shard_map/ppermute | solution.py:356
  12.6 2.2 %collective-permute-done.refs_1_ = f32[37,8,128]{2,1,0:T(8,128)S(1)} collective-permute-done((f32[37,8,128]{2,1,0:T(8,128)S(1)}, f32[37,8,128]{2,1,0:T(8,128)S(1)}, u32[]{:S(2)}, u32[]{:S(2)}) %collective-permute-start) | collective-permute-done | bytes 151584 | tf_op jit(solution)/shard_map/ppermute | solution.py:356
  14.9 5.6 %collective-permute-done.1.refs_2_ = f32[37,8,128]{2,1,0:T(8,128)S(1)} collective-permute-done((f32[37,8,128]{2,1,0:T(8,128)S(1)}, f32[37,8,128]{2,1,0:T(8,128)S(1)}, u32[]{:S(2)}, u32[]{:S(2)}) %collective-permute-start.1) | collective-permute-done | bytes 151584 | tf_op jit(solution)/shard_map/ppermute | solution.py:356
  21.8 5.6 %collective-permute-start.6 = (f32[312,128]{1,0:T(8,128)S(1)}, f32[312,128]{1,0:T(8,128)S(1)}, u32[]{:S(2)}, u32[]{:S(2)}) collective-permute-start(f32[312,128]{1,0:T(8,128)S(1)} %get-tuple-element.27), channel_id=1, source_target_pairs={{0,1},{1,2},{2,3},{3,7},{7,6},{6,5},{5,4},{4,8},{8,9},{9,10},{10,1... | collective-permute-start | bytes 479240 | tf_op jit(solution)/shard_map/ppermute | solution.py:383
  28.7 2.7 %collective-permute-start.3 = (f32[36,8,128]{2,1,0:T(8,128)S(1)}, f32[36,8,128]{2,1,0:T(8,128)S(1)}, u32[]{:S(2)}, u32[]{:S(2)}) collective-permute-start(f32[36,8,128]{2,1,0:T(8,128)S(1)} %bitcast.50), channel_id=1, source_target_pairs={{0,1},{1,2},{2,3},{3,0},{4,5},{5,6},{6,7},{7,4},{8,9},{9,10},{10,1... | collective-permute-start | bytes 442376 | tf_op jit(solution)/shard_map/ppermute | solution.py:356
  34.0 5.1 %collective-permute-done.7.after_ref = f32[312,128]{1,0:T(8,128)S(1)} collective-permute-done((f32[312,128]{1,0:T(8,128)S(1)}, f32[312,128]{1,0:T(8,128)S(1)}, u32[]{:S(2)}, u32[]{:S(2)}) %collective-permute-start.7) | collective-permute-done | bytes 159776 | tf_op jit(solution)/shard_map/ppermute | solution.py:384
  39.1 3.9 %shard_map.78 = (f32[36,8,128]{2,1,0:T(8,128)S(1)}, f32[36,8,128]{2,1,0:T(8,128)S(1)}, f32[36,8,128]{2,1,0:T(8,128)S(1)}, f32[36,8,128]{2,1,0:T(8,128)S(1)}, f32[11,8,128]{2,1,0:T(8,128)S(1)}) custom-call(s32[288]{0:T(512)S(1)} %maximum_convert_fusion.ranks_ref, f32[288,8,128]{2,1,0:T(8,128)S(1)} %get-tuple-element.26.x_ref, ...), custom_call_target="tpu_custom_call" | custom-call | tf_op jit(solution)/shard_map/pallas_call | solution.py:304
  44.2 2.0 %shard_map.79 = (f32[36,8,128]{2,1,0:T(8,128)S(1)}, f32[36,8,128]{2,1,0:T(8,128)S(1)}, f32[36,8,128]{2,1,0:T(8,128)S(1)}, f32[36,8,128]{2,1,0:T(8,128)S(1)}, f32...) custom-call(s32[288]{0:T(512)S(1)} %maximum_convert_fusion.ranks_ref, ...), custom_call_target="tpu_custom_call" | custom-call | tf_op jit(solution)/shard_map/pallas_call | solution.py:304
  48.9 5.1 %collective-permute-start.8 = (f32[2,288,128]{2,1,0:T(8,128)}, f32[2,288,128]{2,1,0:T(8,128)S(1)}, u32[]{:S(2)}, u32[]{:S(2)}) collective-permute-start(f32[2,288,128]{2,1,0:T(8,128)} %get-tuple-element.38), channel_id=1, source_target_pairs={{0,1},{1,2},{2,3},{3,7},{7,6},{6,5},{5,4},{4,8},{8,9},{9,10},{10,1... | collective-permute-start | bytes 884744 | tf_op jit(solution)/shard_map/ppermute | solution.py:398
  55.4 3.5 %collective-permute-start.15 = (f32[36,8,128]{2,1,0:T(8,128)S(1)}, f32[36,8,128]{2,1,0:T(8,128)S(1)}, u32[]{:S(2)}, u32[]{:S(2)}) collective-permute-start(f32[36,8,128]{2,1,0:T(8,128)S(1)} %get-tuple-element.30.refs_5_), channel_id=1, source_target_pairs={{0,3},{1,0},{2,1},{3,2},{4,7},{5,4},{6,5},{7,6},{8,11},{9,8},{10,9... | collective-permute-start | bytes 442376 | tf_op jit(solution)/shard_map/ppermute | solution.py:356
  59.5 1.9 %collective-permute-done.8.before_ref = f32[2,288,128]{2,1,0:T(8,128)S(1)} collective-permute-done((f32[2,288,128]{2,1,0:T(8,128)}, f32[2,288,128]{2,1,0:T(8,128)S(1)}, u32[]{:S(2)}, u32[]{:S(2)}) %collective-permute-start.8) | collective-permute-done | bytes 294944 | tf_op jit(solution)/shard_map/ppermute | solution.py:398
  62.8 3.8 %shard_map.80 = (f32[36,8,128]{2,1,0:T(8,128)S(1)}, f32[36,8,128]{2,1,0:T(8,128)S(1)}, f32[36,8,128]{2,1,0:T(8,128)S(1)}, f32[36,8,128]{2,1,0:T(8,128)S(1)}, f32[288,8,128]{2,1,0:T(8,128)S(1)}) custom-call(s32[288]{0:T(512)S(1)} %maximum_convert_fusion.ranks_ref, f32[288,8,128]{2,1,0:T(8,128)S(1)} %get-tuple-element.37.v_ref, ...), custom_call_target="tpu_custom_call" | custom-call | tf_op jit(solution)/shard_map/pallas_call | solution.py:304
  66.6 4.4 %shard_map.81 = (f32[36,8,128]{2,1,0:T(8,128)S(1)}, f32[36,8,128]{2,1,0:T(8,128)}, f32[36,8,128]{2,1,0:T(8,128)S(1)}, f32[36,8,128]{2,1,0:T(8,128)S(1)}) custom-call(s32[288]{0:T(512)S(1)} %maximum_convert_fusion.ranks_ref, f32[288,8,128]{2,1,0:T(8,128)S(1)} %get-tuple-element.45.v_ref, f32[11,8,128]{2,1,0:T(8,128)S(1)} %get-tuple-element.40.coef_ref), custom_call_target="tpu_custom_call" | custom-call | tf_op jit(solution)/shard_map/pallas_call | solution.py:304
  71.0 3.4 %collective-permute-start.21 = (f32[36,8,128]{2,1,0:T(8,128)}, f32[36,8,128]{2,1,0:T(8,128)S(1)}, u32[]{:S(2)}, u32[]{:S(2)}) collective-permute-start(f32[36,8,128]{2,1,0:T(8,128)} %get-tuple-element.47.refs_9_), channel_id=1, source_target_pairs={{0,3},{1,0},{2,1},{3,2},{4,7},{5,4},{6,5},{7,6},{8,11},{9,8},{10,9... | collective-permute-start | bytes 442376 | tf_op jit(solution)/shard_map/ppermute | solution.py:356
  79.9 2.9 %collective-permute-start.10 = (f32[32,128]{1,0:T(8,128)S(1)}, f32[32,128]{1,0:T(8,128)S(1)}, u32[]{:S(2)}, u32[]{:S(2)}) collective-permute-start(f32[32,128]{1,0:T(8,128)S(1)} %shard_map.82), channel_id=1, source_target_pairs={{0,1},{1,0},{2,3},{3,2},{4,5},{5,4},{6,7},{7,6},{8,9},{9,8},{10,11... | collective-permute-start | bytes 49160 | tf_op jit(solution)/shard_map/ppermute | solution.py:318
  84.5 3.4 %collective-permute-start.11 = (f32[32,128]{1,0:T(8,128)S(1)}, f32[32,128]{1,0:T(8,128)S(1)}, u32[]{:S(2)}, u32[]{:S(2)}) collective-permute-start(f32[32,128]{1,0:T(8,128)S(1)} %add.185), channel_id=1, source_target_pairs={{0,2},{1,3},{2,0},{3,1},{4,6},{5,7},{6,4},{7,5},{8,10},{9,11},{10,... | collective-permute-start | bytes 49160 | tf_op jit(solution)/shard_map/ppermute | solution.py:318
  92.3 2.2 %collective-permute-done.13 = f32[32,128]{1,0:T(8,128)S(1)} collective-permute-done((f32[32,128]{1,0:T(8,128)S(1)}, f32[32,128]{1,0:T(8,128)S(1)}, u32[]{:S(2)}, u32[]{:S(2)}) %collective-permute-start.13) | collective-permute-done | bytes 16416 | tf_op jit(solution)/shard_map/ppermute | solution.py:318
  96.1 2.9 %collective-permute-start.22 = (f32[36,8,128]{2,1,0:T(8,128)S(1)}, f32[36,8,128]{2,1,0:T(8,128)S(1)}, u32[]{:S(2)}, u32[]{:S(2)}) collective-permute-start(f32[36,8,128]{2,1,0:T(8,128)S(1)} %get-tuple-element.48.refs_10_), channel_id=1, source_target_pairs={{0,2},{1,3},{2,0},{3,1},{4,6},{5,7},{6,4},{7,5},{8,10},{9,11},{10,... | collective-permute-start | bytes 442376 | tf_op jit(solution)/shard_map/ppermute | solution.py:356
  99.0 3.8 %collective-permute-start.18 = (f32[36,8,128]{2,1,0:T(8,128)S(1)}, f32[36,8,128]{2,1,0:T(8,128)S(1)}, u32[]{:S(2)}, u32[]{:S(2)}) collective-permute-start(f32[36,8,128]{2,1,0:T(8,128)S(1)} %get-tuple-element.42.refs_5_), channel_id=1, source_target_pairs={{0,3},{1,0},{2,1},{3,2},{4,7},{5,4},{6,5},{7,6},{8,11},{9,8},{10,9... | collective-permute-start | bytes 442376 | tf_op jit(solution)/shard_map/ppermute | solution.py:356
  103.6 6.1 %collective-permute-done.22.refs_10_ = f32[36,8,128]{2,1,0:T(8,128)S(1)} collective-permute-done((f32[36,8,128]{2,1,0:T(8,128)S(1)}, f32[36,8,128]{2,1,0:T(8,128)S(1)}, u32[]{:S(2)}, u32[]{:S(2)}) %collective-permute-start.22) | collective-permute-done | bytes 147488 | tf_op jit(solution)/shard_map/ppermute | solution.py:356
  109.7 11.0 %collective-permute-done.19.refs_6_ = f32[36,8,128]{2,1,0:T(8,128)S(1)} collective-permute-done((f32[36,8,128]{2,1,0:T(8,128)S(1)}, f32[36,8,128]{2,1,0:T(8,128)S(1)}, u32[]{:S(2)}, u32[]{:S(2)}) %collective-permute-start.19) | collective-permute-done | bytes 147488 | tf_op jit(solution)/shard_map/ppermute | solution.py:356
  120.7 2.5 %shard_map.83 = (f32[72,16,128]{2,1,0:T(8,128)}, f32[72,16,128]{2,1,0:T(8,128)}) custom-call(s32[4]{0:T(128)S(1)} %pad_add_fusion.offsets_ref, f32[32,128]{1,0:T(8,128)S(1)} %add.189.table_ref, f32[72,16,128]{2,1,0:T(8,128)S(1)} %copy-done, f32[72,16,128]{2,1,0:T(8,128)S(1)} %copy-done.1, f32[36,8,128]{2,1,0:T(8,128)S(1)} %get-tuple-element.29.refs_4_.refs_0_, ...), custom_call_target="tpu_custom_call" | custom-call | tf_op jit(solution)/shard_map/pallas_call | solution.py:304
  (76 shorter events, 30.5 us)
Async XLA Ops:
  4.9 10.0 %collective-permute-start = (f32[37,8,128]{2,1,0:T(8,128)S(1)}, f32[37,8,128]{2,1,0:T(8,128)S(1)}, u32[]{:S(2)}, u32[]{:S(2)}) collective-permute-start(f32[37,8,128]{2,1,0:T(8,128)S(1)} %get-tuple-element.62), channel_id=1, source_target_pairs={{0,1},{1,2},{2,3},{3,0},{4,5},{5,6},{6,7},{7,4},{8,9},{9,10},{10,1... | collective-permute-start | bytes 454664 | tf_op jit(solution)/shard_map/ppermute | solution.py:356
  8.0 12.5 %collective-permute-start.1 = (f32[37,8,128]{2,1,0:T(8,128)S(1)}, f32[37,8,128]{2,1,0:T(8,128)S(1)}, u32[]{:S(2)}, u32[]{:S(2)}) collective-permute-start(f32[37,8,128]{2,1,0:T(8,128)S(1)} %get-tuple-element.63), channel_id=1, source_target_pairs={{0,2},{1,3},{2,0},{3,1},{4,6},{5,7},{6,4},{7,5},{8,10},{9,11},{10,... | collective-permute-start | bytes 454664 | tf_op jit(solution)/shard_map/ppermute | solution.py:356
  10.6 10.0 %collective-permute-start.2 = (f32[37,8,128]{2,1,0:T(8,128)S(1)}, f32[37,8,128]{2,1,0:T(8,128)S(1)}, u32[]{:S(2)}, u32[]{:S(2)}) collective-permute-start(f32[37,8,128]{2,1,0:T(8,128)S(1)} %get-tuple-element.64), channel_id=1, source_target_pairs={{0,3},{1,0},{2,1},{3,2},{4,7},{5,4},{6,5},{7,6},{8,11},{9,8},{10,9... | collective-permute-start | bytes 454664 | tf_op jit(solution)/shard_map/ppermute | solution.py:356
  21.8 12.2 %collective-permute-start.6 = (f32[312,128]{1,0:T(8,128)S(1)}, f32[312,128]{1,0:T(8,128)S(1)}, u32[]{:S(2)}, u32[]{:S(2)}) collective-permute-start(f32[312,128]{1,0:T(8,128)S(1)} %get-tuple-element.27), channel_id=1, source_target_pairs={{0,1},{1,2},{2,3},{3,7},{7,6},{6,5},{5,4},{4,8},{8,9},{9,10},{10,1... | collective-permute-start | bytes 479240 | tf_op jit(solution)/shard_map/ppermute | solution.py:383
  27.4 11.6 %collective-permute-start.7 = (f32[312,128]{1,0:T(8,128)S(1)}, f32[312,128]{1,0:T(8,128)S(1)}, u32[]{:S(2)}, u32[]{:S(2)}) collective-permute-start(f32[312,128]{1,0:T(8,128)S(1)} %get-tuple-element.28), channel_id=1, source_target_pairs={{1,0},{2,1},{3,2},{7,3},{6,7},{5,6},{4,5},{8,4},{9,8},{10,9},{11,1... | collective-permute-start | bytes 479240 | tf_op jit(solution)/shard_map/ppermute | solution.py:384
  28.7 14.2 %collective-permute-start.3 = (f32[36,8,128]{2,1,0:T(8,128)S(1)}, f32[36,8,128]{2,1,0:T(8,128)S(1)}, u32[]{:S(2)}, u32[]{:S(2)}) collective-permute-start(f32[36,8,128]{2,1,0:T(8,128)S(1)} %bitcast.50), channel_id=1, source_target_pairs={{0,1},{1,2},{2,3},{3,0},{4,5},{5,6},{6,7},{7,4},{8,9},{9,10},{10,1... | collective-permute-start | bytes 442376 | tf_op jit(solution)/shard_map/ppermute | solution.py:356
  31.4 12.8 %collective-permute-start.4 = (f32[36,8,128]{2,1,0:T(8,128)S(1)}, f32[36,8,128]{2,1,0:T(8,128)S(1)}, u32[]{:S(2)}, u32[]{:S(2)}) collective-permute-start(f32[36,8,128]{2,1,0:T(8,128)S(1)} %bitcast.49), channel_id=1, source_target_pairs={{0,2},{1,3},{2,0},{3,1},{4,6},{5,7},{6,4},{7,5},{8,10},{9,11},{10,... | collective-permute-start | bytes 442376 | tf_op jit(solution)/shard_map/ppermute | solution.py:356
  33.1 11.1 %collective-permute-start.5 = (f32[36,8,128]{2,1,0:T(8,128)S(1)}, f32[36,8,128]{2,1,0:T(8,128)S(1)}, u32[]{:S(2)}, u32[]{:S(2)}) collective-permute-start(f32[36,8,128]{2,1,0:T(8,128)S(1)} %bitcast.48), channel_id=1, source_target_pairs={{0,3},{1,0},{2,1},{3,2},{4,7},{5,4},{6,5},{7,6},{8,11},{9,8},{10,9... | collective-permute-start | bytes 442376 | tf_op jit(solution)/shard_map/ppermute | solution.py:356
  48.9 12.6 %collective-permute-start.8 = (f32[2,288,128]{2,1,0:T(8,128)}, f32[2,288,128]{2,1,0:T(8,128)S(1)}, u32[]{:S(2)}, u32[]{:S(2)}) collective-permute-start(f32[2,288,128]{2,1,0:T(8,128)} %get-tuple-element.38), channel_id=1, source_target_pairs={{0,1},{1,2},{2,3},{3,7},{7,6},{6,5},{5,4},{4,8},{8,9},{9,10},{10,1... | collective-permute-start | bytes 884744 | tf_op jit(solution)/shard_map/ppermute | solution.py:398
  54.0 8.7 %collective-permute-start.9 = (f32[2,288,128]{2,1,0:T(8,128)S(1)}, f32[2,288,128]{2,1,0:T(8,128)S(1)}, u32[]{:S(2)}, u32[]{:S(2)}) collective-permute-start(f32[2,288,128]{2,1,0:T(8,128)S(1)} %get-tuple-element.39), channel_id=1, source_target_pairs={{1,0},{2,1},{3,2},{7,3},{6,7},{5,6},{4,5},{8,4},{9,8},{10,9},{11,1... | collective-permute-start | bytes 884744 | tf_op jit(solution)/shard_map/ppermute | solution.py:399
  55.4 40.7 %collective-permute-start.15 = (f32[36,8,128]{2,1,0:T(8,128)S(1)}, f32[36,8,128]{2,1,0:T(8,128)S(1)}, u32[]{:S(2)}, u32[]{:S(2)}) collective-permute-start(f32[36,8,128]{2,1,0:T(8,128)S(1)} %get-tuple-element.30.refs_5_), channel_id=1, source_target_pairs={{0,3},{1,0},{2,1},{3,2},{4,7},{5,4},{6,5},{7,6},{8,11},{9,8},{10,9... | collective-permute-start | bytes 442376 | tf_op jit(solution)/shard_map/ppermute | solution.py:356
  58.8 40.2 %collective-permute-start.16 = (f32[36,8,128]{2,1,0:T(8,128)S(1)}, f32[36,8,128]{2,1,0:T(8,128)S(1)}, u32[]{:S(2)}, u32[]{:S(2)}) collective-permute-start(f32[36,8,128]{2,1,0:T(8,128)S(1)} %get-tuple-element.31.refs_6_), channel_id=1, source_target_pairs={{0,2},{1,3},{2,0},{3,1},{4,6},{5,7},{6,4},{7,5},{8,10},{9,11},{10,... | collective-permute-start | bytes 442376 | tf_op jit(solution)/shard_map/ppermute | solution.py:356
  59.5 39.5 %collective-permute-start.17 = (f32[36,8,128]{2,1,0:T(8,128)S(1)}, f32[36,8,128]{2,1,0:T(8,128)S(1)}, u32[]{:S(2)}, u32[]{:S(2)}) collective-permute-start(f32[36,8,128]{2,1,0:T(8,128)S(1)} %get-tuple-element.32.refs_7_), channel_id=1, source_target_pairs={{0,1},{1,2},{2,3},{3,0},{4,5},{5,6},{6,7},{7,4},{8,9},{9,10},{10,1... | collective-permute-start | bytes 442376 | tf_op jit(solution)/shard_map/ppermute | solution.py:356
  71.0 31.8 %collective-permute-start.21 = (f32[36,8,128]{2,1,0:T(8,128)}, f32[36,8,128]{2,1,0:T(8,128)S(1)}, u32[]{:S(2)}, u32[]{:S(2)}) collective-permute-start(f32[36,8,128]{2,1,0:T(8,128)} %get-tuple-element.47.refs_9_), channel_id=1, source_target_pairs={{0,3},{1,0},{2,1},{3,2},{4,7},{5,4},{6,5},{7,6},{8,11},{9,8},{10,9... | collective-permute-start | bytes 442376 | tf_op jit(solution)/shard_map/ppermute | solution.py:356
  79.9 4.6 %collective-permute-start.10 = (f32[32,128]{1,0:T(8,128)S(1)}, f32[32,128]{1,0:T(8,128)S(1)}, u32[]{:S(2)}, u32[]{:S(2)}) collective-permute-start(f32[32,128]{1,0:T(8,128)S(1)} %shard_map.82), channel_id=1, source_target_pairs={{0,1},{1,0},{2,3},{3,2},{4,5},{5,4},{6,7},{7,6},{8,9},{9,8},{10,11... | collective-permute-start | bytes 49160 | tf_op jit(solution)/shard_map/ppermute | solution.py:318
  84.5 5.1 %collective-permute-start.11 = (f32[32,128]{1,0:T(8,128)S(1)}, f32[32,128]{1,0:T(8,128)S(1)}, u32[]{:S(2)}, u32[]{:S(2)}) collective-permute-start(f32[32,128]{1,0:T(8,128)S(1)} %add.185), channel_id=1, source_target_pairs={{0,2},{1,3},{2,0},{3,1},{4,6},{5,7},{6,4},{7,5},{8,10},{9,11},{10,... | collective-permute-start | bytes 49160 | tf_op jit(solution)/shard_map/ppermute | solution.py:318
  89.6 1.2 collective-permute-start.12
  90.8 3.7 %collective-permute-start.13 = (f32[32,128]{1,0:T(8,128)S(1)}, f32[32,128]{1,0:T(8,128)S(1)}, u32[]{:S(2)}, u32[]{:S(2)}) collective-permute-start(f32[32,128]{1,0:T(8,128)S(1)} %add.187), channel_id=1, source_target_pairs={{0,8},{1,9},{2,10},{3,11},{4,12},{5,13},{6,14},{7,15},{8,0},{9,1},... | collective-permute-start | bytes 49160 | tf_op jit(solution)/shard_map/ppermute | solution.py:318
  94.6 8.3 %collective-permute-start.14 = (f32[32,128]{1,0:T(8,128)S(1)}, f32[32,128]{1,0:T(8,128)S(1)}, u32[]{:S(2)}, u32[]{:S(2)}) collective-permute-start(f32[32,128]{1,0:T(8,128)S(1)} %add.188), channel_id=1, source_target_pairs={{0,16},{1,17},{2,18},{3,19},{4,20},{5,21},{6,22},{7,23},{8,24},{9,... | collective-permute-start | bytes 49160 | tf_op jit(solution)/shard_map/ppermute | solution.py:318
  96.1 13.6 %collective-permute-start.22 = (f32[36,8,128]{2,1,0:T(8,128)S(1)}, f32[36,8,128]{2,1,0:T(8,128)S(1)}, u32[]{:S(2)}, u32[]{:S(2)}) collective-permute-start(f32[36,8,128]{2,1,0:T(8,128)S(1)} %get-tuple-element.48.refs_10_), channel_id=1, source_target_pairs={{0,2},{1,3},{2,0},{3,1},{4,6},{5,7},{6,4},{7,5},{8,10},{9,11},{10,... | collective-permute-start | bytes 442376 | tf_op jit(solution)/shard_map/ppermute | solution.py:356
  99.0 10.7 %collective-permute-start.23 = (f32[36,8,128]{2,1,0:T(8,128)S(1)}, f32[36,8,128]{2,1,0:T(8,128)S(1)}, u32[]{:S(2)}, u32[]{:S(2)}) collective-permute-start(f32[36,8,128]{2,1,0:T(8,128)S(1)} %get-tuple-element.49.refs_11_), channel_id=1, source_target_pairs={{0,1},{1,2},{2,3},{3,0},{4,5},{5,6},{6,7},{7,4},{8,9},{9,10},{10,1... | collective-permute-start | bytes 442376 | tf_op jit(solution)/shard_map/ppermute | solution.py:356
  99.0 10.7 %collective-permute-start.18 = (f32[36,8,128]{2,1,0:T(8,128)S(1)}, f32[36,8,128]{2,1,0:T(8,128)S(1)}, u32[]{:S(2)}, u32[]{:S(2)}) collective-permute-start(f32[36,8,128]{2,1,0:T(8,128)S(1)} %get-tuple-element.42.refs_5_), channel_id=1, source_target_pairs={{0,3},{1,0},{2,1},{3,2},{4,7},{5,4},{6,5},{7,6},{8,11},{9,8},{10,9... | collective-permute-start | bytes 442376 | tf_op jit(solution)/shard_map/ppermute | solution.py:356
  102.9 17.9 %collective-permute-start.19 = (f32[36,8,128]{2,1,0:T(8,128)S(1)}, f32[36,8,128]{2,1,0:T(8,128)S(1)}, u32[]{:S(2)}, u32[]{:S(2)}) collective-permute-start(f32[36,8,128]{2,1,0:T(8,128)S(1)} %get-tuple-element.43.refs_6_), channel_id=1, source_target_pairs={{0,2},{1,3},{2,0},{3,1},{4,6},{5,7},{6,4},{7,5},{8,10},{9,11},{10,... | collective-permute-start | bytes 442376 | tf_op jit(solution)/shard_map/ppermute | solution.py:356
  102.9 17.9 %collective-permute-start.20 = (f32[36,8,128]{2,1,0:T(8,128)S(1)}, f32[36,8,128]{2,1,0:T(8,128)S(1)}, u32[]{:S(2)}, u32[]{:S(2)}) collective-permute-start(f32[36,8,128]{2,1,0:T(8,128)S(1)} %get-tuple-element.44.refs_7_), channel_id=1, source_target_pairs={{0,1},{1,2},{2,3},{3,0},{4,5},{5,6},{6,7},{7,4},{8,9},{9,10},{10,1... | collective-permute-start | bytes 442376 | tf_op jit(solution)/shard_map/ppermute | solution.py:356
  (12 other events, 119.8 us)

commit v3 on v2

--- a/solution.py
+++ b/solution.py
@@ -12,7 +12,7 @@
 DEGREE = 3
 SUB = 8
 LANES = 128
-PARAMS = pltpu.CompilerParams(vmem_limit_bytes=24 * 1024 * 1024)
+PARAMS = pltpu.CompilerParams(vmem_limit_bytes=12 * 1024 * 1024)
 
 
 def term_list(modes):
@@ -37,17 +37,34 @@
     return edges
 
 
-def rank_of(multi_index):
-    modes = multi_index.shape[1]
-    from_top = jnp.asarray(np.tril(np.ones((modes, modes), np.int32)))
-    above = jnp.sum(jnp.maximum(multi_index, 0)[:, :, None] * from_top[None], axis=1)
-    a, b, c = (jnp.sum((above >= n).astype(jnp.int32), axis=1) for n in (1, 2, 3))
+def rank_row(multi_index):
+    here, modes = multi_index.shape
+    above = jnp.zeros((here, 1), jnp.int32)
+    symbols = [jnp.zeros((here, 1), jnp.int32)] * DEGREE
+    for k in reversed(range(modes)):
+        above += jnp.maximum(multi_index[:, k : k + 1], 0)
+        symbols = [a + jnp.where(above > n, 1, 0) for n, a in enumerate(symbols)]
+    a, b, c = symbols
     rank = a * (a + 1) * (a + 2) // 6 + b * (b + 1) // 2 + c
-    return jnp.where(multi_index[:, 0] < 0, math.comb(modes + DEGREE, DEGREE), rank)
-
-
-def columns_at(value, start, width):
-    return lax.dynamic_slice_in_dim(value, start, width, axis=1)
+    rank = jnp.where(multi_index[:, 0:1] < 0, math.comb(modes + DEGREE, DEGREE), rank).astype(jnp.float32)
+    lane = lax.broadcasted_iota(jnp.int32, (here, LANES), 1)
+    slot = lax.broadcasted_iota(jnp.int32, (here, LANES), 0)
+    return jnp.sum(jnp.where(lane == slot, rank, 0.0), axis=0, keepdims=True)
+
+
+def cut_kernel(n, columns, rows, offsets_ref, source_ref, *refs):
+    per = SUB // columns
+    index, parts = refs[:-n], refs[-n:]
+    for d, out in enumerate(parts):
+        at = pl.ds(pl.multiple_of(offsets_ref[d], columns), columns)
+        for g in range(per):
+            for q in range(rows):
+                out[q, g * columns : (g + 1) * columns] = source_ref[q * per + g, at]
+    if index:
+        first = lax.broadcasted_iota(jnp.int32, (SUB, LANES), 0) == 0
+        tag = jnp.where(first, rank_row(index[0][...]), 0.0)
+        for out in parts:
+            out[rows] = tag
 
 
 def lane_next(u):
@@ -97,9 +114,8 @@
         store(s, pltpu.roll(across, 1, 0) - across + along)
 
 
-def pack_rows(ranks_ref, packed_refs, field_ref, columns):
+def pack_rows(ranks_ref, packed_refs, field_ref, columns, rows, first=0):
     per = SUB // columns
-    rows = packed_refs[0].shape[0]
     sub = lax.broadcasted_iota(jnp.int32, (SUB, LANES), 0)
     for d, out in enumerate(packed_refs):
 
@@ -108,7 +124,7 @@
             for g in range(1, per):
                 other = field_ref[ranks_ref[(d * rows + q) * per + g]]
                 row = jnp.where(sub < g * columns, row, pltpu.roll(other, g * columns, 0))
-            out[q] = row
+            out[first + q] = row
             return carry
 
         lax.fori_loop(0, rows, one, 0, unroll=4)
@@ -125,7 +141,7 @@
     return flat_ref[pl.ds(j, rows, stride=SUB), :]
 
 
-def enter_kernel(n, columns, rows, ranks_ref, coef_ref, *refs):
+def enter_kernel(n, columns, rows, ranks_ref, coef_ref, _, *refs):
     parts, (field_ref, first_ref, last_ref) = refs[:n], refs[n:]
     slots = field_ref.shape[0]
     fields = coef_ref.shape[0]
@@ -168,22 +184,19 @@
         y_ref[s] = value
 
     apply_operator(u_ref, coef_ref, edges, store, diff_ref)
-    pack_rows(ranks_ref, packed, y_ref, columns)
+    pack_rows(ranks_ref, packed, y_ref, columns, packed[0].shape[0])
 
 
 def residual_kernel(n, columns, ranks_ref, *refs):
     forcing, image = refs[:n], refs[n : 2 * n]
-    packed = refs[2 * n : 3 * n]
-    field_ref, first_ref, last_ref = refs[3 * n :]
+    field_ref, first_ref, last_ref = refs[2 * n :]
     rows = forcing[0].shape[0]
     slots = field_ref.shape[0]
     field_ref[...] = jnp.zeros_like(field_ref)
     for d in range(n):
 
         def one(q, carry, d=d):
-            v = forcing[d][q] - image[d][q]
-            packed[d][q] = v
-            scatter_row(ranks_ref, d * rows + q, v, field_ref, columns)
+            scatter_row(ranks_ref, d * rows + q, forcing[d][q] - image[d][q], field_ref, columns)
             return carry
 
         lax.fori_loop(0, rows, one, 0, unroll=4)
@@ -193,66 +206,61 @@
         last_ref[j] = take_column(flat, columns - 2 + j, slots)
 
 
-def first_kernel(n, columns, edges, ranks_ref, v_ref, before_ref, after_ref, coef_ref, inside_ref, *refs):
-    packed, (out_ref, u_ref, diff_ref) = refs[:n], refs[n:]
-    slots = v_ref.shape[0]
-    u_ref[...] = v_ref[...]
-    flat = u_ref.reshape(slots * SUB, LANES)
+def krylov_kernel(
+    n, columns, edges, ranks_ref, place_ref, v_ref, before_ref, after_ref, coef_ref, inside_ref, *refs
+):
+    packed, (table_ref, v0_ref, v1_ref, v2_ref, diff_ref) = refs[:n], refs[n:]
+    rows = packed[0].shape[0] // 2
+    slots, terms = v_ref.shape[0], len(edges)
+    v0_ref[...] = v_ref[...]
+    flat = v0_ref.reshape(slots * SUB, LANES)
     for j in range(2):
         flat[pl.ds(SUB - 2 + j, slots, stride=SUB), :] = before_ref[j]
         flat[pl.ds(columns + j, slots, stride=SUB), :] = after_ref[j]
-    out_ref[len(edges) :] = jnp.zeros((slots - len(edges), SUB, LANES), jnp.float32)
     inside = inside_ref[...] > 0.0
 
-    def store(s, value):
-        out_ref[s] = jnp.where(inside, value, 0.0)
-
-    apply_operator(u_ref, coef_ref, edges, store, diff_ref)
-    pack_rows(ranks_ref, packed, out_ref, columns)
-
-
-def second_kernel(n, columns, edges, ranks_ref, v_ref, coef_ref, *refs):
-    packed, (y_ref, diff_ref) = refs[:n], refs[n:]
-    slots = v_ref.shape[0]
-    y_ref[len(edges) :] = jnp.zeros((slots - len(edges), SUB, LANES), jnp.float32)
-
-    def store(s, value):
-        y_ref[s] = value
-
-    apply_operator(v_ref, coef_ref, edges, store, diff_ref)
-    pack_rows(ranks_ref, packed, y_ref, columns)
-
-
-def row_sums(n, rows, of_row, count):
-    totals = (jnp.zeros((SUB, LANES), jnp.float32),) * count
-    for d in range(n):
-
-        def one(q, totals, d=d):
-            return tuple(t + x for t, x in zip(totals, of_row(d, q)))
-
-        totals = lax.fori_loop(0, rows, one, totals, unroll=4)
+    def store_first(s, value):
+        v1_ref[s] = jnp.where(inside, value, 0.0)
+
+    def store_second(s, value):
+        v2_ref[s] = value
+
+    for source, target, store in ((v0_ref, v1_ref, store_first), (v1_ref, v2_ref, store_second)):
+        target[terms:] = jnp.zeros((slots - terms, SUB, LANES), jnp.float32)
+        apply_operator(source, coef_ref, edges, store, diff_ref)
+    pack_rows(ranks_ref, packed, v1_ref, columns, rows)
+    pack_rows(ranks_ref, packed, v2_ref, columns, rows, rows)
+    dot_products(place_ref, columns, v0_ref, v1_ref, v2_ref, table_ref)
+
+
+def own_sums(count, terms, columns, of_term):
+    def one(s, totals):
+        return tuple(t + x for t, x in zip(totals, of_term(s)))
+
+    totals = lax.fori_loop(0, terms, one, (jnp.zeros((SUB, LANES), jnp.float32),) * count, unroll=11)
+    own = lax.broadcasted_iota(jnp.int32, (SUB, LANES), 0) < columns
+    totals = [jnp.where(own, t, 0.0) for t in totals]
     return [jnp.sum(jnp.sum(t, axis=0, keepdims=True), axis=1, keepdims=True) for t in totals]
 
 
-def dots_kernel(n, place_ref, *refs):
-    v0, v1, v2, out_ref = refs[:n], refs[n : 2 * n], refs[2 * n : 3 * n], refs[3 * n]
-    rows = v0[0].shape[0]
-    aa, ab = row_sums(n, rows, lambda d, q: (v0[d][q] * v0[d][q], v0[d][q] * v1[d][q]), 2)
+def dot_products(place_ref, columns, v0_ref, v1_ref, v2_ref, table_ref):
+    slots = v0_ref.shape[0]
+    aa, ab = own_sums(2, slots, columns, lambda s: (v0_ref[s] * v0_ref[s], v0_ref[s] * v1_ref[s]))
     m = jnp.where(aa > 0.0, ab / jnp.where(aa > 0.0, aa, 1.0), 0.0)
 
-    def products(d, q):
-        a, b, c = v0[d][q], v1[d][q], v2[d][q]
+    def products(s):
+        a, b, c = v0_ref[s], v1_ref[s], v2_ref[s]
         w = b - m * a
         e = c - m * b
         return a * w, w * w, a * e, w * b, w * e
 
-    entries = [aa, ab, m] + row_sums(n, rows, products, 5)
-    lane = lax.broadcasted_iota(jnp.int32, out_ref.shape, 1)
-    row = lax.broadcasted_iota(jnp.int32, out_ref.shape, 0)
-    table = jnp.zeros(out_ref.shape, jnp.float32)
+    entries = [aa, ab, m] + own_sums(5, slots, columns, products)
+    lane = lax.broadcasted_iota(jnp.int32, table_ref.shape, 1)
+    row = lax.broadcasted_iota(jnp.int32, table_ref.shape, 0)
+    table = jnp.zeros(table_ref.shape, jnp.float32)
     for k, value in enumerate(entries):
         table = jnp.where(lane == k, value, table)
-    out_ref[...] = jnp.where(row == place_ref[0], table, 0.0)
+    table_ref[...] = jnp.where(row == place_ref[0], table, 0.0)
 
 
 def step_lengths(table):
@@ -274,18 +282,18 @@
     return step, beta, rr / (r_ar + beta * mixed + beta * beta * curve)
 
 
-def finish_kernel(n, columns, offsets_ref, table_ref, x_ref, f_ref, *refs):
-    image, v1, v2 = refs[:n], refs[n : 2 * n], refs[2 * n : 3 * n]
+def finish_kernel(n, columns, offsets_ref, x_ref, f_ref, *refs):
+    tables, image, krylov = refs[:n], refs[n : 2 * n], refs[2 * n : 3 * n]
     approx_ref, residual_ref = refs[3 * n :]
     per = SUB // columns
     rows = image[0].shape[0]
-    step, beta, last = step_lengths(table_ref[...])
+    step, beta, last = step_lengths(functools.reduce(jnp.add, [t[...] for t in tables]))
     whole = step + last * beta
     for d in range(n):
         at = pl.ds(pl.multiple_of(offsets_ref[d], columns), columns)
 
         def one(q, carry, d=d, at=at):
-            y, b, c = image[d][q], v1[d][q], v2[d][q]
+            y, b, c = image[d][q], krylov[d][q], krylov[d][rows + q]
             for g in range(per):
                 part = slice(g * columns, (g + 1) * columns)
                 s = q * per + g
@@ -299,11 +307,20 @@
         lax.fori_loop(0, rows, one, 0, unroll=2)
 
 
+class Anywhere:
+    def __init__(self, value):
+        self.value = value
+
+
 def call(kernel, scalars, arrays, outs, scratch=()):
     whole = pl.BlockSpec(memory_space=pltpu.VMEM)
+    specs = [
+        pl.BlockSpec(memory_space=pl.ANY) if isinstance(a, Anywhere) else whole for a in arrays
+    ]
+    arrays = [a.value if isinstance(a, Anywhere) else a for a in arrays]
     return pl.pallas_call(
         kernel,
-        in_specs=[pl.BlockSpec(memory_space=pltpu.SMEM)] * len(scalars) + [whole] * len(arrays),
+        in_specs=[pl.BlockSpec(memory_space=pltpu.SMEM)] * len(scalars) + specs,
         out_specs=[whole] * len(outs),
         out_shape=[jax.ShapeDtypeStruct(s, jnp.float32) for s in outs],
         scratch_shapes=[pltpu.VMEM(s, jnp.float32) for s in scratch],
@@ -311,11 +328,11 @@
     )(*scalars, *arrays)
 
 
-def butterfly(value, sizes):
-    count = math.prod(sizes)
+def butterfly(value, axis):
+    count = lax.axis_size(axis)
     bit = 1
     while bit < count:
-        value = value + lax.ppermute(value, ("space", "chaos"), [(i, i ^ bit) for i in range(count)])
+        value = value + lax.ppermute(value, axis, [(i, i ^ bit) for i in range(count)])
         bit *= 2
     return value
 
@@ -349,20 +366,29 @@
 
     offsets = [columns * chunk(i, (z + d) % n) for d in range(n)]
 
-    def cut(value, d):
-        return columns_at(value, offsets[d], columns).reshape(rows, SUB, lanes)
-
-    def sent(parts, way):
-        return parts[:1] + [lax.ppermute(parts[d], "chaos", way(d)) for d in range(1, n)]
-
-    rank = rank_of(multi_index)
-    tag = jnp.pad(rank.astype(jnp.float32)[None, None], ((0, 0), (0, SUB - 1), (0, lanes - here)))
-    x_parts = sent([jnp.concatenate([cut(start_guess, d), tag], axis=0) for d in range(n)], outward)
+    def sent(parts, way, after=None):
+        out = [parts[0]]
+        for d in range(1, n):
+            value = parts[d]
+            if after is not None and after[d] is not None:
+                value = lax.optimization_barrier((value, after[d]))[0]
+            out.append(lax.ppermute(value, "chaos", way(d)))
+        return out
+
+    field, part, fields = (slots, SUB, lanes), (rows, SUB, lanes), (modes + 1, SUB, lanes)
+    diff = (3,) + field
+    edge = (-(-(slots + 2 * (modes + 1)) // SUB) * SUB, lanes)
+    offsets_array = jnp.stack(offsets).astype(jnp.int32)
+
+    cut = functools.partial(cut_kernel, n, columns, rows)
+    x_parts = call(cut, [offsets_array], [start_guess, multi_index], [(rows + 1, SUB, lanes)] * n)
+    x_parts = sent(list(x_parts), outward)
     ranks = jnp.concatenate([p[rows, 0, :here] for p in x_parts]).astype(jnp.int32)
-    f_parts = sent([cut(forcing, d) for d in range(n)], outward)
+    f_parts = sent(list(call(cut, [offsets_array], [forcing], [part] * n)), outward)
 
     stacked = jnp.concatenate([mean_field[None], mode_fields], axis=0)
-    own_coef = jnp.pad(columns_at(stacked, offsets[0], columns), ((0, 0), (0, SUB - columns), (0, 0)))
+    own_coef = lax.dynamic_slice_in_dim(stacked, offsets[0], columns, axis=1)
+    own_coef = jnp.pad(own_coef, ((0, 0), (0, SUB - columns), (0, 0)))
     sub = lax.broadcasted_iota(jnp.int32, (SUB, lanes), 0)
     position = i * n + chunk(i, z)
     outside = ((position == 0) & (sub >= SUB - 2)) | (
@@ -370,14 +396,10 @@
     )
     inside = jnp.where(outside, 0.0, 1.0)
 
-    field, part, fields = (slots, SUB, lanes), (rows, SUB, lanes), (modes + 1, SUB, lanes)
-    diff = (3,) + field
-    edge = (-(-(slots + 2 * (modes + 1)) // SUB) * SUB, lanes)
-
     x, x_first, x_last = call(
         functools.partial(enter_kernel, n, columns, rows),
         [ranks],
-        [own_coef] + x_parts,
+        [own_coef, Anywhere(f_parts[1])] + x_parts,
         [field, edge, edge],
     )
     x_before = lax.ppermute(x_last, both, line)
@@ -389,42 +411,30 @@
         [part] * n + [fields],
         [field, field, diff],
     )
-    *v0_parts, v0, v0_first, v0_last = call(
+    v0, v0_first, v0_last = call(
         functools.partial(residual_kernel, n, columns),
         [ranks],
         f_parts + image,
-        [part] * n + [field, (2, slots, lanes), (2, slots, lanes)],
+        [field, (2, slots, lanes), (2, slots, lanes)],
     )
     v0_before = lax.ppermute(v0_last, both, line)
     v0_after = lax.ppermute(v0_first, both, back_line)
     image_home = sent(image, homeward)
-    *v1_parts, v1 = call(
-        functools.partial(first_kernel, n, columns, edges),
-        [ranks],
+    *krylov, table = call(
+        functools.partial(krylov_kernel, n, columns, edges),
+        [ranks, (i * n + z).astype(jnp.int32)[None]],
         [v0, v0_before, v0_after, coef, inside],
-        [part] * n + [field],
-        [field, diff],
-    )
-    v1_home = sent(v1_parts, homeward)
-    v2_parts = call(
-        functools.partial(second_kernel, n, columns, edges),
-        [ranks],
-        [v1, coef],
-        [part] * n,
-        [field, diff],
-    )
-    v2_home = sent(list(v2_parts), homeward)
-    (table,) = call(
-        functools.partial(dots_kernel, n),
-        [(i * n + z).astype(jnp.int32)[None]],
-        v0_parts + v1_parts + list(v2_parts),
-        [(-(-spaces * n // SUB) * SUB, lanes)],
-    )
-    table = butterfly(table, (spaces, n))
+        [(2 * rows, SUB, lanes)] * n + [(-(-spaces * n // SUB) * SUB, lanes)],
+        [field, field, field, diff],
+    )
+    krylov, image_home = lax.optimization_barrier((krylov, image_home))
+    krylov_home = sent(krylov, homeward)
+    table = butterfly(table, "space")
+    tables = sent([table] * n, homeward, [None, krylov_home[n - 1]] + [None] * (n - 2))
     return call(
         functools.partial(finish_kernel, n, columns),
-        [jnp.stack(offsets).astype(jnp.int32)],
-        [table, start_guess, forcing] + image_home + v1_home + v2_home,
+        [offsets_array],
+        [start_guess, forcing] + tables + image_home + krylov_home,
         [forcing.shape] * 2,
     )
 

time: 124 us -> 103 us (0.83)
  starting transfers between devices: 50.2 us -> 42.6 us
  waiting for transfers between devices: 41.1 us -> 34.1 us
  local copies, waits for them, and re-layouts: 8.23 us -> 3.81 us
  other arithmetic: 3.16 us -> 0.19 us
    ppermute x20 -> x18, starting transfers between devices: 36.8 us -> 29.8 us  [the longest x15 26.6 us: sent(): out.append(lax.ppermute(value, 'chaos', way(d)))]
    ppermute x20 -> x18, waiting for transfers between devices: 32.9 us -> 26.4 us  [the longest x15 20.9 us: sent(): out.append(lax.ppermute(value, 'chaos', way(d)))]
    unnamed x24 -> x17, local copies, waits for them, and re-layouts: 6.29 us -> 3.72 us
    dynamic_slice x1 -> x0, local copies, waits for them, and re-layouts: 1.86 us -> none  [columns_at(): return lax.dynamic_slice_in_dim(value, start, width, axis=1)]
    ppermute x1, waiting for transfers between devices: 5.07 us -> 3.28 us  [per_device(): x_after = lax.ppermute(x_first, both, back_line)]
    convert_element_type x2 -> x0, other arithmetic: 1.42 us -> none  [per_device(): rank.astype(jnp.float32)[None, None]]
    ppermute x1, waiting for transfers between devices: 1.25 us -> 2.51 us  [per_device(): v0_after = lax.ppermute(v0_first, both, back_line)]
  transfers between devices with their start and end apart: 24 -> 22, of which waited for: 12 -> 13; matrix products, arithmetic and copies ran while one was open for 1% -> 0% of each run, Pallas kernels for 11% -> 13%
where the time goes in v3:
time: 103 us; the launch traced here: 102 us
  starting transfers between devices  42.6 us (41%)
  waiting for transfers between devices  34.1 us (33%)
  Pallas kernels  20.5 us (20%)
  local copies, waits for them, and re-layouts  3.81 us (4%)
    ppermute x15, starting transfers between devices, sent(): out.append(lax.ppermute(value, 'chaos', way(d)))  26.6 us
    ppermute x15, waiting for transfers between devices, sent(): out.append(lax.ppermute(value, 'chaos', way(d)))  20.9 us
    pallas_call x7, Pallas kernels, call(): pl.pallas_call(kernel, in_specs=[pl.BlockSpec(memory_space=pltpu.SMEM)] *...  20.5 us
    ppermute x1, starting transfers between devices, per_device(): x_before = lax.ppermute(x_last, both, line)  5.67 us
    ppermute x3, waiting for transfers between devices, butterfly(): lax.ppermute(value, axis, [(i, i ^ bit) for i in range(count)])  5.48 us
    ppermute x1, starting transfers between devices, per_device(): v0_before = lax.ppermute(v0_last, both, line)  4.51 us
    unnamed x17, local copies, waits for them, and re-layouts  3.72 us
    ppermute x1, waiting for transfers between devices, per_device(): x_after = lax.ppermute(x_first, both, back_line)  3.28 us
  transfers between devices with their start and end apart: 22, of which 13 were waited for; matrix products, arithmetic and copies ran while one was open for 0% of the time, Pallas kernels for 13%

profile of v3, /device:TPU:0, one launch (start us, length us, event | category | flops | bytes accessed | tf_op | source)
XLA Modules:
  0.0 102.0 jit_solution(976700781290484330)
XLA Ops:
  3.6 3.1 %collective-permute-start = (f32[37,8,128]{2,1,0:T(8,128)S(1)}, f32[37,8,128]{2,1,0:T(8,128)S(1)}, u32[]{:S(2)}, u32[]{:S(2)}) collective-permute-start(f32[37,8,128]{2,1,0:T(8,128)S(1)} %get-tuple-element.36), channel_id=1, source_target_pairs={{0,1},{1,2},{2,3},{3,0},{4,5},{5,6},{6,7},{7,4},{8,9},{9,10},{10,1... | collective-permute-start | bytes 454664 | tf_op jit(solution)/shard_map/ppermute | solution.py:375
  6.6 2.6 %collective-permute-start.1 = (f32[37,8,128]{2,1,0:T(8,128)S(1)}, f32[37,8,128]{2,1,0:T(8,128)S(1)}, u32[]{:S(2)}, u32[]{:S(2)}) collective-permute-start(f32[37,8,128]{2,1,0:T(8,128)S(1)} %get-tuple-element.37), channel_id=1, source_target_pairs={{0,2},{1,3},{2,0},{3,1},{4,6},{5,7},{6,4},{7,5},{8,10},{9,11},{10,... | collective-permute-start | bytes 454664 | tf_op jit(solution)/shard_map/ppermute | solution.py:375
  13.5 6.5 %collective-permute-done.1.refs_2_ = f32[37,8,128]{2,1,0:T(8,128)S(1)} collective-permute-done((f32[37,8,128]{2,1,0:T(8,128)S(1)}, f32[37,8,128]{2,1,0:T(8,128)S(1)}, u32[]{:S(2)}, u32[]{:S(2)}) %collective-permute-start.1) | collective-permute-done | bytes 151584 | tf_op jit(solution)/shard_map/ppermute | solution.py:375
  20.1 2.3 %collective-permute-done.3._.refs_1_ = f32[36,8,128]{2,1,0:T(8,128)S(1)} collective-permute-done((f32[36,8,128]{2,1,0:T(8,128)S(1)}, f32[36,8,128]{2,1,0:T(8,128)S(1)}, u32[]{:S(2)}, u32[]{:S(2)}) %collective-permute-start.3) | collective-permute-done | bytes 147488 | tf_op jit(solution)/shard_map/ppermute | solution.py:375
  23.6 5.7 %collective-permute-start.6 = (f32[312,128]{1,0:T(8,128)S(1)}, f32[312,128]{1,0:T(8,128)S(1)}, u32[]{:S(2)}, u32[]{:S(2)}) collective-permute-start(f32[312,128]{1,0:T(8,128)S(1)} %get-tuple-element.44), channel_id=1, source_target_pairs={{0,1},{1,2},{2,3},{3,7},{7,6},{6,5},{5,4},{4,8},{8,9},{9,10},{10,1... | collective-permute-start | bytes 479240 | tf_op jit(solution)/shard_map/ppermute | solution.py:405
  30.6 2.8 %collective-permute-start.4 = (f32[36,8,128]{2,1,0:T(8,128)S(1)}, f32[36,8,128]{2,1,0:T(8,128)S(1)}, u32[]{:S(2)}, u32[]{:S(2)}) collective-permute-start(f32[36,8,128]{2,1,0:T(8,128)S(1)} %get-tuple-element.41), channel_id=1, source_target_pairs={{0,2},{1,3},{2,0},{3,1},{4,6},{5,7},{6,4},{7,5},{8,10},{9,11},{10,... | collective-permute-start | bytes 442376 | tf_op jit(solution)/shard_map/ppermute | solution.py:375
  33.4 2.2 %collective-permute-start.5 = (f32[36,8,128]{2,1,0:T(8,128)S(1)}, f32[36,8,128]{2,1,0:T(8,128)S(1)}, u32[]{:S(2)}, u32[]{:S(2)}) collective-permute-start(f32[36,8,128]{2,1,0:T(8,128)S(1)} %get-tuple-element.42), channel_id=1, source_target_pairs={{0,3},{1,0},{2,1},{3,2},{4,7},{5,4},{6,5},{7,6},{8,11},{9,8},{10,9... | collective-permute-start | bytes 442376 | tf_op jit(solution)/shard_map/ppermute | solution.py:375
  35.7 3.3 %collective-permute-done.7.after_ref = f32[312,128]{1,0:T(8,128)S(1)} collective-permute-done((f32[312,128]{1,0:T(8,128)S(1)}, f32[312,128]{1,0:T(8,128)S(1)}, u32[]{:S(2)}, u32[]{:S(2)}) %collective-permute-start.7) | collective-permute-done | bytes 159776 | tf_op jit(solution)/shard_map/ppermute | solution.py:406
  38.9 4.7 %shard_map.71 = (f32[36,8,128]{2,1,0:T(8,128)S(1)}, f32[36,8,128]{2,1,0:T(8,128)}, f32[36,8,128]{2,1,0:T(8,128)}, f32[36,8,128]{2,1,0:T(8,128)}, f32[11,8,128]{2,1,0:T(8,128)S(1)}) custom-call(s32[288]{0:T(512)S(1)} %maximum_convert_fusion.ranks_ref, f32[288,8,128]{2,1,0:T(8,128)S(1)} %get-tuple-element.43.x_ref, ...), custom_call_target="tpu_custom_call" | custom-call | tf_op jit(solution)/shard_map/pallas_call | solution.py:321
  44.1 2.6 %shard_map.72 = (f32[288,8,128]{2,1,0:T(8,128)S(1)}, f32[2,288,128]{2,1,0:T(8,128)}, f32[2,288,128]{2,1,0:T(8,128)}) custom-call(s32[288]{0:T(512)S(1)} %maximum_convert_fusion.ranks_ref, f32[36,8,128]{2,1,0:T(8,128)S(1)} %get-tuple-element.39.refs_0_, f32[36,8,128]{2,1,0:T(8,128)S(1)} %collective-permute-done.3._.refs_1_, ...), custom_call_target="tpu_custom_call" | custom-call | tf_op jit(solution)/shard_map/pallas_call | solution.py:321
  46.7 4.5 %collective-permute-start.8 = (f32[2,288,128]{2,1,0:T(8,128)}, f32[2,288,128]{2,1,0:T(8,128)S(1)}, u32[]{:S(2)}, u32[]{:S(2)}) collective-permute-start(f32[2,288,128]{2,1,0:T(8,128)} %get-tuple-element.51), channel_id=1, source_target_pairs={{0,1},{1,2},{2,3},{3,7},{7,6},{6,5},{5,4},{4,8},{8,9},{9,10},{10,1... | collective-permute-start | bytes 884744 | tf_op jit(solution)/shard_map/ppermute | solution.py:420
  52.5 2.9 %collective-permute-start.13 = (f32[36,8,128]{2,1,0:T(8,128)}, f32[36,8,128]{2,1,0:T(8,128)S(1)}, u32[]{:S(2)}, u32[]{:S(2)}) collective-permute-start(f32[36,8,128]{2,1,0:T(8,128)} %get-tuple-element.47.refs_5_), channel_id=1, source_target_pairs={{0,3},{1,0},{2,1},{3,2},{4,7},{5,4},{6,5},{7,6},{8,11},{9,8},{10,9... | collective-permute-start | bytes 442376 | tf_op jit(solution)/shard_map/ppermute | solution.py:375
  56.7 1.9 %collective-permute-done.8.before_ref = f32[2,288,128]{2,1,0:T(8,128)S(1)} collective-permute-done((f32[2,288,128]{2,1,0:T(8,128)}, f32[2,288,128]{2,1,0:T(8,128)S(1)}, u32[]{:S(2)}, u32[]{:S(2)}) %collective-permute-start.8) | collective-permute-done | bytes 294944 | tf_op jit(solution)/shard_map/ppermute | solution.py:420
  58.6 2.5 %collective-permute-done.9.after_ref = f32[2,288,128]{2,1,0:T(8,128)S(1)} collective-permute-done((f32[2,288,128]{2,1,0:T(8,128)}, f32[2,288,128]{2,1,0:T(8,128)S(1)}, u32[]{:S(2)}, u32[]{:S(2)}) %collective-permute-start.9) | collective-permute-done | bytes 294944 | tf_op jit(solution)/shard_map/ppermute | solution.py:421
  62.0 8.1 %shard_map.73 = (f32[72,8,128]{2,1,0:T(8,128)S(1)}, f32[72,8,128]{2,1,0:T(8,128)S(1)}, f32[72,8,128]{2,1,0:T(8,128)S(1)}, f32[72,8,128]{2,1,0:T(8,128)S(1)}, f32[32,128]{1,0:T(8,128)S(1)}) custom-call(s32[288]{0:T(512)S(1)} %maximum_convert_fusion.ranks_ref, s32[1]{0:T(128)} %bitcast.8.place_ref, f32[288,8,128]{2,1,0:T(8,128)S(1)} %get-tuple-element.50.v_ref, ...), custom_call_target="tpu_custom_call" | custom-call | tf_op jit(solution)/shard_map/pallas_call | solution.py:321
  70.7 3.1 %collective-permute-start.16 = (f32[72,8,128]{2,1,0:T(8,128)S(1)}, f32[72,8,128]{2,1,0:T(8,128)S(1)}, u32[]{:S(2)}, u32[]{:S(2)}) collective-permute-start(f32[72,8,128]{2,1,0:T(8,128)S(1)} %get-tuple-element.59), channel_id=1, source_target_pairs={{0,1},{1,2},{2,3},{3,0},{4,5},{5,6},{6,7},{7,4},{8,9},{9,10},{10,1... | collective-permute-start | bytes 884744 | tf_op jit(solution)/shard_map/ppermute | solution.py:375
  78.1 2.2 %collective-permute-done.11 = f32[32,128]{1,0:T(8,128)S(1)} collective-permute-done((f32[32,128]{1,0:T(8,128)S(1)}, f32[32,128]{1,0:T(8,128)S(1)}, u32[]{:S(2)}, u32[]{:S(2)}) %collective-permute-start.11) | collective-permute-done | bytes 16416 | tf_op jit(solution)/shard_map/ppermute | solution.py:335
  80.3 1.7 %collective-permute-start.12 = (f32[32,128]{1,0:T(8,128)S(1)}, f32[32,128]{1,0:T(8,128)S(1)}, u32[]{:S(2)}, u32[]{:S(2)}) collective-permute-start(f32[32,128]{1,0:T(8,128)S(1)} %add.61), channel_id=1, source_target_pairs={{0,16},{4,20},{8,24},{12,28},{16,0},{20,4},{24,8},{28,12},{1,17},{... | collective-permute-start | bytes 49160 | tf_op jit(solution)/shard_map/ppermute | solution.py:335
  82.0 2.0 %collective-permute-done.12 = f32[32,128]{1,0:T(8,128)S(1)} collective-permute-done((f32[32,128]{1,0:T(8,128)S(1)}, f32[32,128]{1,0:T(8,128)S(1)}, u32[]{:S(2)}, u32[]{:S(2)}) %collective-permute-start.12) | collective-permute-done | bytes 16416 | tf_op jit(solution)/shard_map/ppermute | solution.py:335
  84.6 2.9 %collective-permute-start.18 = (f32[32,128]{1,0:T(8,128)S(1)}, f32[32,128]{1,0:T(8,128)S(1)}, u32[]{:S(2)}, u32[]{:S(2)}) collective-permute-start(f32[32,128]{1,0:T(8,128)S(1)} %add.62.refs_0_), channel_id=1, source_target_pairs={{0,2},{1,3},{2,0},{3,1},{4,6},{5,7},{6,4},{7,5},{8,10},{9,11},{10,... | collective-permute-start | bytes 49160 | tf_op jit(solution)/shard_map/ppermute | solution.py:375
  87.5 1.6 %collective-permute-start.17 = (f32[32,128]{1,0:T(8,128)S(1)}, f32[32,128]{1,0:T(8,128)S(1)}, u32[]{:S(2)}, u32[]{:S(2)}) collective-permute-start(f32[32,128]{1,0:T(8,128)S(1)} %add.62.refs_0_), channel_id=1, source_target_pairs={{0,3},{1,0},{2,1},{3,2},{4,7},{5,4},{6,5},{7,6},{8,11},{9,8},{10,9... | collective-permute-start | bytes 49160 | tf_op jit(solution)/shard_map/ppermute | solution.py:375
  89.1 3.6 %collective-permute-done.19.refs_3_ = f32[32,128]{1,0:T(8,128)S(1)} collective-permute-done((f32[32,128]{1,0:T(8,128)S(1)}, f32[32,128]{1,0:T(8,128)S(1)}, u32[]{:S(2)}, u32[]{:S(2)}) %collective-permute-start.19) | collective-permute-done | bytes 16416 | tf_op jit(solution)/shard_map/ppermute | solution.py:375
  92.7 6.9 %collective-permute-done.18.refs_2_ = f32[32,128]{1,0:T(8,128)S(1)} collective-permute-done((f32[32,128]{1,0:T(8,128)S(1)}, f32[32,128]{1,0:T(8,128)S(1)}, u32[]{:S(2)}, u32[]{:S(2)}) %collective-permute-start.18) | collective-permute-done | bytes 16416 | tf_op jit(solution)/shard_map/ppermute | solution.py:375
  99.6 2.4 %shard_map.74 = (f32[72,16,128]{2,1,0:T(8,128)}, f32[72,16,128]{2,1,0:T(8,128)}) custom-call(s32[4]{0:T(128)S(1)} %pad_add_fusion.offsets_ref, f32[72,16,128]{2,1,0:T(8,128)S(1)} %copy-done.1, f32[72,16,128]{2,1,0:T(8,128)S(1)} %copy-done.3, f32[32,128]{1,0:T(8,128)S(1)} %add.62.refs_0_, f32[32,128]{1,0:T(8,128)S(1)} %collective-permute-done.17.refs_1_, ...), custom_call_target="tpu_custom_call" | custom-call | tf_op jit(solution)/shard_map/pallas_call | solution.py:321
  (57 shorter events, 19.0 us)
Async XLA Ops:
  3.6 10.0 %collective-permute-start = (f32[37,8,128]{2,1,0:T(8,128)S(1)}, f32[37,8,128]{2,1,0:T(8,128)S(1)}, u32[]{:S(2)}, u32[]{:S(2)}) collective-permute-start(f32[37,8,128]{2,1,0:T(8,128)S(1)} %get-tuple-element.36), channel_id=1, source_target_pairs={{0,1},{1,2},{2,3},{3,0},{4,5},{5,6},{6,7},{7,4},{8,9},{9,10},{10,1... | collective-permute-start | bytes 454664 | tf_op jit(solution)/shard_map/ppermute | solution.py:375
  6.6 13.4 %collective-permute-start.1 = (f32[37,8,128]{2,1,0:T(8,128)S(1)}, f32[37,8,128]{2,1,0:T(8,128)S(1)}, u32[]{:S(2)}, u32[]{:S(2)}) collective-permute-start(f32[37,8,128]{2,1,0:T(8,128)S(1)} %get-tuple-element.37), channel_id=1, source_target_pairs={{0,2},{1,3},{2,0},{3,1},{4,6},{5,7},{6,4},{7,5},{8,10},{9,11},{10,... | collective-permute-start | bytes 454664 | tf_op jit(solution)/shard_map/ppermute | solution.py:375
  9.2 10.8 %collective-permute-start.2 = (f32[37,8,128]{2,1,0:T(8,128)S(1)}, f32[37,8,128]{2,1,0:T(8,128)S(1)}, u32[]{:S(2)}, u32[]{:S(2)}) collective-permute-start(f32[37,8,128]{2,1,0:T(8,128)S(1)} %get-tuple-element.38), channel_id=1, source_target_pairs={{0,3},{1,0},{2,1},{3,2},{4,7},{5,4},{6,5},{7,6},{8,11},{9,8},{10,9... | collective-permute-start | bytes 454664 | tf_op jit(solution)/shard_map/ppermute | solution.py:375
  12.3 10.1 %collective-permute-start.3 = (f32[36,8,128]{2,1,0:T(8,128)S(1)}, f32[36,8,128]{2,1,0:T(8,128)S(1)}, u32[]{:S(2)}, u32[]{:S(2)}) collective-permute-start(f32[36,8,128]{2,1,0:T(8,128)S(1)} %get-tuple-element.40), channel_id=1, source_target_pairs={{0,1},{1,2},{2,3},{3,0},{4,5},{5,6},{6,7},{7,4},{8,9},{9,10},{10,1... | collective-permute-start | bytes 442376 | tf_op jit(solution)/shard_map/ppermute | solution.py:375
  23.6 12.0 %collective-permute-start.6 = (f32[312,128]{1,0:T(8,128)S(1)}, f32[312,128]{1,0:T(8,128)S(1)}, u32[]{:S(2)}, u32[]{:S(2)}) collective-permute-start(f32[312,128]{1,0:T(8,128)S(1)} %get-tuple-element.44), channel_id=1, source_target_pairs={{0,1},{1,2},{2,3},{3,7},{7,6},{6,5},{5,4},{4,8},{8,9},{9,10},{10,1... | collective-permute-start | bytes 479240 | tf_op jit(solution)/shard_map/ppermute | solution.py:405
  29.3 9.7 %collective-permute-start.7 = (f32[312,128]{1,0:T(8,128)S(1)}, f32[312,128]{1,0:T(8,128)S(1)}, u32[]{:S(2)}, u32[]{:S(2)}) collective-permute-start(f32[312,128]{1,0:T(8,128)S(1)} %get-tuple-element.45), channel_id=1, source_target_pairs={{1,0},{2,1},{3,2},{7,3},{6,7},{5,6},{4,5},{8,4},{9,8},{10,9},{11,1... | collective-permute-start | bytes 479240 | tf_op jit(solution)/shard_map/ppermute | solution.py:406
  30.6 13.5 %collective-permute-start.4 = (f32[36,8,128]{2,1,0:T(8,128)S(1)}, f32[36,8,128]{2,1,0:T(8,128)S(1)}, u32[]{:S(2)}, u32[]{:S(2)}) collective-permute-start(f32[36,8,128]{2,1,0:T(8,128)S(1)} %get-tuple-element.41), channel_id=1, source_target_pairs={{0,2},{1,3},{2,0},{3,1},{4,6},{5,7},{6,4},{7,5},{8,10},{9,11},{10,... | collective-permute-start | bytes 442376 | tf_op jit(solution)/shard_map/ppermute | solution.py:375
  33.4 10.7 %collective-permute-start.5 = (f32[36,8,128]{2,1,0:T(8,128)S(1)}, f32[36,8,128]{2,1,0:T(8,128)S(1)}, u32[]{:S(2)}, u32[]{:S(2)}) collective-permute-start(f32[36,8,128]{2,1,0:T(8,128)S(1)} %get-tuple-element.42), channel_id=1, source_target_pairs={{0,3},{1,0},{2,1},{3,2},{4,7},{5,4},{6,5},{7,6},{8,11},{9,8},{10,9... | collective-permute-start | bytes 442376 | tf_op jit(solution)/shard_map/ppermute | solution.py:375
  46.7 52.9 %copy-start.1 = (f32[72,16,128]{2,1,0:T(8,128)S(1)}, f32[72,16,128]{2,1,0:T(8,128)}, u32[]{:S(2)}) copy-start(f32[72,16,128]{2,1,0:T(8,128)} %x_ref.1) | copy-start | bytes 1769476
  46.7 52.9 %copy-start.3 = (f32[72,16,128]{2,1,0:T(8,128)S(1)}, f32[72,16,128]{2,1,0:T(8,128)}, u32[]{:S(2)}) copy-start(f32[72,16,128]{2,1,0:T(8,128)} %f_ref.1) | copy-start | bytes 1769476
  46.7 11.9 %collective-permute-start.8 = (f32[2,288,128]{2,1,0:T(8,128)}, f32[2,288,128]{2,1,0:T(8,128)S(1)}, u32[]{:S(2)}, u32[]{:S(2)}) collective-permute-start(f32[2,288,128]{2,1,0:T(8,128)} %get-tuple-element.51), channel_id=1, source_target_pairs={{0,1},{1,2},{2,3},{3,7},{7,6},{6,5},{5,4},{4,8},{8,9},{9,10},{10,1... | collective-permute-start | bytes 884744 | tf_op jit(solution)/shard_map/ppermute | solution.py:420
  51.2 9.9 %collective-permute-start.9 = (f32[2,288,128]{2,1,0:T(8,128)}, f32[2,288,128]{2,1,0:T(8,128)S(1)}, u32[]{:S(2)}, u32[]{:S(2)}) collective-permute-start(f32[2,288,128]{2,1,0:T(8,128)} %get-tuple-element.52), channel_id=1, source_target_pairs={{1,0},{2,1},{3,2},{7,3},{6,7},{5,6},{4,5},{8,4},{9,8},{10,9},{11,1... | collective-permute-start | bytes 884744 | tf_op jit(solution)/shard_map/ppermute | solution.py:421
  52.5 17.6 %collective-permute-start.13 = (f32[36,8,128]{2,1,0:T(8,128)}, f32[36,8,128]{2,1,0:T(8,128)S(1)}, u32[]{:S(2)}, u32[]{:S(2)}) collective-permute-start(f32[36,8,128]{2,1,0:T(8,128)} %get-tuple-element.47.refs_5_), channel_id=1, source_target_pairs={{0,3},{1,0},{2,1},{3,2},{4,7},{5,4},{6,5},{7,6},{8,11},{9,8},{10,9... | collective-permute-start | bytes 442376 | tf_op jit(solution)/shard_map/ppermute | solution.py:375
  55.5 15.2 %collective-permute-start.14 = (f32[36,8,128]{2,1,0:T(8,128)}, f32[36,8,128]{2,1,0:T(8,128)S(1)}, u32[]{:S(2)}, u32[]{:S(2)}) collective-permute-start(f32[36,8,128]{2,1,0:T(8,128)} %get-tuple-element.48.refs_6_), channel_id=1, source_target_pairs={{0,2},{1,3},{2,0},{3,1},{4,6},{5,7},{6,4},{7,5},{8,10},{9,11},{10,... | collective-permute-start | bytes 442376 | tf_op jit(solution)/shard_map/ppermute | solution.py:375
  56.7 14.0 %collective-permute-start.15 = (f32[36,8,128]{2,1,0:T(8,128)}, f32[36,8,128]{2,1,0:T(8,128)S(1)}, u32[]{:S(2)}, u32[]{:S(2)}) collective-permute-start(f32[36,8,128]{2,1,0:T(8,128)} %get-tuple-element.49.refs_7_), channel_id=1, source_target_pairs={{0,1},{1,2},{2,3},{3,0},{4,5},{5,6},{6,7},{7,4},{8,9},{9,10},{10,1... | collective-permute-start | bytes 442376 | tf_op jit(solution)/shard_map/ppermute | solution.py:375
  70.7 16.8 %collective-permute-start.16 = (f32[72,8,128]{2,1,0:T(8,128)S(1)}, f32[72,8,128]{2,1,0:T(8,128)S(1)}, u32[]{:S(2)}, u32[]{:S(2)}) collective-permute-start(f32[72,8,128]{2,1,0:T(8,128)S(1)} %get-tuple-element.59), channel_id=1, source_target_pairs={{0,1},{1,2},{2,3},{3,0},{4,5},{5,6},{6,7},{7,4},{8,9},{9,10},{10,1... | collective-permute-start | bytes 884744 | tf_op jit(solution)/shard_map/ppermute | solution.py:375
  73.9 25.7 %collective-permute-start.20 = (f32[72,8,128]{2,1,0:T(8,128)S(1)}, f32[72,8,128]{2,1,0:T(8,128)S(1)}, u32[]{:S(2)}, u32[]{:S(2)}) collective-permute-start(f32[72,8,128]{2,1,0:T(8,128)S(1)} %get-tuple-element.66), channel_id=1, source_target_pairs={{0,3},{1,0},{2,1},{3,2},{4,7},{5,4},{6,5},{7,6},{8,11},{9,8},{10,9... | collective-permute-start | bytes 884744 | tf_op jit(solution)/shard_map/ppermute | solution.py:375
  74.5 25.1 %collective-permute-start.21 = (f32[72,8,128]{2,1,0:T(8,128)S(1)}, f32[72,8,128]{2,1,0:T(8,128)S(1)}, u32[]{:S(2)}, u32[]{:S(2)}) collective-permute-start(f32[72,8,128]{2,1,0:T(8,128)S(1)} %get-tuple-element.67), channel_id=1, source_target_pairs={{0,2},{1,3},{2,0},{3,1},{4,6},{5,7},{6,4},{7,5},{8,10},{9,11},{10,... | collective-permute-start | bytes 884744 | tf_op jit(solution)/shard_map/ppermute | solution.py:375
  75.4 1.2 %collective-permute-start.10 = (f32[32,128]{1,0:T(8,128)S(1)}, f32[32,128]{1,0:T(8,128)S(1)}, u32[]{:S(2)}, u32[]{:S(2)}) collective-permute-start(f32[32,128]{1,0:T(8,128)S(1)} %get-tuple-element.54), channel_id=1, source_target_pairs={{0,4},{4,0},{8,12},{12,8},{16,20},{20,16},{24,28},{28,24},{1,5},{5... | collective-permute-start | bytes 49160 | tf_op jit(solution)/shard_map/ppermute | solution.py:335
  76.6 3.7 %collective-permute-start.11 = (f32[32,128]{1,0:T(8,128)S(1)}, f32[32,128]{1,0:T(8,128)S(1)}, u32[]{:S(2)}, u32[]{:S(2)}) collective-permute-start(f32[32,128]{1,0:T(8,128)S(1)} %add.60), channel_id=1, source_target_pairs={{0,8},{4,12},{8,0},{12,4},{16,24},{20,28},{24,16},{28,20},{1,9},{5... | collective-permute-start | bytes 49160 | tf_op jit(solution)/shard_map/ppermute | solution.py:335
  80.3 3.7 %collective-permute-start.12 = (f32[32,128]{1,0:T(8,128)S(1)}, f32[32,128]{1,0:T(8,128)S(1)}, u32[]{:S(2)}, u32[]{:S(2)}) collective-permute-start(f32[32,128]{1,0:T(8,128)S(1)} %add.61), channel_id=1, source_target_pairs={{0,16},{4,20},{8,24},{12,28},{16,0},{20,4},{24,8},{28,12},{1,17},{... | collective-permute-start | bytes 49160 | tf_op jit(solution)/shard_map/ppermute | solution.py:335
  84.1 8.6 %collective-permute-start.19 = (f32[32,128]{1,0:T(8,128)S(1)}, f32[32,128]{1,0:T(8,128)S(1)}, u32[]{:S(2)}, u32[]{:S(2)}) collective-permute-start(f32[32,128]{1,0:T(8,128)S(1)} %add.62.refs_0_), channel_id=1, source_target_pairs={{0,1},{1,2},{2,3},{3,0},{4,5},{5,6},{6,7},{7,4},{8,9},{9,10},{10,1... | collective-permute-start | bytes 49160 | tf_op jit(solution)/shard_map/ppermute | solution.py:375
  84.6 15.0 %collective-permute-start.18 = (f32[32,128]{1,0:T(8,128)S(1)}, f32[32,128]{1,0:T(8,128)S(1)}, u32[]{:S(2)}, u32[]{:S(2)}) collective-permute-start(f32[32,128]{1,0:T(8,128)S(1)} %add.62.refs_0_), channel_id=1, source_target_pairs={{0,2},{1,3},{2,0},{3,1},{4,6},{5,7},{6,4},{7,5},{8,10},{9,11},{10,... | collective-permute-start | bytes 49160 | tf_op jit(solution)/shard_map/ppermute | solution.py:375
  87.5 12.1 %collective-permute-start.17 = (f32[32,128]{1,0:T(8,128)S(1)}, f32[32,128]{1,0:T(8,128)S(1)}, u32[]{:S(2)}, u32[]{:S(2)}) collective-permute-start(f32[32,128]{1,0:T(8,128)S(1)} %add.62.refs_0_), channel_id=1, source_target_pairs={{0,3},{1,0},{2,1},{3,2},{4,7},{5,4},{6,5},{7,6},{8,11},{9,8},{10,9... | collective-permute-start | bytes 49160 | tf_op jit(solution)/shard_map/ppermute | solution.py:375
  (6 other events, 39.6 us)

commit v4 on v3

--- a/solution.py
+++ b/solution.py
@@ -12,6 +12,7 @@
 DEGREE = 3
 SUB = 8
 LANES = 128
+UNROLL = 12
 PARAMS = pltpu.CompilerParams(vmem_limit_bytes=12 * 1024 * 1024)
 
 
@@ -37,19 +38,16 @@
     return edges
 
 
-def rank_row(multi_index):
-    here, modes = multi_index.shape
-    above = jnp.zeros((here, 1), jnp.int32)
-    symbols = [jnp.zeros((here, 1), jnp.int32)] * DEGREE
+def rank_row(powers):
+    modes, here = powers.shape
+    above = jnp.zeros((1, here), jnp.int32)
+    symbols = [jnp.zeros((1, here), jnp.int32)] * DEGREE
     for k in reversed(range(modes)):
-        above += jnp.maximum(multi_index[:, k : k + 1], 0)
+        above += jnp.maximum(powers[k : k + 1], 0)
         symbols = [a + jnp.where(above > n, 1, 0) for n, a in enumerate(symbols)]
     a, b, c = symbols
     rank = a * (a + 1) * (a + 2) // 6 + b * (b + 1) // 2 + c
-    rank = jnp.where(multi_index[:, 0:1] < 0, math.comb(modes + DEGREE, DEGREE), rank).astype(jnp.float32)
-    lane = lax.broadcasted_iota(jnp.int32, (here, LANES), 1)
-    slot = lax.broadcasted_iota(jnp.int32, (here, LANES), 0)
-    return jnp.sum(jnp.where(lane == slot, rank, 0.0), axis=0, keepdims=True)
+    return jnp.where(powers[0:1] < 0, math.comb(modes + DEGREE, DEGREE), rank).astype(jnp.float32)
 
 
 def cut_kernel(n, columns, rows, offsets_ref, source_ref, *refs):
@@ -61,10 +59,10 @@
             for q in range(rows):
                 out[q, g * columns : (g + 1) * columns] = source_ref[q * per + g, at]
     if index:
-        first = lax.broadcasted_iota(jnp.int32, (SUB, LANES), 0) == 0
-        tag = jnp.where(first, rank_row(index[0][...]), 0.0)
+        ranks = rank_row(index[0][...])
         for out in parts:
-            out[rows] = tag
+            out[rows] = jnp.zeros((SUB, LANES), jnp.float32)
+            out[rows, 0:1, 0 : ranks.shape[1]] = ranks
 
 
 def lane_next(u):
@@ -127,7 +125,7 @@
             out[first + q] = row
             return carry
 
-        lax.fori_loop(0, rows, one, 0, unroll=4)
+        lax.fori_loop(0, rows, one, 0, unroll=min(rows, UNROLL))
 
 
 def scatter_row(ranks_ref, at, row, field_ref, columns):
@@ -141,7 +139,7 @@
     return flat_ref[pl.ds(j, rows, stride=SUB), :]
 
 
-def enter_kernel(n, columns, rows, ranks_ref, coef_ref, _, *refs):
+def enter_kernel(n, columns, rows, ranks_ref, coef_ref, *refs):
     parts, (field_ref, first_ref, last_ref) = refs[:n], refs[n:]
     slots = field_ref.shape[0]
     fields = coef_ref.shape[0]
@@ -152,54 +150,59 @@
             scatter_row(ranks_ref, d * rows + q, part[q], field_ref, columns)
             return carry
 
-        lax.fori_loop(0, rows, one, 0, unroll=4)
+        lax.fori_loop(0, rows, one, 0, unroll=min(rows, UNROLL))
     flat = field_ref.reshape(slots * SUB, LANES)
-    first_ref[slots:] = jnp.zeros_like(first_ref[slots:])
-    last_ref[slots:] = jnp.zeros_like(last_ref[slots:])
-    first_ref[0:slots] = take_column(flat, 0, slots)
-    last_ref[0:slots] = take_column(flat, columns - 1, slots)
+    terms = first_ref.shape[0] - 2 * fields
+    first_ref[0:terms] = take_column(flat, 0, terms)
+    last_ref[0:terms] = take_column(flat, columns - 1, terms)
     flat = coef_ref.reshape(fields * SUB, LANES)
     for j in range(2):
-        at = slots + j * fields
+        at = terms + j * fields
         first_ref[at : at + fields] = take_column(flat, j, fields)
         last_ref[at : at + fields] = take_column(flat, columns - 2 + j, fields)
 
 
-def start_kernel(n, columns, edges, ranks_ref, x_ref, before_ref, after_ref, own_ref, *refs):
-    packed, (coef_ref, u_ref, y_ref, diff_ref) = refs[:n], refs[n:]
-    slots, fields = x_ref.shape[0], own_ref.shape[0]
+def start_kernel(columns, edges, x_ref, before_ref, after_ref, own_ref, y_ref, coef_ref, u_ref, diff_ref):
+    slots, fields, terms = x_ref.shape[0], own_ref.shape[0], len(edges)
     coef_ref[...] = own_ref[...]
     flat = coef_ref.reshape(fields * SUB, LANES)
     for j in range(2):
-        at = slots + j * fields
+        at = terms + j * fields
         flat[pl.ds(SUB - 2 + j, fields, stride=SUB), :] = before_ref[at : at + fields]
         flat[pl.ds(columns + j, fields, stride=SUB), :] = after_ref[at : at + fields]
     u_ref[...] = x_ref[...]
     flat = u_ref.reshape(slots * SUB, LANES)
-    flat[pl.ds(SUB - 1, slots, stride=SUB), :] = before_ref[0:slots]
-    flat[pl.ds(columns, slots, stride=SUB), :] = after_ref[0:slots]
+    flat[pl.ds(SUB - 1, terms, stride=SUB), :] = before_ref[0:terms]
+    flat[pl.ds(columns, terms, stride=SUB), :] = after_ref[0:terms]
     y_ref[len(edges) :] = jnp.zeros((slots - len(edges), SUB, LANES), jnp.float32)
 
     def store(s, value):
         y_ref[s] = value
 
     apply_operator(u_ref, coef_ref, edges, store, diff_ref)
-    pack_rows(ranks_ref, packed, y_ref, columns, packed[0].shape[0])
-
-
-def residual_kernel(n, columns, ranks_ref, *refs):
-    forcing, image = refs[:n], refs[n : 2 * n]
-    field_ref, first_ref, last_ref = refs[2 * n :]
-    rows = forcing[0].shape[0]
+
+
+def residual_kernel(n, columns, rows, ranks_ref, y_ref, *refs):
+    forcing, packed, (field_ref, first_ref, last_ref) = refs[:n], refs[n : 2 * n], refs[2 * n :]
+    per = SUB // columns
     slots = field_ref.shape[0]
+    sub = lax.broadcasted_iota(jnp.int32, (SUB, LANES), 0)
     field_ref[...] = jnp.zeros_like(field_ref)
     for d in range(n):
 
         def one(q, carry, d=d):
-            scatter_row(ranks_ref, d * rows + q, forcing[d][q] - image[d][q], field_ref, columns)
+            at = [ranks_ref[(d * rows + q) * per + g] for g in range(per)]
+            y = y_ref[at[0]]
+            for g in range(1, per):
+                y = jnp.where(sub < g * columns, y, pltpu.roll(y_ref[at[g]], g * columns, 0))
+            v = forcing[d][q] - y
+            packed[d][q] = v
+            for g in range(per):
+                own = v if g == 0 else pltpu.roll(v, SUB - g * columns, 0)
+                field_ref[at[g], 0:columns] = own[0:columns]
             return carry
 
-        lax.fori_loop(0, rows, one, 0, unroll=4)
+        lax.fori_loop(0, rows, one, 0, unroll=min(rows, UNROLL))
     flat = field_ref.reshape(slots * SUB, LANES)
     for j in range(2):
         first_ref[j] = take_column(flat, j, slots)
@@ -237,7 +240,7 @@
     def one(s, totals):
         return tuple(t + x for t, x in zip(totals, of_term(s)))
 
-    totals = lax.fori_loop(0, terms, one, (jnp.zeros((SUB, LANES), jnp.float32),) * count, unroll=11)
+    totals = lax.fori_loop(0, terms, one, (jnp.zeros((SUB, LANES), jnp.float32),) * count, unroll=16)
     own = lax.broadcasted_iota(jnp.int32, (SUB, LANES), 0) < columns
     totals = [jnp.where(own, t, 0.0) for t in totals]
     return [jnp.sum(jnp.sum(t, axis=0, keepdims=True), axis=1, keepdims=True) for t in totals]
@@ -282,29 +285,28 @@
     return step, beta, rr / (r_ar + beta * mixed + beta * beta * curve)
 
 
-def finish_kernel(n, columns, offsets_ref, x_ref, f_ref, *refs):
-    tables, image, krylov = refs[:n], refs[n : 2 * n], refs[2 * n : 3 * n]
+def finish_kernel(n, columns, offsets_ref, x_ref, *refs):
+    tables, v0, krylov = refs[:n], refs[n : 2 * n], refs[2 * n : 3 * n]
     approx_ref, residual_ref = refs[3 * n :]
     per = SUB // columns
-    rows = image[0].shape[0]
+    rows = v0[0].shape[0]
     step, beta, last = step_lengths(functools.reduce(jnp.add, [t[...] for t in tables]))
     whole = step + last * beta
     for d in range(n):
         at = pl.ds(pl.multiple_of(offsets_ref[d], columns), columns)
 
         def one(q, carry, d=d, at=at):
-            y, b, c = image[d][q], krylov[d][q], krylov[d][rows + q]
+            a, b, c = v0[d][q], krylov[d][q], krylov[d][rows + q]
             for g in range(per):
                 part = slice(g * columns, (g + 1) * columns)
                 s = q * per + g
-                yg, bg, cg = y[part], b[part], c[part]
-                v0 = f_ref[s, at] - yg
-                r1 = v0 - step * bg
-                approx_ref[s, at] = x_ref[s, at] + whole * v0 + last * r1
+                ag, bg, cg = a[part], b[part], c[part]
+                r1 = ag - step * bg
+                approx_ref[s, at] = x_ref[s, at] + whole * ag + last * r1
                 residual_ref[s, at] = r1 - last * ((1.0 + beta) * bg - step * cg)
             return carry
 
-        lax.fori_loop(0, rows, one, 0, unroll=2)
+        lax.fori_loop(0, rows, one, 0, unroll=min(rows, UNROLL))
 
 
 class Anywhere:
@@ -377,14 +379,16 @@
 
     field, part, fields = (slots, SUB, lanes), (rows, SUB, lanes), (modes + 1, SUB, lanes)
     diff = (3,) + field
-    edge = (-(-(slots + 2 * (modes + 1)) // SUB) * SUB, lanes)
+    edge = (len(edges) + 2 * (modes + 1), lanes)
     offsets_array = jnp.stack(offsets).astype(jnp.int32)
 
+    f_rows = max(rows, edge[0] // SUB + 1)
+    f_shapes = [(f_rows + (d != n // 2), SUB, lanes) for d in range(n)]
     cut = functools.partial(cut_kernel, n, columns, rows)
-    x_parts = call(cut, [offsets_array], [start_guess, multi_index], [(rows + 1, SUB, lanes)] * n)
+    x_parts = call(cut, [offsets_array], [start_guess, multi_index.T], [(rows + 1 + (d == n // 2), SUB, lanes) for d in range(n)])
     x_parts = sent(list(x_parts), outward)
     ranks = jnp.concatenate([p[rows, 0, :here] for p in x_parts]).astype(jnp.int32)
-    f_parts = sent(list(call(cut, [offsets_array], [forcing], [part] * n)), outward)
+    f_parts = sent(list(call(cut, [offsets_array], [forcing], f_shapes)), outward)
 
     stacked = jnp.concatenate([mean_field[None], mode_fields], axis=0)
     own_coef = lax.dynamic_slice_in_dim(stacked, offsets[0], columns, axis=1)
@@ -399,27 +403,27 @@
     x, x_first, x_last = call(
         functools.partial(enter_kernel, n, columns, rows),
         [ranks],
-        [own_coef, Anywhere(f_parts[1])] + x_parts,
+        [own_coef] + x_parts,
         [field, edge, edge],
     )
     x_before = lax.ppermute(x_last, both, line)
     x_after = lax.ppermute(x_first, both, back_line)
-    *image, coef = call(
-        functools.partial(start_kernel, n, columns, edges),
+    image, coef = call(
+        functools.partial(start_kernel, columns, edges),
+        [],
+        [x, x_before, x_after, own_coef],
+        [field, fields],
+        [field, diff],
+    )
+    *v0_parts, v0, v0_first, v0_last = call(
+        functools.partial(residual_kernel, n, columns, rows),
         [ranks],
-        [x, x_before, x_after, own_coef],
-        [part] * n + [fields],
-        [field, field, diff],
-    )
-    v0, v0_first, v0_last = call(
-        functools.partial(residual_kernel, n, columns),
-        [ranks],
-        f_parts + image,
-        [field, (2, slots, lanes), (2, slots, lanes)],
+        [image] + f_parts,
+        [part] * n + [field, (2, slots, lanes), (2, slots, lanes)],
     )
     v0_before = lax.ppermute(v0_last, both, line)
     v0_after = lax.ppermute(v0_first, both, back_line)
-    image_home = sent(image, homeward)
+    v0_home = sent(v0_parts, homeward)
     *krylov, table = call(
         functools.partial(krylov_kernel, n, columns, edges),
         [ranks, (i * n + z).astype(jnp.int32)[None]],
@@ -427,14 +431,14 @@
         [(2 * rows, SUB, lanes)] * n + [(-(-spaces * n // SUB) * SUB, lanes)],
         [field, field, field, diff],
     )
-    krylov, image_home = lax.optimization_barrier((krylov, image_home))
+    krylov, v0_home = lax.optimization_barrier((krylov, v0_home))
     krylov_home = sent(krylov, homeward)
     table = butterfly(table, "space")
     tables = sent([table] * n, homeward, [None, krylov_home[n - 1]] + [None] * (n - 2))
     return call(
         functools.partial(finish_kernel, n, columns),
         [offsets_array],
-        [start_guess, forcing] + tables + image_home + krylov_home,
+        [start_guess] + tables + v0_home + krylov_home,
         [forcing.shape] * 2,
     )
 

time: 103 us -> 100 us (0.971)
  starting transfers between devices: 42.6 us -> 50.4 us
  waiting for transfers between devices: 34.1 us -> 28 us
  Pallas kernels: 20.5 us -> 16.9 us
    ppermute x15, starting transfers between devices: 26.6 us -> 37 us  [sent(): out.append(lax.ppermute(value, 'chaos', way(d)))]
    ppermute x15, waiting for transfers between devices: 20.9 us -> 13 us  [sent(): out.append(lax.ppermute(value, 'chaos', way(d)))]
    pallas_call x7, Pallas kernels: 20.5 us -> 16.9 us  [call(): pl.pallas_call(kernel, in_specs=[pl.BlockSpec(memory_space=pltpu.SMEM)] *...]
    ppermute x1, starting transfers between devices: 5.67 us -> 2.95 us  [per_device(): x_before = lax.ppermute(x_last, both, line)]
    ppermute x1, waiting for transfers between devices: 1.92 us -> 0.01 us  [per_device(): v0_before = lax.ppermute(v0_last, both, line)]
    ppermute x1, waiting for transfers between devices: 3.28 us -> 4.99 us  [per_device(): x_after = lax.ppermute(x_first, both, back_line)]
    ppermute x1, waiting for transfers between devices: 0.01 us -> 1.47 us  [per_device(): x_before = lax.ppermute(x_last, both, line)]
    unnamed x17 -> x12, local copies, waits for them, and re-layouts: 3.72 us -> 2.84 us
  transfers between devices with their start and end apart: 22 -> 22, of which waited for: 13 -> 10; matrix products, arithmetic and copies ran while one was open for 0% -> 0% of each run, Pallas kernels for 13% -> 12%
where the time goes in v4:
time: 100 us; the launch traced here: 99.3 us
  starting transfers between devices  50.4 us (50%)
  waiting for transfers between devices  28 us (28%)
  Pallas kernels  16.9 us (17%)
  local copies, waits for them, and re-layouts  2.92 us (3%)
    ppermute x15, starting transfers between devices, sent(): out.append(lax.ppermute(value, 'chaos', way(d)))  37 us
    pallas_call x7, Pallas kernels, call(): pl.pallas_call(kernel, in_specs=[pl.BlockSpec(memory_space=pltpu.SMEM)] *...  16.9 us
    ppermute x15, waiting for transfers between devices, sent(): out.append(lax.ppermute(value, 'chaos', way(d)))  13 us
    ppermute x3, waiting for transfers between devices, butterfly(): lax.ppermute(value, axis, [(i, i ^ bit) for i in range(count)])  5.3 us
    ppermute x1, waiting for transfers between devices, per_device(): x_after = lax.ppermute(x_first, both, back_line)  4.99 us
    ppermute x1, starting transfers between devices, per_device(): v0_before = lax.ppermute(v0_last, both, line)  4.33 us
    ppermute x3, starting transfers between devices, butterfly(): lax.ppermute(value, axis, [(i, i ^ bit) for i in range(count)])  3.61 us
    ppermute x1, waiting for transfers between devices, per_device(): v0_after = lax.ppermute(v0_first, both, back_line)  3.19 us
  transfers between devices with their start and end apart: 22, of which 10 were waited for; matrix products, arithmetic and copies ran while one was open for 0% of the time, Pallas kernels for 12%

profile of v4, /device:TPU:0, one launch (start us, length us, event | category | flops | bytes accessed | tf_op | source)
XLA Modules:
  0.0 99.3 jit_solution(4137471652003631806)
XLA Ops:
  3.2 4.1 %collective-permute-start.1 = (f32[38,8,128]{2,1,0:T(8,128)S(1)}, f32[38,8,128]{2,1,0:T(8,128)S(1)}, u32[]{:S(2)}, u32[]{:S(2)}) collective-permute-start(f32[38,8,128]{2,1,0:T(8,128)S(1)} %get-tuple-element.38), channel_id=1, source_target_pairs={{0,2},{1,3},{2,0},{3,1},{4,6},{5,7},{6,4},{7,5},{8,10},{9,11},{10,... | collective-permute-start | bytes 466952 | tf_op jit(solution)/shard_map/ppermute | solution.py:377
  11.1 1.6 %collective-permute-start.5 = (f32[40,8,128]{2,1,0:T(8,128)S(1)}, f32[40,8,128]{2,1,0:T(8,128)S(1)}, u32[]{:S(2)}, u32[]{:S(2)}) collective-permute-start(f32[40,8,128]{2,1,0:T(8,128)S(1)} %get-tuple-element.45), channel_id=1, source_target_pairs={{0,1},{1,2},{2,3},{3,0},{4,5},{5,6},{6,7},{7,4},{8,9},{9,10},{10,1... | collective-permute-start | bytes 491528 | tf_op jit(solution)/shard_map/ppermute | solution.py:377
  12.7 2.2 %collective-permute-start.7 = (f32[40,8,128]{2,1,0:T(8,128)S(1)}, f32[40,8,128]{2,1,0:T(8,128)S(1)}, u32[]{:S(2)}, u32[]{:S(2)}) collective-permute-start(f32[40,8,128]{2,1,0:T(8,128)S(1)} %get-tuple-element.47), channel_id=1, source_target_pairs={{0,3},{1,0},{2,1},{3,2},{4,7},{5,4},{6,5},{7,6},{8,11},{9,8},{10,9... | collective-permute-start | bytes 491528 | tf_op jit(solution)/shard_map/ppermute | solution.py:377
  15.1 10.0 %collective-permute-start.6 = (f32[39,8,128]{2,1,0:T(8,128)S(1)}, f32[39,8,128]{2,1,0:T(8,128)S(1)}, u32[]{:S(2)}, u32[]{:S(2)}) collective-permute-start(f32[39,8,128]{2,1,0:T(8,128)S(1)} %get-tuple-element.46), channel_id=1, source_target_pairs={{0,2},{1,3},{2,0},{3,1},{4,6},{5,7},{6,4},{7,5},{8,10},{9,11},{10,... | collective-permute-start | bytes 479240 | tf_op jit(solution)/shard_map/ppermute | solution.py:377
  26.3 3.0 %collective-permute-start.3 = (f32[308,128]{1,0:T(8,128)S(1)}, f32[308,128]{1,0:T(8,128)S(1)}, u32[]{:S(2)}, u32[]{:S(2)}) collective-permute-start(f32[308,128]{1,0:T(8,128)S(1)} %get-tuple-element.41), channel_id=1, source_target_pairs={{0,1},{1,2},{2,3},{3,7},{7,6},{6,5},{5,4},{4,8},{8,9},{9,10},{10,1... | collective-permute-start | bytes 473096 | tf_op jit(solution)/shard_map/ppermute | solution.py:409
  30.5 1.5 %collective-permute-done.3.before_ref = f32[308,128]{1,0:T(8,128)S(1)} collective-permute-done((f32[308,128]{1,0:T(8,128)S(1)}, f32[308,128]{1,0:T(8,128)S(1)}, u32[]{:S(2)}, u32[]{:S(2)}) %collective-permute-start.3) | collective-permute-done | bytes 157728 | tf_op jit(solution)/shard_map/ppermute | solution.py:409
  32.0 5.0 %collective-permute-done.4.after_ref = f32[308,128]{1,0:T(8,128)S(1)} collective-permute-done((f32[308,128]{1,0:T(8,128)S(1)}, f32[308,128]{1,0:T(8,128)S(1)}, u32[]{:S(2)}, u32[]{:S(2)}) %collective-permute-start.4) | collective-permute-done | bytes 157728 | tf_op jit(solution)/shard_map/ppermute | solution.py:410
  37.0 2.7 %shard_map.70 = (f32[288,8,128]{2,1,0:T(8,128)S(1)}, f32[11,8,128]{2,1,0:T(8,128)S(1)}) custom-call(f32[288,8,128]{2,1,0:T(8,128)S(1)} %get-tuple-element.40.x_ref, f32[308,128]{1,0:T(8,128)S(1)} %collective-permute-done.3.before_ref, f32[308,128]{1,0:T(8,128)S(1)} %collective-permute-done.4.after_ref, f32[11,8,128]{2,1,0:T(8,128)S(1)} %pad.4.coef_ref.own_ref), custom_call_target="tpu_custom_call" | custom-call | tf_op jit(solution)/shard_map/pallas_call | solution.py:323
  39.7 2.1 %shard_map.72 = (f32[36,8,128]{2,1,0:T(8,128)S(1)}, f32[36,8,128]{2,1,0:T(8,128)}, f32[36,8,128]{2,1,0:T(8,128)}, f32[36,8,128]{2,1,0:T(8,128)S(1)}, f32[288,8,1...) custom-call(s32[288]{0:T(512)S(1)} %maximum_convert_fusion.ranks_ref, ...), custom_call_target="tpu_custom_call" | custom-call | tf_op jit(solution)/shard_map/pallas_call | solution.py:323
  41.8 4.3 %collective-permute-start.8 = (f32[2,288,128]{2,1,0:T(8,128)}, f32[2,288,128]{2,1,0:T(8,128)S(1)}, u32[]{:S(2)}, u32[]{:S(2)}) collective-permute-start(f32[2,288,128]{2,1,0:T(8,128)} %get-tuple-element.49), channel_id=1, source_target_pairs={{0,1},{1,2},{2,3},{3,7},{7,6},{6,5},{5,4},{4,8},{8,9},{9,10},{10,1... | collective-permute-start | bytes 884744 | tf_op jit(solution)/shard_map/ppermute | solution.py:424
  47.5 4.5 %collective-permute-start.13 = (f32[36,8,128]{2,1,0:T(8,128)}, f32[36,8,128]{2,1,0:T(8,128)S(1)}, u32[]{:S(2)}, u32[]{:S(2)}) collective-permute-start(f32[36,8,128]{2,1,0:T(8,128)} %get-tuple-element.58), channel_id=1, source_target_pairs={{0,3},{1,0},{2,1},{3,2},{4,7},{5,4},{6,5},{7,6},{8,11},{9,8},{10,9... | collective-permute-start | bytes 442376 | tf_op jit(solution)/shard_map/ppermute | solution.py:377
  52.1 1.9 %collective-permute-start.15 = (f32[36,8,128]{2,1,0:T(8,128)S(1)}, f32[36,8,128]{2,1,0:T(8,128)S(1)}, u32[]{:S(2)}, u32[]{:S(2)}) collective-permute-start(f32[36,8,128]{2,1,0:T(8,128)S(1)} %get-tuple-element.60), channel_id=1, source_target_pairs={{0,1},{1,2},{2,3},{3,0},{4,5},{5,6},{6,7},{7,4},{8,9},{9,10},{10,1... | collective-permute-start | bytes 442376 | tf_op jit(solution)/shard_map/ppermute | solution.py:377
  54.1 3.2 %collective-permute-done.9.after_ref = f32[2,288,128]{2,1,0:T(8,128)S(1)} collective-permute-done((f32[2,288,128]{2,1,0:T(8,128)S(1)}, f32[2,288,128]{2,1,0:T(8,128)S(1)}, u32[]{:S(2)}, u32[]{:S(2)}) %collective-permute-start.9) | collective-permute-done | bytes 294944 | tf_op jit(solution)/shard_map/ppermute | solution.py:425
  57.4 7.7 %shard_map.73 = (f32[72,8,128]{2,1,0:T(8,128)S(1)}, f32[72,8,128]{2,1,0:T(8,128)S(1)}, f32[72,8,128]{2,1,0:T(8,128)S(1)}, f32[72,8,128]{2,1,0:T(8,128)S(1)}, f32[32,128]{1,0:T(8,128)S(1)}) custom-call(s32[288]{0:T(512)S(1)} %maximum_convert_fusion.ranks_ref, s32[1]{0:T(128)} %bitcast.9.place_ref, f32[288,8,128]{2,1,0:T(8,128)S(1)} %get-tuple-element.48.v_ref, ...), custom_call_target="tpu_custom_call" | custom-call | tf_op jit(solution)/shard_map/pallas_call | solution.py:323
  65.1 3.3 %collective-permute-done.14.refs_6_ = f32[36,8,128]{2,1,0:T(8,128)S(1)} collective-permute-done((f32[36,8,128]{2,1,0:T(8,128)}, f32[36,8,128]{2,1,0:T(8,128)S(1)}, u32[]{:S(2)}, u32[]{:S(2)}) %collective-permute-start.14) | collective-permute-done | bytes 147488 | tf_op jit(solution)/shard_map/ppermute | solution.py:377
  69.3 2.9 %collective-permute-start.20 = (f32[72,8,128]{2,1,0:T(8,128)S(1)}, f32[72,8,128]{2,1,0:T(8,128)S(1)}, u32[]{:S(2)}, u32[]{:S(2)}) collective-permute-start(f32[72,8,128]{2,1,0:T(8,128)S(1)} %get-tuple-element.68), channel_id=1, source_target_pairs={{0,3},{1,0},{2,1},{3,2},{4,7},{5,4},{6,5},{7,6},{8,11},{9,8},{10,9... | collective-permute-start | bytes 884744 | tf_op jit(solution)/shard_map/ppermute | solution.py:377
  74.9 1.5 %collective-permute-start.11 = (f32[32,128]{1,0:T(8,128)S(1)}, f32[32,128]{1,0:T(8,128)S(1)}, u32[]{:S(2)}, u32[]{:S(2)}) collective-permute-start(f32[32,128]{1,0:T(8,128)S(1)} %add.60), channel_id=1, source_target_pairs={{0,8},{4,12},{8,0},{12,4},{16,24},{20,28},{24,16},{28,20},{1,9},{5... | collective-permute-start | bytes 49160 | tf_op jit(solution)/shard_map/ppermute | solution.py:337
  76.4 2.2 %collective-permute-done.11 = f32[32,128]{1,0:T(8,128)S(1)} collective-permute-done((f32[32,128]{1,0:T(8,128)S(1)}, f32[32,128]{1,0:T(8,128)S(1)}, u32[]{:S(2)}, u32[]{:S(2)}) %collective-permute-start.11) | collective-permute-done | bytes 16416 | tf_op jit(solution)/shard_map/ppermute | solution.py:337
  78.6 1.5 %collective-permute-start.12 = (f32[32,128]{1,0:T(8,128)S(1)}, f32[32,128]{1,0:T(8,128)S(1)}, u32[]{:S(2)}, u32[]{:S(2)}) collective-permute-start(f32[32,128]{1,0:T(8,128)S(1)} %add.61), channel_id=1, source_target_pairs={{0,16},{4,20},{8,24},{12,28},{16,0},{20,4},{24,8},{28,12},{1,17},{... | collective-permute-start | bytes 49160 | tf_op jit(solution)/shard_map/ppermute | solution.py:337
  80.1 2.2 %collective-permute-done.12 = f32[32,128]{1,0:T(8,128)S(1)} collective-permute-done((f32[32,128]{1,0:T(8,128)S(1)}, f32[32,128]{1,0:T(8,128)S(1)}, u32[]{:S(2)}, u32[]{:S(2)}) %collective-permute-start.12) | collective-permute-done | bytes 16416 | tf_op jit(solution)/shard_map/ppermute | solution.py:337
  82.4 1.5 %collective-permute-start.18 = (f32[32,128]{1,0:T(8,128)S(1)}, f32[32,128]{1,0:T(8,128)S(1)}, u32[]{:S(2)}, u32[]{:S(2)}) collective-permute-start(f32[32,128]{1,0:T(8,128)S(1)} %add.62.refs_0_), channel_id=1, source_target_pairs={{0,2},{1,3},{2,0},{3,1},{4,6},{5,7},{6,4},{7,5},{8,10},{9,11},{10,... | collective-permute-start | bytes 49160 | tf_op jit(solution)/shard_map/ppermute | solution.py:377
  84.1 3.5 %collective-permute-start.17 = (f32[32,128]{1,0:T(8,128)S(1)}, f32[32,128]{1,0:T(8,128)S(1)}, u32[]{:S(2)}, u32[]{:S(2)}) collective-permute-start(f32[32,128]{1,0:T(8,128)S(1)} %add.62.refs_0_), channel_id=1, source_target_pairs={{0,3},{1,0},{2,1},{3,2},{4,7},{5,4},{6,5},{7,6},{8,11},{9,8},{10,9... | collective-permute-start | bytes 49160 | tf_op jit(solution)/shard_map/ppermute | solution.py:377
  87.6 9.4 %collective-permute-done.18.refs_2_ = f32[32,128]{1,0:T(8,128)S(1)} collective-permute-done((f32[32,128]{1,0:T(8,128)S(1)}, f32[32,128]{1,0:T(8,128)S(1)}, u32[]{:S(2)}, u32[]{:S(2)}) %collective-permute-start.18) | collective-permute-done | bytes 16416 | tf_op jit(solution)/shard_map/ppermute | solution.py:377
  97.3 2.0 %shard_map.74 = (f32[72,16,128]{2,1,0:T(8,128)}, f32[72,16,128]{2,1,0:T(8,128)}) custom-call(s32[4]{0:T(128)S(1)} %pad_add_fusion.offsets_ref, f32[72,16,128]{2,1,0:T(8,128)S(1)} %copy-done.1, f32[32,128]{1,0:T(8,128)S(1)} %add.62.refs_0_, f32[32,128]{1,0:T(8,128)S(1)} %collective-permute-done.17.refs_1_, f32[32,128]{1,0:T(8,128)S(1)} %collective-permute-done.18.refs_2_, ...), custom_call_target="tpu_custom_call" | custom-call | tf_op jit(solution)/shard_map/pallas_call | solution.py:323
  (52 shorter events, 14.5 us)
Async XLA Ops:
  0.6 14.3 %copy-start.5 = (f32[16,128]{1,0:T(8,128)S(1)}, f32[16,128]{1,0:T(8,128)}, u32[]{:S(2)}) copy-start(f32[16,128]{1,0:T(8,128)} %param.8) | copy-start | bytes 24580
  3.2 21.9 %collective-permute-start.1 = (f32[38,8,128]{2,1,0:T(8,128)S(1)}, f32[38,8,128]{2,1,0:T(8,128)S(1)}, u32[]{:S(2)}, u32[]{:S(2)}) collective-permute-start(f32[38,8,128]{2,1,0:T(8,128)S(1)} %get-tuple-element.38), channel_id=1, source_target_pairs={{0,2},{1,3},{2,0},{3,1},{4,6},{5,7},{6,4},{7,5},{8,10},{9,11},{10,... | collective-permute-start | bytes 466952 | tf_op jit(solution)/shard_map/ppermute | solution.py:377
  7.3 7.7 %collective-permute-start.2 = (f32[37,8,128]{2,1,0:T(8,128)S(1)}, f32[37,8,128]{2,1,0:T(8,128)S(1)}, u32[]{:S(2)}, u32[]{:S(2)}) collective-permute-start(f32[37,8,128]{2,1,0:T(8,128)S(1)} %get-tuple-element.39), channel_id=1, source_target_pairs={{0,3},{1,0},{2,1},{3,2},{4,7},{5,4},{6,5},{7,6},{8,11},{9,8},{10,9... | collective-permute-start | bytes 454664 | tf_op jit(solution)/shard_map/ppermute | solution.py:377
  8.7 16.4 %collective-permute-start = (f32[37,8,128]{2,1,0:T(8,128)S(1)}, f32[37,8,128]{2,1,0:T(8,128)S(1)}, u32[]{:S(2)}, u32[]{:S(2)}) collective-permute-start(f32[37,8,128]{2,1,0:T(8,128)S(1)} %get-tuple-element.37), channel_id=1, source_target_pairs={{0,1},{1,2},{2,3},{3,0},{4,5},{5,6},{6,7},{7,4},{8,9},{9,10},{10,1... | collective-permute-start | bytes 454664 | tf_op jit(solution)/shard_map/ppermute | solution.py:377
  11.1 28.6 %collective-permute-start.5 = (f32[40,8,128]{2,1,0:T(8,128)S(1)}, f32[40,8,128]{2,1,0:T(8,128)S(1)}, u32[]{:S(2)}, u32[]{:S(2)}) collective-permute-start(f32[40,8,128]{2,1,0:T(8,128)S(1)} %get-tuple-element.45), channel_id=1, source_target_pairs={{0,1},{1,2},{2,3},{3,0},{4,5},{5,6},{6,7},{7,4},{8,9},{9,10},{10,1... | collective-permute-start | bytes 491528 | tf_op jit(solution)/shard_map/ppermute | solution.py:377
  12.7 27.0 %collective-permute-start.7 = (f32[40,8,128]{2,1,0:T(8,128)S(1)}, f32[40,8,128]{2,1,0:T(8,128)S(1)}, u32[]{:S(2)}, u32[]{:S(2)}) collective-permute-start(f32[40,8,128]{2,1,0:T(8,128)S(1)} %get-tuple-element.47), channel_id=1, source_target_pairs={{0,3},{1,0},{2,1},{3,2},{4,7},{5,4},{6,5},{7,6},{8,11},{9,8},{10,9... | collective-permute-start | bytes 491528 | tf_op jit(solution)/shard_map/ppermute | solution.py:377
  15.1 24.6 %collective-permute-start.6 = (f32[39,8,128]{2,1,0:T(8,128)S(1)}, f32[39,8,128]{2,1,0:T(8,128)S(1)}, u32[]{:S(2)}, u32[]{:S(2)}) collective-permute-start(f32[39,8,128]{2,1,0:T(8,128)S(1)} %get-tuple-element.46), channel_id=1, source_target_pairs={{0,2},{1,3},{2,0},{3,1},{4,6},{5,7},{6,4},{7,5},{8,10},{9,11},{10,... | collective-permute-start | bytes 479240 | tf_op jit(solution)/shard_map/ppermute | solution.py:377
  26.3 5.7 %collective-permute-start.3 = (f32[308,128]{1,0:T(8,128)S(1)}, f32[308,128]{1,0:T(8,128)S(1)}, u32[]{:S(2)}, u32[]{:S(2)}) collective-permute-start(f32[308,128]{1,0:T(8,128)S(1)} %get-tuple-element.41), channel_id=1, source_target_pairs={{0,1},{1,2},{2,3},{3,7},{7,6},{6,5},{5,4},{4,8},{8,9},{9,10},{10,1... | collective-permute-start | bytes 473096 | tf_op jit(solution)/shard_map/ppermute | solution.py:409
  29.2 7.8 %collective-permute-start.4 = (f32[308,128]{1,0:T(8,128)S(1)}, f32[308,128]{1,0:T(8,128)S(1)}, u32[]{:S(2)}, u32[]{:S(2)}) collective-permute-start(f32[308,128]{1,0:T(8,128)S(1)} %get-tuple-element.42), channel_id=1, source_target_pairs={{1,0},{2,1},{3,2},{7,3},{6,7},{5,6},{4,5},{8,4},{9,8},{10,9},{11,1... | collective-permute-start | bytes 473096 | tf_op jit(solution)/shard_map/ppermute | solution.py:410
  41.8 55.5 %copy-start.1 = (f32[72,16,128]{2,1,0:T(8,128)S(1)}, f32[72,16,128]{2,1,0:T(8,128)}, u32[]{:S(2)}) copy-start(f32[72,16,128]{2,1,0:T(8,128)} %x_ref.1) | copy-start | bytes 1769476
  41.8 12.3 %collective-permute-start.8 = (f32[2,288,128]{2,1,0:T(8,128)}, f32[2,288,128]{2,1,0:T(8,128)S(1)}, u32[]{:S(2)}, u32[]{:S(2)}) collective-permute-start(f32[2,288,128]{2,1,0:T(8,128)} %get-tuple-element.49), channel_id=1, source_target_pairs={{0,1},{1,2},{2,3},{3,7},{7,6},{6,5},{5,4},{4,8},{8,9},{9,10},{10,1... | collective-permute-start | bytes 884744 | tf_op jit(solution)/shard_map/ppermute | solution.py:424
  46.2 11.1 %collective-permute-start.9 = (f32[2,288,128]{2,1,0:T(8,128)S(1)}, f32[2,288,128]{2,1,0:T(8,128)S(1)}, u32[]{:S(2)}, u32[]{:S(2)}) collective-permute-start(f32[2,288,128]{2,1,0:T(8,128)S(1)} %get-tuple-element.50), channel_id=1, source_target_pairs={{1,0},{2,1},{3,2},{7,3},{6,7},{5,6},{4,5},{8,4},{9,8},{10,9},{11,1... | collective-permute-start | bytes 884744 | tf_op jit(solution)/shard_map/ppermute | solution.py:425
  47.5 17.6 %collective-permute-start.13 = (f32[36,8,128]{2,1,0:T(8,128)}, f32[36,8,128]{2,1,0:T(8,128)S(1)}, u32[]{:S(2)}, u32[]{:S(2)}) collective-permute-start(f32[36,8,128]{2,1,0:T(8,128)} %get-tuple-element.58), channel_id=1, source_target_pairs={{0,3},{1,0},{2,1},{3,2},{4,7},{5,4},{6,5},{7,6},{8,11},{9,8},{10,9... | collective-permute-start | bytes 442376 | tf_op jit(solution)/shard_map/ppermute | solution.py:377
  52.0 16.4 %collective-permute-start.14 = (f32[36,8,128]{2,1,0:T(8,128)}, f32[36,8,128]{2,1,0:T(8,128)S(1)}, u32[]{:S(2)}, u32[]{:S(2)}) collective-permute-start(f32[36,8,128]{2,1,0:T(8,128)} %get-tuple-element.59), channel_id=1, source_target_pairs={{0,2},{1,3},{2,0},{3,1},{4,6},{5,7},{6,4},{7,5},{8,10},{9,11},{10,... | collective-permute-start | bytes 442376 | tf_op jit(solution)/shard_map/ppermute | solution.py:377
  52.1 16.2 %collective-permute-start.15 = (f32[36,8,128]{2,1,0:T(8,128)S(1)}, f32[36,8,128]{2,1,0:T(8,128)S(1)}, u32[]{:S(2)}, u32[]{:S(2)}) collective-permute-start(f32[36,8,128]{2,1,0:T(8,128)S(1)} %get-tuple-element.60), channel_id=1, source_target_pairs={{0,1},{1,2},{2,3},{3,0},{4,5},{5,6},{6,7},{7,4},{8,9},{9,10},{10,1... | collective-permute-start | bytes 442376 | tf_op jit(solution)/shard_map/ppermute | solution.py:377
  68.4 15.7 %collective-permute-start.16 = (f32[72,8,128]{2,1,0:T(8,128)S(1)}, f32[72,8,128]{2,1,0:T(8,128)S(1)}, u32[]{:S(2)}, u32[]{:S(2)}) collective-permute-start(f32[72,8,128]{2,1,0:T(8,128)S(1)} %get-tuple-element.61), channel_id=1, source_target_pairs={{0,1},{1,2},{2,3},{3,0},{4,5},{5,6},{6,7},{7,4},{8,9},{9,10},{10,1... | collective-permute-start | bytes 884744 | tf_op jit(solution)/shard_map/ppermute | solution.py:377
  69.3 27.7 %collective-permute-start.20 = (f32[72,8,128]{2,1,0:T(8,128)S(1)}, f32[72,8,128]{2,1,0:T(8,128)S(1)}, u32[]{:S(2)}, u32[]{:S(2)}) collective-permute-start(f32[72,8,128]{2,1,0:T(8,128)S(1)} %get-tuple-element.68), channel_id=1, source_target_pairs={{0,3},{1,0},{2,1},{3,2},{4,7},{5,4},{6,5},{7,6},{8,11},{9,8},{10,9... | collective-permute-start | bytes 884744 | tf_op jit(solution)/shard_map/ppermute | solution.py:377
  72.2 24.8 %collective-permute-start.21 = (f32[72,8,128]{2,1,0:T(8,128)S(1)}, f32[72,8,128]{2,1,0:T(8,128)S(1)}, u32[]{:S(2)}, u32[]{:S(2)}) collective-permute-start(f32[72,8,128]{2,1,0:T(8,128)S(1)} %get-tuple-element.69), channel_id=1, source_target_pairs={{0,2},{1,3},{2,0},{3,1},{4,6},{5,7},{6,4},{7,5},{8,10},{9,11},{10,... | collective-permute-start | bytes 884744 | tf_op jit(solution)/shard_map/ppermute | solution.py:377
  73.4 1.4 %collective-permute-start.10 = (f32[32,128]{1,0:T(8,128)S(1)}, f32[32,128]{1,0:T(8,128)S(1)}, u32[]{:S(2)}, u32[]{:S(2)}) collective-permute-start(f32[32,128]{1,0:T(8,128)S(1)} %get-tuple-element.52), channel_id=1, source_target_pairs={{0,4},{4,0},{8,12},{12,8},{16,20},{20,16},{24,28},{28,24},{1,5},{5... | collective-permute-start | bytes 49160 | tf_op jit(solution)/shard_map/ppermute | solution.py:337
  74.9 3.7 %collective-permute-start.11 = (f32[32,128]{1,0:T(8,128)S(1)}, f32[32,128]{1,0:T(8,128)S(1)}, u32[]{:S(2)}, u32[]{:S(2)}) collective-permute-start(f32[32,128]{1,0:T(8,128)S(1)} %add.60), channel_id=1, source_target_pairs={{0,8},{4,12},{8,0},{12,4},{16,24},{20,28},{24,16},{28,20},{1,9},{5... | collective-permute-start | bytes 49160 | tf_op jit(solution)/shard_map/ppermute | solution.py:337
  78.6 3.7 %collective-permute-start.12 = (f32[32,128]{1,0:T(8,128)S(1)}, f32[32,128]{1,0:T(8,128)S(1)}, u32[]{:S(2)}, u32[]{:S(2)}) collective-permute-start(f32[32,128]{1,0:T(8,128)S(1)} %add.61), channel_id=1, source_target_pairs={{0,16},{4,20},{8,24},{12,28},{16,0},{20,4},{24,8},{28,12},{1,17},{... | collective-permute-start | bytes 49160 | tf_op jit(solution)/shard_map/ppermute | solution.py:337
  82.4 14.7 %collective-permute-start.18 = (f32[32,128]{1,0:T(8,128)S(1)}, f32[32,128]{1,0:T(8,128)S(1)}, u32[]{:S(2)}, u32[]{:S(2)}) collective-permute-start(f32[32,128]{1,0:T(8,128)S(1)} %add.62.refs_0_), channel_id=1, source_target_pairs={{0,2},{1,3},{2,0},{3,1},{4,6},{5,7},{6,4},{7,5},{8,10},{9,11},{10,... | collective-permute-start | bytes 49160 | tf_op jit(solution)/shard_map/ppermute | solution.py:377
  83.8 13.2 %collective-permute-start.19 = (f32[32,128]{1,0:T(8,128)S(1)}, f32[32,128]{1,0:T(8,128)S(1)}, u32[]{:S(2)}, u32[]{:S(2)}) collective-permute-start(f32[32,128]{1,0:T(8,128)S(1)} %add.62.refs_0_), channel_id=1, source_target_pairs={{0,1},{1,2},{2,3},{3,0},{4,5},{5,6},{6,7},{7,4},{8,9},{9,10},{10,1... | collective-permute-start | bytes 49160 | tf_op jit(solution)/shard_map/ppermute | solution.py:377
  84.1 13.2 %collective-permute-start.17 = (f32[32,128]{1,0:T(8,128)S(1)}, f32[32,128]{1,0:T(8,128)S(1)}, u32[]{:S(2)}, u32[]{:S(2)}) collective-permute-start(f32[32,128]{1,0:T(8,128)S(1)} %add.62.refs_0_), channel_id=1, source_target_pairs={{0,3},{1,0},{2,1},{3,2},{4,7},{5,4},{6,5},{7,6},{8,11},{9,8},{10,9... | collective-permute-start | bytes 49160 | tf_op jit(solution)/shard_map/ppermute | solution.py:377
  (4 other events, 17.1 us)

commit v5 on v4

--- a/solution.py
+++ b/solution.py
@@ -13,6 +13,7 @@
 SUB = 8
 LANES = 128
 UNROLL = 12
+SPARE_ROWS = 3
 PARAMS = pltpu.CompilerParams(vmem_limit_bytes=12 * 1024 * 1024)
 
 
@@ -368,6 +369,9 @@
 
     offsets = [columns * chunk(i, (z + d) % n) for d in range(n)]
 
+    def longer(count):
+        return [(count + (d == n // 2), SUB, lanes) for d in range(n)]
+
     def sent(parts, way, after=None):
         out = [parts[0]]
         for d in range(1, n):
@@ -383,9 +387,9 @@
     offsets_array = jnp.stack(offsets).astype(jnp.int32)
 
     f_rows = max(rows, edge[0] // SUB + 1)
-    f_shapes = [(f_rows + (d != n // 2), SUB, lanes) for d in range(n)]
+    f_shapes = [(f_rows, SUB, lanes)] * n
     cut = functools.partial(cut_kernel, n, columns, rows)
-    x_parts = call(cut, [offsets_array], [start_guess, multi_index.T], [(rows + 1 + (d == n // 2), SUB, lanes) for d in range(n)])
+    x_parts = call(cut, [offsets_array], [start_guess, multi_index.T], longer(rows + 1))
     x_parts = sent(list(x_parts), outward)
     ranks = jnp.concatenate([p[rows, 0, :here] for p in x_parts]).astype(jnp.int32)
     f_parts = sent(list(call(cut, [offsets_array], [forcing], f_shapes)), outward)
@@ -424,16 +428,20 @@
     v0_before = lax.ppermute(v0_last, both, line)
     v0_after = lax.ppermute(v0_first, both, back_line)
     v0_home = sent(v0_parts, homeward)
+    table_rows = -(-spaces * n // SUB) * SUB
     *krylov, table = call(
         functools.partial(krylov_kernel, n, columns, edges),
         [ranks, (i * n + z).astype(jnp.int32)[None]],
         [v0, v0_before, v0_after, coef, inside],
-        [(2 * rows, SUB, lanes)] * n + [(-(-spaces * n // SUB) * SUB, lanes)],
+        [(2 * rows, SUB, lanes)] * n + [(SPARE_ROWS + table_rows, lanes)],
         [field, field, field, diff],
     )
-    krylov, v0_home = lax.optimization_barrier((krylov, v0_home))
+    far = n // 2
+    near_home = [v0_home[d] for d in range(1, n) if d != far]
+    krylov, near_home = lax.optimization_barrier((krylov, near_home))
     krylov_home = sent(krylov, homeward)
-    table = butterfly(table, "space")
+    table, v0_home[far] = lax.optimization_barrier((table, v0_home[far]))
+    table = butterfly(table, "space")[:table_rows]
     tables = sent([table] * n, homeward, [None, krylov_home[n - 1]] + [None] * (n - 2))
     return call(
         functools.partial(finish_kernel, n, columns),

time: 100 us -> 98.6 us (0.986)
    ppermute x1, starting transfers between devices: 2.95 us -> 11.2 us  [per_device(): x_before = lax.ppermute(x_last, both, line)]
    ppermute x15, starting transfers between devices: 37 us -> 29 us  [sent(): out.append(lax.ppermute(value, 'chaos', way(d)))]
    ppermute x15, waiting for transfers between devices: 13 us -> 9.92 us  [sent(): out.append(lax.ppermute(value, 'chaos', way(d)))]
    ppermute x1, waiting for transfers between devices: 3.19 us -> 5.91 us  [per_device(): v0_after = lax.ppermute(v0_first, both, back_line)]
    ppermute x1, waiting for transfers between devices: 4.99 us -> 3.3 us  [per_device(): x_after = lax.ppermute(x_first, both, back_line)]
    ppermute x1, waiting for transfers between devices: 0.01 us -> 1.23 us  [per_device(): v0_before = lax.ppermute(v0_last, both, line)]
    ppermute x1, waiting for transfers between devices: 1.47 us -> 2.57 us  [per_device(): x_before = lax.ppermute(x_last, both, line)]
  transfers between devices with their start and end apart: 22 -> 22, of which waited for: 10 -> 9; matrix products, arithmetic and copies ran while one was open for 0% -> 0% of each run, Pallas kernels for 12% -> 12%
where the time goes in v5:
time: 98.6 us; the launch traced here: 98.3 us
  starting transfers between devices  49.6 us (50%)
  waiting for transfers between devices  27.8 us (28%)
  Pallas kernels  16.9 us (17%)
  local copies, waits for them, and re-layouts  2.92 us (3%)
    ppermute x15, starting transfers between devices, sent(): out.append(lax.ppermute(value, 'chaos', way(d)))  29 us
    pallas_call x7, Pallas kernels, call(): pl.pallas_call(kernel, in_specs=[pl.BlockSpec(memory_space=pltpu.SMEM)] *...  16.9 us
    ppermute x1, starting transfers between devices, per_device(): x_before = lax.ppermute(x_last, both, line)  11.2 us
    ppermute x15, waiting for transfers between devices, sent(): out.append(lax.ppermute(value, 'chaos', way(d)))  9.92 us
    ppermute x1, waiting for transfers between devices, per_device(): v0_after = lax.ppermute(v0_first, both, back_line)  5.91 us
    ppermute x3, waiting for transfers between devices, butterfly(): lax.ppermute(value, axis, [(i, i ^ bit) for i in range(count)])  4.88 us
    ppermute x1, starting transfers between devices, per_device(): v0_before = lax.ppermute(v0_last, both, line)  4.02 us
    ppermute x1, waiting for transfers between devices, per_device(): x_after = lax.ppermute(x_first, both, back_line)  3.3 us
  transfers between devices with their start and end apart: 22, of which 9 were waited for; matrix products, arithmetic and copies ran while one was open for 0% of the time, Pallas kernels for 12%

profile of v5, /device:TPU:0, one launch (start us, length us, event | category | flops | bytes accessed | tf_op | source)
XLA Modules:
  0.0 98.3 jit_solution(129300716514945721)
XLA Ops:
  3.2 4.1 %collective-permute-start.1 = (f32[38,8,128]{2,1,0:T(8,128)S(1)}, f32[38,8,128]{2,1,0:T(8,128)S(1)}, u32[]{:S(2)}, u32[]{:S(2)}) collective-permute-start(f32[38,8,128]{2,1,0:T(8,128)S(1)} %get-tuple-element.36), channel_id=1, source_target_pairs={{0,2},{1,3},{2,0},{3,1},{4,6},{5,7},{6,4},{7,5},{8,10},{9,11},{10,... | collective-permute-start | bytes 466952 | tf_op jit(solution)/shard_map/ppermute | solution.py:381
  7.3 1.3 %collective-permute-start.2 = (f32[37,8,128]{2,1,0:T(8,128)S(1)}, f32[37,8,128]{2,1,0:T(8,128)S(1)}, u32[]{:S(2)}, u32[]{:S(2)}) collective-permute-start(f32[37,8,128]{2,1,0:T(8,128)S(1)} %get-tuple-element.37), channel_id=1, source_target_pairs={{0,3},{1,0},{2,1},{3,2},{4,7},{5,4},{6,5},{7,6},{8,11},{9,8},{10,9... | collective-permute-start | bytes 454664 | tf_op jit(solution)/shard_map/ppermute | solution.py:381
  11.1 1.6 %collective-permute-start.5 = (f32[39,8,128]{2,1,0:T(8,128)S(1)}, f32[39,8,128]{2,1,0:T(8,128)S(1)}, u32[]{:S(2)}, u32[]{:S(2)}) collective-permute-start(f32[39,8,128]{2,1,0:T(8,128)S(1)} %get-tuple-element.43), channel_id=1, source_target_pairs={{0,1},{1,2},{2,3},{3,0},{4,5},{5,6},{6,7},{7,4},{8,9},{9,10},{10,1... | collective-permute-start | bytes 479240 | tf_op jit(solution)/shard_map/ppermute | solution.py:381
  12.7 2.1 %collective-permute-start.6 = (f32[39,8,128]{2,1,0:T(8,128)S(1)}, f32[39,8,128]{2,1,0:T(8,128)S(1)}, u32[]{:S(2)}, u32[]{:S(2)}) collective-permute-start(f32[39,8,128]{2,1,0:T(8,128)S(1)} %get-tuple-element.44), channel_id=1, source_target_pairs={{0,2},{1,3},{2,0},{3,1},{4,6},{5,7},{6,4},{7,5},{8,10},{9,11},{10,... | collective-permute-start | bytes 479240 | tf_op jit(solution)/shard_map/ppermute | solution.py:381
  15.1 4.3 %collective-permute-start.7 = (f32[39,8,128]{2,1,0:T(8,128)S(1)}, f32[39,8,128]{2,1,0:T(8,128)S(1)}, u32[]{:S(2)}, u32[]{:S(2)}) collective-permute-start(f32[39,8,128]{2,1,0:T(8,128)S(1)} %get-tuple-element.45), channel_id=1, source_target_pairs={{0,3},{1,0},{2,1},{3,2},{4,7},{5,4},{6,5},{7,6},{8,11},{9,8},{10,9... | collective-permute-start | bytes 479240 | tf_op jit(solution)/shard_map/ppermute | solution.py:381
  21.4 11.2 %collective-permute-start.3 = (f32[308,128]{1,0:T(8,128)S(1)}, f32[308,128]{1,0:T(8,128)S(1)}, u32[]{:S(2)}, u32[]{:S(2)}) collective-permute-start(f32[308,128]{1,0:T(8,128)S(1)} %get-tuple-element.39), channel_id=1, source_target_pairs={{0,1},{1,2},{2,3},{3,7},{7,6},{6,5},{5,4},{4,8},{8,9},{9,10},{10,1... | collective-permute-start | bytes 473096 | tf_op jit(solution)/shard_map/ppermute | solution.py:413
  33.9 2.6 %collective-permute-done.3.before_ref = f32[308,128]{1,0:T(8,128)S(1)} collective-permute-done((f32[308,128]{1,0:T(8,128)S(1)}, f32[308,128]{1,0:T(8,128)S(1)}, u32[]{:S(2)}, u32[]{:S(2)}) %collective-permute-start.3) | collective-permute-done | bytes 157728 | tf_op jit(solution)/shard_map/ppermute | solution.py:413
  36.5 3.3 %collective-permute-done.4.after_ref = f32[308,128]{1,0:T(8,128)S(1)} collective-permute-done((f32[308,128]{1,0:T(8,128)S(1)}, f32[308,128]{1,0:T(8,128)S(1)}, u32[]{:S(2)}, u32[]{:S(2)}) %collective-permute-start.4) | collective-permute-done | bytes 157728 | tf_op jit(solution)/shard_map/ppermute | solution.py:414
  39.8 2.7 %shard_map.70 = (f32[288,8,128]{2,1,0:T(8,128)S(1)}, f32[11,8,128]{2,1,0:T(8,128)S(1)}) custom-call(f32[288,8,128]{2,1,0:T(8,128)S(1)} %get-tuple-element.38.x_ref, f32[308,128]{1,0:T(8,128)S(1)} %collective-permute-done.3.before_ref, f32[308,128]{1,0:T(8,128)S(1)} %collective-permute-done.4.after_ref, f32[11,8,128]{2,1,0:T(8,128)S(1)} %pad.4.coef_ref.own_ref), custom_call_target="tpu_custom_call" | custom-call | tf_op jit(solution)/shard_map/pallas_call | solution.py:324
  42.5 2.1 %shard_map.72 = (f32[36,8,128]{2,1,0:T(8,128)S(1)}, f32[36,8,128]{2,1,0:T(8,128)}, f32[36,8,128]{2,1,0:T(8,128)S(1)}, f32[36,8,128]{2,1,0:T(8,128)}, f32[288,8,1...) custom-call(s32[288]{0:T(512)S(1)} %maximum_convert_fusion.ranks_ref, ...), custom_call_target="tpu_custom_call" | custom-call | tf_op jit(solution)/shard_map/pallas_call | solution.py:324
  44.5 4.0 %collective-permute-start.8 = (f32[2,288,128]{2,1,0:T(8,128)}, f32[2,288,128]{2,1,0:T(8,128)S(1)}, u32[]{:S(2)}, u32[]{:S(2)}) collective-permute-start(f32[2,288,128]{2,1,0:T(8,128)} %get-tuple-element.47), channel_id=1, source_target_pairs={{0,1},{1,2},{2,3},{3,7},{7,6},{6,5},{5,4},{4,8},{8,9},{9,10},{10,1... | collective-permute-start | bytes 884744 | tf_op jit(solution)/shard_map/ppermute | solution.py:428
  49.9 2.7 %collective-permute-start.14 = (f32[36,8,128]{2,1,0:T(8,128)}, f32[36,8,128]{2,1,0:T(8,128)S(1)}, u32[]{:S(2)}, u32[]{:S(2)}) collective-permute-start(f32[36,8,128]{2,1,0:T(8,128)} %get-tuple-element.57), channel_id=1, source_target_pairs={{0,3},{1,0},{2,1},{3,2},{4,7},{5,4},{6,5},{7,6},{8,11},{9,8},{10,9... | collective-permute-start | bytes 442376 | tf_op jit(solution)/shard_map/ppermute | solution.py:381
  52.6 1.4 %collective-permute-start.10 = (f32[36,8,128]{2,1,0:T(8,128)S(1)}, f32[36,8,128]{2,1,0:T(8,128)S(1)}, u32[]{:S(2)}, u32[]{:S(2)}) collective-permute-start(f32[36,8,128]{2,1,0:T(8,128)S(1)} %get-tuple-element.51), channel_id=1, source_target_pairs={{0,2},{1,3},{2,0},{3,1},{4,6},{5,7},{6,4},{7,5},{8,10},{9,11},{10,... | collective-permute-start | bytes 442376 | tf_op jit(solution)/shard_map/ppermute | solution.py:381
  55.3 5.9 %collective-permute-done.9.after_ref = f32[2,288,128]{2,1,0:T(8,128)S(1)} collective-permute-done((f32[2,288,128]{2,1,0:T(8,128)S(1)}, f32[2,288,128]{2,1,0:T(8,128)S(1)}, u32[]{:S(2)}, u32[]{:S(2)}) %collective-permute-start.9) | collective-permute-done | bytes 294944 | tf_op jit(solution)/shard_map/ppermute | solution.py:429
  61.3 7.7 %shard_map.73 = (f32[72,8,128]{2,1,0:T(8,128)S(1)}, f32[72,8,128]{2,1,0:T(8,128)S(1)}, f32[72,8,128]{2,1,0:T(8,128)S(1)}, f32[72,8,128]{2,1,0:T(8,128)S(1)}, f32[35,128]{1,0:T(8,128)S(1)}) custom-call(s32[288]{0:T(512)S(1)} %maximum_convert_fusion.ranks_ref, s32[1]{0:T(128)} %bitcast.9.place_ref, f32[288,8,128]{2,1,0:T(8,128)S(1)} %get-tuple-element.46.v_ref, ...), custom_call_target="tpu_custom_call" | custom-call | tf_op jit(solution)/shard_map/pallas_call | solution.py:324
  69.8 3.0 %collective-permute-start.20 = (f32[72,8,128]{2,1,0:T(8,128)S(1)}, f32[72,8,128]{2,1,0:T(8,128)S(1)}, u32[]{:S(2)}, u32[]{:S(2)}) collective-permute-start(f32[72,8,128]{2,1,0:T(8,128)S(1)} %get-tuple-element.64), channel_id=1, source_target_pairs={{0,3},{1,0},{2,1},{3,2},{4,7},{5,4},{6,5},{7,6},{8,11},{9,8},{10,9... | collective-permute-start | bytes 884744 | tf_op jit(solution)/shard_map/ppermute | solution.py:381
  72.9 1.4 %collective-permute-start.12 = (f32[35,128]{1,0:T(8,128)S(1)}, f32[35,128]{1,0:T(8,128)S(1)}, u32[]{:S(2)}, u32[]{:S(2)}) collective-permute-start(f32[35,128]{1,0:T(8,128)S(1)} %add.60), channel_id=1, source_target_pairs={{0,8},{4,12},{8,0},{12,4},{16,24},{20,28},{24,16},{28,20},{1,9},{5... | collective-permute-start | bytes 53768 | tf_op jit(solution)/shard_map/ppermute | solution.py:338
  74.3 2.5 %collective-permute-done.12 = f32[35,128]{1,0:T(8,128)S(1)} collective-permute-done((f32[35,128]{1,0:T(8,128)S(1)}, f32[35,128]{1,0:T(8,128)S(1)}, u32[]{:S(2)}, u32[]{:S(2)}) %collective-permute-start.12) | collective-permute-done | bytes 17952 | tf_op jit(solution)/shard_map/ppermute | solution.py:338
  76.7 1.4 %collective-permute-start.13 = (f32[35,128]{1,0:T(8,128)S(1)}, f32[35,128]{1,0:T(8,128)S(1)}, u32[]{:S(2)}, u32[]{:S(2)}) collective-permute-start(f32[35,128]{1,0:T(8,128)S(1)} %add.61), channel_id=1, source_target_pairs={{0,16},{4,20},{8,24},{12,28},{16,0},{20,4},{24,8},{28,12},{1,17},{... | collective-permute-start | bytes 53768 | tf_op jit(solution)/shard_map/ppermute | solution.py:338
  78.1 2.4 %collective-permute-done.13 = f32[35,128]{1,0:T(8,128)S(1)} collective-permute-done((f32[35,128]{1,0:T(8,128)S(1)}, f32[35,128]{1,0:T(8,128)S(1)}, u32[]{:S(2)}, u32[]{:S(2)}) %collective-permute-start.13) | collective-permute-done | bytes 17952 | tf_op jit(solution)/shard_map/ppermute | solution.py:338
  80.5 2.9 %collective-permute-start.18 = (f32[32,128]{1,0:T(8,128)S(1)}, f32[32,128]{1,0:T(8,128)S(1)}, u32[]{:S(2)}, u32[]{:S(2)}) collective-permute-start(f32[32,128]{1,0:T(8,128)S(1)} %slice_add_fusion.refs_0_), channel_id=1, source_target_pairs={{0,2},{1,3},{2,0},{3,1},{4,6},{5,7},{6,4},{7,5},{8,10},{9,11},{10,... | collective-permute-start | bytes 49160 | tf_op jit(solution)/shard_map/ppermute | solution.py:381
  83.4 3.8 %collective-permute-start.17 = (f32[32,128]{1,0:T(8,128)S(1)}, f32[32,128]{1,0:T(8,128)S(1)}, u32[]{:S(2)}, u32[]{:S(2)}) collective-permute-start(f32[32,128]{1,0:T(8,128)S(1)} %slice_add_fusion.refs_0_), channel_id=1, source_target_pairs={{0,3},{1,0},{2,1},{3,2},{4,7},{5,4},{6,5},{7,6},{8,11},{9,8},{10,9... | collective-permute-start | bytes 49160 | tf_op jit(solution)/shard_map/ppermute | solution.py:381
  87.3 9.0 %collective-permute-done.18.refs_2_ = f32[32,128]{1,0:T(8,128)S(1)} collective-permute-done((f32[32,128]{1,0:T(8,128)S(1)}, f32[32,128]{1,0:T(8,128)S(1)}, u32[]{:S(2)}, u32[]{:S(2)}) %collective-permute-start.18) | collective-permute-done | bytes 16416 | tf_op jit(solution)/shard_map/ppermute | solution.py:381
  96.2 2.0 %shard_map.74 = (f32[72,16,128]{2,1,0:T(8,128)}, f32[72,16,128]{2,1,0:T(8,128)}) custom-call(s32[4]{0:T(128)S(1)} %pad_add_fusion.offsets_ref, f32[72,16,128]{2,1,0:T(8,128)S(1)} %copy-done.1, f32[32,128]{1,0:T(8,128)S(1)} %slice_add_fusion.refs_0_, f32[32,128]{1,0:T(8,128)S(1)} %collective-permute-done.17.refs_1_, ...), custom_call_target="tpu_custom_call" | custom-call | tf_op jit(solution)/shard_map/pallas_call | solution.py:324
  (52 shorter events, 11.9 us)
Async XLA Ops:
  0.6 14.2 %copy-start.5 = (f32[16,128]{1,0:T(8,128)S(1)}, f32[16,128]{1,0:T(8,128)}, u32[]{:S(2)}) copy-start(f32[16,128]{1,0:T(8,128)} %param.8) | copy-start | bytes 24580
  3.2 16.9 %collective-permute-start.1 = (f32[38,8,128]{2,1,0:T(8,128)S(1)}, f32[38,8,128]{2,1,0:T(8,128)S(1)}, u32[]{:S(2)}, u32[]{:S(2)}) collective-permute-start(f32[38,8,128]{2,1,0:T(8,128)S(1)} %get-tuple-element.36), channel_id=1, source_target_pairs={{0,2},{1,3},{2,0},{3,1},{4,6},{5,7},{6,4},{7,5},{8,10},{9,11},{10,... | collective-permute-start | bytes 466952 | tf_op jit(solution)/shard_map/ppermute | solution.py:381
  7.3 7.7 %collective-permute-start.2 = (f32[37,8,128]{2,1,0:T(8,128)S(1)}, f32[37,8,128]{2,1,0:T(8,128)S(1)}, u32[]{:S(2)}, u32[]{:S(2)}) collective-permute-start(f32[37,8,128]{2,1,0:T(8,128)S(1)} %get-tuple-element.37), channel_id=1, source_target_pairs={{0,3},{1,0},{2,1},{3,2},{4,7},{5,4},{6,5},{7,6},{8,11},{9,8},{10,9... | collective-permute-start | bytes 454664 | tf_op jit(solution)/shard_map/ppermute | solution.py:381
  8.7 11.5 %collective-permute-start = (f32[37,8,128]{2,1,0:T(8,128)S(1)}, f32[37,8,128]{2,1,0:T(8,128)S(1)}, u32[]{:S(2)}, u32[]{:S(2)}) collective-permute-start(f32[37,8,128]{2,1,0:T(8,128)S(1)} %get-tuple-element.35), channel_id=1, source_target_pairs={{0,1},{1,2},{2,3},{3,0},{4,5},{5,6},{6,7},{7,4},{8,9},{9,10},{10,1... | collective-permute-start | bytes 454664 | tf_op jit(solution)/shard_map/ppermute | solution.py:381
  11.1 31.4 %collective-permute-start.5 = (f32[39,8,128]{2,1,0:T(8,128)S(1)}, f32[39,8,128]{2,1,0:T(8,128)S(1)}, u32[]{:S(2)}, u32[]{:S(2)}) collective-permute-start(f32[39,8,128]{2,1,0:T(8,128)S(1)} %get-tuple-element.43), channel_id=1, source_target_pairs={{0,1},{1,2},{2,3},{3,0},{4,5},{5,6},{6,7},{7,4},{8,9},{9,10},{10,1... | collective-permute-start | bytes 479240 | tf_op jit(solution)/shard_map/ppermute | solution.py:381
  12.7 29.8 %collective-permute-start.6 = (f32[39,8,128]{2,1,0:T(8,128)S(1)}, f32[39,8,128]{2,1,0:T(8,128)S(1)}, u32[]{:S(2)}, u32[]{:S(2)}) collective-permute-start(f32[39,8,128]{2,1,0:T(8,128)S(1)} %get-tuple-element.44), channel_id=1, source_target_pairs={{0,2},{1,3},{2,0},{3,1},{4,6},{5,7},{6,4},{7,5},{8,10},{9,11},{10,... | collective-permute-start | bytes 479240 | tf_op jit(solution)/shard_map/ppermute | solution.py:381
  15.1 27.4 %collective-permute-start.7 = (f32[39,8,128]{2,1,0:T(8,128)S(1)}, f32[39,8,128]{2,1,0:T(8,128)S(1)}, u32[]{:S(2)}, u32[]{:S(2)}) collective-permute-start(f32[39,8,128]{2,1,0:T(8,128)S(1)} %get-tuple-element.45), channel_id=1, source_target_pairs={{0,3},{1,0},{2,1},{3,2},{4,7},{5,4},{6,5},{7,6},{8,11},{9,8},{10,9... | collective-permute-start | bytes 479240 | tf_op jit(solution)/shard_map/ppermute | solution.py:381
  21.4 15.1 %collective-permute-start.3 = (f32[308,128]{1,0:T(8,128)S(1)}, f32[308,128]{1,0:T(8,128)S(1)}, u32[]{:S(2)}, u32[]{:S(2)}) collective-permute-start(f32[308,128]{1,0:T(8,128)S(1)} %get-tuple-element.39), channel_id=1, source_target_pairs={{0,1},{1,2},{2,3},{3,7},{7,6},{6,5},{5,4},{4,8},{8,9},{9,10},{10,1... | collective-permute-start | bytes 473096 | tf_op jit(solution)/shard_map/ppermute | solution.py:413
  32.6 7.2 %collective-permute-start.4 = (f32[308,128]{1,0:T(8,128)S(1)}, f32[308,128]{1,0:T(8,128)S(1)}, u32[]{:S(2)}, u32[]{:S(2)}) collective-permute-start(f32[308,128]{1,0:T(8,128)S(1)} %get-tuple-element.40), channel_id=1, source_target_pairs={{1,0},{2,1},{3,2},{7,3},{6,7},{5,6},{4,5},{8,4},{9,8},{10,9},{11,1... | collective-permute-start | bytes 473096 | tf_op jit(solution)/shard_map/ppermute | solution.py:414
  44.5 51.7 %copy-start.1 = (f32[72,16,128]{2,1,0:T(8,128)S(1)}, f32[72,16,128]{2,1,0:T(8,128)}, u32[]{:S(2)}) copy-start(f32[72,16,128]{2,1,0:T(8,128)} %x_ref.1) | copy-start | bytes 1769476
  44.5 10.7 %collective-permute-start.8 = (f32[2,288,128]{2,1,0:T(8,128)}, f32[2,288,128]{2,1,0:T(8,128)S(1)}, u32[]{:S(2)}, u32[]{:S(2)}) collective-permute-start(f32[2,288,128]{2,1,0:T(8,128)} %get-tuple-element.47), channel_id=1, source_target_pairs={{0,1},{1,2},{2,3},{3,7},{7,6},{6,5},{5,4},{4,8},{8,9},{9,10},{10,1... | collective-permute-start | bytes 884744 | tf_op jit(solution)/shard_map/ppermute | solution.py:428
  48.6 12.6 %collective-permute-start.9 = (f32[2,288,128]{2,1,0:T(8,128)S(1)}, f32[2,288,128]{2,1,0:T(8,128)S(1)}, u32[]{:S(2)}, u32[]{:S(2)}) collective-permute-start(f32[2,288,128]{2,1,0:T(8,128)S(1)} %get-tuple-element.48), channel_id=1, source_target_pairs={{1,0},{2,1},{3,2},{7,3},{6,7},{5,6},{4,5},{8,4},{9,8},{10,9},{11,1... | collective-permute-start | bytes 884744 | tf_op jit(solution)/shard_map/ppermute | solution.py:429
  49.9 19.1 %collective-permute-start.14 = (f32[36,8,128]{2,1,0:T(8,128)}, f32[36,8,128]{2,1,0:T(8,128)S(1)}, u32[]{:S(2)}, u32[]{:S(2)}) collective-permute-start(f32[36,8,128]{2,1,0:T(8,128)} %get-tuple-element.57), channel_id=1, source_target_pairs={{0,3},{1,0},{2,1},{3,2},{4,7},{5,4},{6,5},{7,6},{8,11},{9,8},{10,9... | collective-permute-start | bytes 442376 | tf_op jit(solution)/shard_map/ppermute | solution.py:381
  52.6 16.4 %collective-permute-start.15 = (f32[36,8,128]{2,1,0:T(8,128)}, f32[36,8,128]{2,1,0:T(8,128)S(1)}, u32[]{:S(2)}, u32[]{:S(2)}) collective-permute-start(f32[36,8,128]{2,1,0:T(8,128)} %get-tuple-element.58), channel_id=1, source_target_pairs={{0,1},{1,2},{2,3},{3,0},{4,5},{5,6},{6,7},{7,4},{8,9},{9,10},{10,1... | collective-permute-start | bytes 442376 | tf_op jit(solution)/shard_map/ppermute | solution.py:381
  52.6 17.2 %collective-permute-start.10 = (f32[36,8,128]{2,1,0:T(8,128)S(1)}, f32[36,8,128]{2,1,0:T(8,128)S(1)}, u32[]{:S(2)}, u32[]{:S(2)}) collective-permute-start(f32[36,8,128]{2,1,0:T(8,128)S(1)} %get-tuple-element.51), channel_id=1, source_target_pairs={{0,2},{1,3},{2,0},{3,1},{4,6},{5,7},{6,4},{7,5},{8,10},{9,11},{10,... | collective-permute-start | bytes 442376 | tf_op jit(solution)/shard_map/ppermute | solution.py:381
  69.0 14.5 %collective-permute-start.16 = (f32[72,8,128]{2,1,0:T(8,128)S(1)}, f32[72,8,128]{2,1,0:T(8,128)S(1)}, u32[]{:S(2)}, u32[]{:S(2)}) collective-permute-start(f32[72,8,128]{2,1,0:T(8,128)S(1)} %get-tuple-element.59), channel_id=1, source_target_pairs={{0,1},{1,2},{2,3},{3,0},{4,5},{5,6},{6,7},{7,4},{8,9},{9,10},{10,1... | collective-permute-start | bytes 884744 | tf_op jit(solution)/shard_map/ppermute | solution.py:381
  69.8 3.0 %collective-permute-start.11 = (f32[35,128]{1,0:T(8,128)S(1)}, f32[35,128]{1,0:T(8,128)S(1)}, u32[]{:S(2)}, u32[]{:S(2)}) collective-permute-start(f32[35,128]{1,0:T(8,128)S(1)} %get-tuple-element.52), channel_id=1, source_target_pairs={{0,4},{4,0},{8,12},{12,8},{16,20},{20,16},{24,28},{28,24},{1,5},{5... | collective-permute-start | bytes 53768 | tf_op jit(solution)/shard_map/ppermute | solution.py:338
  69.8 26.4 %collective-permute-start.20 = (f32[72,8,128]{2,1,0:T(8,128)S(1)}, f32[72,8,128]{2,1,0:T(8,128)S(1)}, u32[]{:S(2)}, u32[]{:S(2)}) collective-permute-start(f32[72,8,128]{2,1,0:T(8,128)S(1)} %get-tuple-element.64), channel_id=1, source_target_pairs={{0,3},{1,0},{2,1},{3,2},{4,7},{5,4},{6,5},{7,6},{8,11},{9,8},{10,9... | collective-permute-start | bytes 884744 | tf_op jit(solution)/shard_map/ppermute | solution.py:381
  72.9 23.4 %collective-permute-start.21 = (f32[72,8,128]{2,1,0:T(8,128)S(1)}, f32[72,8,128]{2,1,0:T(8,128)S(1)}, u32[]{:S(2)}, u32[]{:S(2)}) collective-permute-start(f32[72,8,128]{2,1,0:T(8,128)S(1)} %get-tuple-element.65), channel_id=1, source_target_pairs={{0,2},{1,3},{2,0},{3,1},{4,6},{5,7},{6,4},{7,5},{8,10},{9,11},{10,... | collective-permute-start | bytes 884744 | tf_op jit(solution)/shard_map/ppermute | solution.py:381
  72.9 3.8 %collective-permute-start.12 = (f32[35,128]{1,0:T(8,128)S(1)}, f32[35,128]{1,0:T(8,128)S(1)}, u32[]{:S(2)}, u32[]{:S(2)}) collective-permute-start(f32[35,128]{1,0:T(8,128)S(1)} %add.60), channel_id=1, source_target_pairs={{0,8},{4,12},{8,0},{12,4},{16,24},{20,28},{24,16},{28,20},{1,9},{5... | collective-permute-start | bytes 53768 | tf_op jit(solution)/shard_map/ppermute | solution.py:338
  76.7 3.8 %collective-permute-start.13 = (f32[35,128]{1,0:T(8,128)S(1)}, f32[35,128]{1,0:T(8,128)S(1)}, u32[]{:S(2)}, u32[]{:S(2)}) collective-permute-start(f32[35,128]{1,0:T(8,128)S(1)} %add.61), channel_id=1, source_target_pairs={{0,16},{4,20},{8,24},{12,28},{16,0},{20,4},{24,8},{28,12},{1,17},{... | collective-permute-start | bytes 53768 | tf_op jit(solution)/shard_map/ppermute | solution.py:338
  80.5 15.7 %collective-permute-start.18 = (f32[32,128]{1,0:T(8,128)S(1)}, f32[32,128]{1,0:T(8,128)S(1)}, u32[]{:S(2)}, u32[]{:S(2)}) collective-permute-start(f32[32,128]{1,0:T(8,128)S(1)} %slice_add_fusion.refs_0_), channel_id=1, source_target_pairs={{0,2},{1,3},{2,0},{3,1},{4,6},{5,7},{6,4},{7,5},{8,10},{9,11},{10,... | collective-permute-start | bytes 49160 | tf_op jit(solution)/shard_map/ppermute | solution.py:381
  83.4 12.8 %collective-permute-start.19 = (f32[32,128]{1,0:T(8,128)S(1)}, f32[32,128]{1,0:T(8,128)S(1)}, u32[]{:S(2)}, u32[]{:S(2)}) collective-permute-start(f32[32,128]{1,0:T(8,128)S(1)} %slice_add_fusion.refs_0_), channel_id=1, source_target_pairs={{0,1},{1,2},{2,3},{3,0},{4,5},{5,6},{6,7},{7,4},{8,9},{9,10},{10,1... | collective-permute-start | bytes 49160 | tf_op jit(solution)/shard_map/ppermute | solution.py:381
  83.4 12.8 %collective-permute-start.17 = (f32[32,128]{1,0:T(8,128)S(1)}, f32[32,128]{1,0:T(8,128)S(1)}, u32[]{:S(2)}, u32[]{:S(2)}) collective-permute-start(f32[32,128]{1,0:T(8,128)S(1)} %slice_add_fusion.refs_0_), channel_id=1, source_target_pairs={{0,3},{1,0},{2,1},{3,2},{4,7},{5,4},{6,5},{7,6},{8,11},{9,8},{10,9... | collective-permute-start | bytes 49160 | tf_op jit(solution)/shard_map/ppermute | solution.py:381
  (4 other events, 17.0 us)

commit v6 on v5

--- a/solution.py
+++ b/solution.py
@@ -163,7 +163,8 @@
         last_ref[at : at + fields] = take_column(flat, columns - 2 + j, fields)
 
 
-def start_kernel(columns, edges, x_ref, before_ref, after_ref, own_ref, y_ref, coef_ref, u_ref, diff_ref):
+def start_kernel(n, columns, rows, edges, ranks_ref, x_ref, before_ref, after_ref, own_ref, *refs):
+    residual_refs, (coef_ref, u_ref, y_ref, diff_ref) = refs[:-4], refs[-4:]
     slots, fields, terms = x_ref.shape[0], own_ref.shape[0], len(edges)
     coef_ref[...] = own_ref[...]
     flat = coef_ref.reshape(fields * SUB, LANES)
@@ -181,9 +182,10 @@
         y_ref[s] = value
 
     apply_operator(u_ref, coef_ref, edges, store, diff_ref)
-
-
-def residual_kernel(n, columns, rows, ranks_ref, y_ref, *refs):
+    residual(n, columns, rows, ranks_ref, y_ref, *residual_refs)
+
+
+def residual(n, columns, rows, ranks_ref, y_ref, *refs):
     forcing, packed, (field_ref, first_ref, last_ref) = refs[:n], refs[n : 2 * n], refs[2 * n :]
     per = SUB // columns
     slots = field_ref.shape[0]
@@ -412,18 +414,12 @@
     )
     x_before = lax.ppermute(x_last, both, line)
     x_after = lax.ppermute(x_first, both, back_line)
-    image, coef = call(
-        functools.partial(start_kernel, columns, edges),
-        [],
-        [x, x_before, x_after, own_coef],
-        [field, fields],
-        [field, diff],
-    )
-    *v0_parts, v0, v0_first, v0_last = call(
-        functools.partial(residual_kernel, n, columns, rows),
+    *v0_parts, v0, v0_first, v0_last, coef = call(
+        functools.partial(start_kernel, n, columns, rows, edges),
         [ranks],
-        [image] + f_parts,
-        [part] * n + [field, (2, slots, lanes), (2, slots, lanes)],
+        [x, x_before, x_after, own_coef] + f_parts,
+        [part] * n + [field, (2, slots, lanes), (2, slots, lanes), fields],
+        [field, field, diff],
     )
     v0_before = lax.ppermute(v0_last, both, line)
     v0_after = lax.ppermute(v0_first, both, back_line)

time: 98.6 us -> 98.6 us (level)
    ppermute x1, waiting for transfers between devices: 2.57 us -> 1.4 us  [per_device(): x_before = lax.ppermute(x_last, both, line)]
    ppermute x15, waiting for transfers between devices: 9.92 us -> 11.1 us  [sent(): out.append(lax.ppermute(value, 'chaos', way(d)))]
    pallas_call x7 -> x6, Pallas kernels: 16.9 us -> 16.9 us  [call(): pl.pallas_call(kernel, in_specs=[pl.BlockSpec(memory_space=pltpu.SMEM)] *...]
  transfers between devices with their start and end apart: 22 -> 22, of which waited for: 9 -> 10; matrix products, arithmetic and copies ran while one was open for 0% -> 0% of each run, Pallas kernels for 12% -> 10%
where the time goes in v6:
time: 98.6 us; the launch traced here: 98.3 us
  starting transfers between devices  49.6 us (50%)
  waiting for transfers between devices  27.8 us (28%)
  Pallas kernels  16.9 us (17%)
  local copies, waits for them, and re-layouts  2.92 us (3%)
    ppermute x15, starting transfers between devices, sent(): out.append(lax.ppermute(value, 'chaos', way(d)))  29 us
    pallas_call x6, Pallas kernels, call(): pl.pallas_call(kernel, in_specs=[pl.BlockSpec(memory_space=pltpu.SMEM)] *...  16.9 us
    ppermute x1, starting transfers between devices, per_device(): x_before = lax.ppermute(x_last, both, line)  11.2 us
    ppermute x15, waiting for transfers between devices, sent(): out.append(lax.ppermute(value, 'chaos', way(d)))  11.1 us
    ppermute x1, waiting for transfers between devices, per_device(): v0_after = lax.ppermute(v0_first, both, back_line)  5.9 us
    ppermute x3, waiting for transfers between devices, butterfly(): lax.ppermute(value, axis, [(i, i ^ bit) for i in range(count)])  4.88 us
    ppermute x1, starting transfers between devices, per_device(): v0_before = lax.ppermute(v0_last, both, line)  4.03 us
    ppermute x1, waiting for transfers between devices, per_device(): x_after = lax.ppermute(x_first, both, back_line)  3.3 us
  transfers between devices with their start and end apart: 22, of which 10 were waited for; matrix products, arithmetic and copies ran while one was open for 0% of the time, Pallas kernels for 10%

profile of v6, /device:TPU:0, one launch (start us, length us, event | category | flops | bytes accessed | tf_op | source)
XLA Modules:
  0.0 98.3 jit_solution(7867455887732470861)
XLA Ops:
  3.2 4.1 %collective-permute-start.1 = (f32[38,8,128]{2,1,0:T(8,128)S(1)}, f32[38,8,128]{2,1,0:T(8,128)S(1)}, u32[]{:S(2)}, u32[]{:S(2)}) collective-permute-start(f32[38,8,128]{2,1,0:T(8,128)S(1)} %get-tuple-element.35), channel_id=1, source_target_pairs={{0,2},{1,3},{2,0},{3,1},{4,6},{5,7},{6,4},{7,5},{8,10},{9,11},{10,... | collective-permute-start | bytes 466952 | tf_op jit(solution)/shard_map/ppermute | solution.py:383
  7.3 1.3 %collective-permute-start.2 = (f32[37,8,128]{2,1,0:T(8,128)S(1)}, f32[37,8,128]{2,1,0:T(8,128)S(1)}, u32[]{:S(2)}, u32[]{:S(2)}) collective-permute-start(f32[37,8,128]{2,1,0:T(8,128)S(1)} %get-tuple-element.36), channel_id=1, source_target_pairs={{0,3},{1,0},{2,1},{3,2},{4,7},{5,4},{6,5},{7,6},{8,11},{9,8},{10,9... | collective-permute-start | bytes 454664 | tf_op jit(solution)/shard_map/ppermute | solution.py:383
  11.1 1.6 %collective-permute-start.5 = (f32[39,8,128]{2,1,0:T(8,128)S(1)}, f32[39,8,128]{2,1,0:T(8,128)S(1)}, u32[]{:S(2)}, u32[]{:S(2)}) collective-permute-start(f32[39,8,128]{2,1,0:T(8,128)S(1)} %get-tuple-element.41), channel_id=1, source_target_pairs={{0,1},{1,2},{2,3},{3,0},{4,5},{5,6},{6,7},{7,4},{8,9},{9,10},{10,1... | collective-permute-start | bytes 479240 | tf_op jit(solution)/shard_map/ppermute | solution.py:383
  12.7 2.1 %collective-permute-start.6 = (f32[39,8,128]{2,1,0:T(8,128)S(1)}, f32[39,8,128]{2,1,0:T(8,128)S(1)}, u32[]{:S(2)}, u32[]{:S(2)}) collective-permute-start(f32[39,8,128]{2,1,0:T(8,128)S(1)} %get-tuple-element.42), channel_id=1, source_target_pairs={{0,2},{1,3},{2,0},{3,1},{4,6},{5,7},{6,4},{7,5},{8,10},{9,11},{10,... | collective-permute-start | bytes 479240 | tf_op jit(solution)/shard_map/ppermute | solution.py:383
  15.1 4.3 %collective-permute-start.7 = (f32[39,8,128]{2,1,0:T(8,128)S(1)}, f32[39,8,128]{2,1,0:T(8,128)S(1)}, u32[]{:S(2)}, u32[]{:S(2)}) collective-permute-start(f32[39,8,128]{2,1,0:T(8,128)S(1)} %get-tuple-element.43), channel_id=1, source_target_pairs={{0,3},{1,0},{2,1},{3,2},{4,7},{5,4},{6,5},{7,6},{8,11},{9,8},{10,9... | collective-permute-start | bytes 479240 | tf_op jit(solution)/shard_map/ppermute | solution.py:383
  21.4 11.2 %collective-permute-start.3 = (f32[308,128]{1,0:T(8,128)S(1)}, f32[308,128]{1,0:T(8,128)S(1)}, u32[]{:S(2)}, u32[]{:S(2)}) collective-permute-start(f32[308,128]{1,0:T(8,128)S(1)} %get-tuple-element.38), channel_id=1, source_target_pairs={{0,1},{1,2},{2,3},{3,7},{7,6},{6,5},{5,4},{4,8},{8,9},{9,10},{10,1... | collective-permute-start | bytes 473096 | tf_op jit(solution)/shard_map/ppermute | solution.py:415
  32.6 1.3 %collective-permute-start.4 = (f32[308,128]{1,0:T(8,128)S(1)}, f32[308,128]{1,0:T(8,128)S(1)}, u32[]{:S(2)}, u32[]{:S(2)}) collective-permute-start(f32[308,128]{1,0:T(8,128)S(1)} %get-tuple-element.39), channel_id=1, source_target_pairs={{1,0},{2,1},{3,2},{7,3},{6,7},{5,6},{4,5},{8,4},{9,8},{10,9},{11,1... | collective-permute-start | bytes 473096 | tf_op jit(solution)/shard_map/ppermute | solution.py:416
  35.1 1.4 %collective-permute-done.3.before_ref = f32[308,128]{1,0:T(8,128)S(1)} collective-permute-done((f32[308,128]{1,0:T(8,128)S(1)}, f32[308,128]{1,0:T(8,128)S(1)}, u32[]{:S(2)}, u32[]{:S(2)}) %collective-permute-start.3) | collective-permute-done | bytes 157728 | tf_op jit(solution)/shard_map/ppermute | solution.py:415
  36.5 3.3 %collective-permute-done.4.after_ref = f32[308,128]{1,0:T(8,128)S(1)} collective-permute-done((f32[308,128]{1,0:T(8,128)S(1)}, f32[308,128]{1,0:T(8,128)S(1)}, u32[]{:S(2)}, u32[]{:S(2)}) %collective-permute-start.4) | collective-permute-done | bytes 157728 | tf_op jit(solution)/shard_map/ppermute | solution.py:416
  39.8 4.7 %shard_map.71 = (f32[36,8,128]{2,1,0:T(8,128)S(1)}, f32[36,8,128]{2,1,0:T(8,128)}, f32[36,8,128]{2,1,0:T(8,128)S(1)}, f32[36,8,128]{2,1,0:T(8,128)}, f32[288,8,1...) custom-call(s32[288]{0:T(512)S(1)} %maximum_convert_fusion.ranks_ref, ...), custom_call_target="tpu_custom_call" | custom-call | tf_op jit(solution)/shard_map/pallas_call | solution.py:326
  44.5 4.0 %collective-permute-start.8 = (f32[2,288,128]{2,1,0:T(8,128)}, f32[2,288,128]{2,1,0:T(8,128)S(1)}, u32[]{:S(2)}, u32[]{:S(2)}) collective-permute-start(f32[2,288,128]{2,1,0:T(8,128)} %get-tuple-element.45), channel_id=1, source_target_pairs={{0,1},{1,2},{2,3},{3,7},{7,6},{6,5},{5,4},{4,8},{8,9},{9,10},{10,1... | collective-permute-start | bytes 884744 | tf_op jit(solution)/shard_map/ppermute | solution.py:424
  49.8 2.7 %collective-permute-start.14 = (f32[36,8,128]{2,1,0:T(8,128)}, f32[36,8,128]{2,1,0:T(8,128)S(1)}, u32[]{:S(2)}, u32[]{:S(2)}) collective-permute-start(f32[36,8,128]{2,1,0:T(8,128)} %get-tuple-element.55), channel_id=1, source_target_pairs={{0,3},{1,0},{2,1},{3,2},{4,7},{5,4},{6,5},{7,6},{8,11},{9,8},{10,9... | collective-permute-start | bytes 442376 | tf_op jit(solution)/shard_map/ppermute | solution.py:383
  52.6 1.4 %collective-permute-start.10 = (f32[36,8,128]{2,1,0:T(8,128)S(1)}, f32[36,8,128]{2,1,0:T(8,128)S(1)}, u32[]{:S(2)}, u32[]{:S(2)}) collective-permute-start(f32[36,8,128]{2,1,0:T(8,128)S(1)} %get-tuple-element.49), channel_id=1, source_target_pairs={{0,2},{1,3},{2,0},{3,1},{4,6},{5,7},{6,4},{7,5},{8,10},{9,11},{10,... | collective-permute-start | bytes 442376 | tf_op jit(solution)/shard_map/ppermute | solution.py:383
  55.3 5.9 %collective-permute-done.9.after_ref = f32[2,288,128]{2,1,0:T(8,128)S(1)} collective-permute-done((f32[2,288,128]{2,1,0:T(8,128)S(1)}, f32[2,288,128]{2,1,0:T(8,128)S(1)}, u32[]{:S(2)}, u32[]{:S(2)}) %collective-permute-start.9) | collective-permute-done | bytes 294944 | tf_op jit(solution)/shard_map/ppermute | solution.py:425
  61.2 7.7 %shard_map.72 = (f32[72,8,128]{2,1,0:T(8,128)S(1)}, f32[72,8,128]{2,1,0:T(8,128)S(1)}, f32[72,8,128]{2,1,0:T(8,128)S(1)}, f32[72,8,128]{2,1,0:T(8,128)S(1)}, f32[35,128]{1,0:T(8,128)S(1)}) custom-call(s32[288]{0:T(512)S(1)} %maximum_convert_fusion.ranks_ref, s32[1]{0:T(128)} %bitcast.9.place_ref, f32[288,8,128]{2,1,0:T(8,128)S(1)} %get-tuple-element.44.v_ref, ...), custom_call_target="tpu_custom_call" | custom-call | tf_op jit(solution)/shard_map/pallas_call | solution.py:326
  69.8 3.0 %collective-permute-start.20 = (f32[72,8,128]{2,1,0:T(8,128)S(1)}, f32[72,8,128]{2,1,0:T(8,128)S(1)}, u32[]{:S(2)}, u32[]{:S(2)}) collective-permute-start(f32[72,8,128]{2,1,0:T(8,128)S(1)} %get-tuple-element.62), channel_id=1, source_target_pairs={{0,3},{1,0},{2,1},{3,2},{4,7},{5,4},{6,5},{7,6},{8,11},{9,8},{10,9... | collective-permute-start | bytes 884744 | tf_op jit(solution)/shard_map/ppermute | solution.py:383
  72.8 1.4 %collective-permute-start.12 = (f32[35,128]{1,0:T(8,128)S(1)}, f32[35,128]{1,0:T(8,128)S(1)}, u32[]{:S(2)}, u32[]{:S(2)}) collective-permute-start(f32[35,128]{1,0:T(8,128)S(1)} %add.60), channel_id=1, source_target_pairs={{0,8},{4,12},{8,0},{12,4},{16,24},{20,28},{24,16},{28,20},{1,9},{5... | collective-permute-start | bytes 53768 | tf_op jit(solution)/shard_map/ppermute | solution.py:340
  74.2 2.5 %collective-permute-done.12 = f32[35,128]{1,0:T(8,128)S(1)} collective-permute-done((f32[35,128]{1,0:T(8,128)S(1)}, f32[35,128]{1,0:T(8,128)S(1)}, u32[]{:S(2)}, u32[]{:S(2)}) %collective-permute-start.12) | collective-permute-done | bytes 17952 | tf_op jit(solution)/shard_map/ppermute | solution.py:340
  76.7 1.4 %collective-permute-start.13 = (f32[35,128]{1,0:T(8,128)S(1)}, f32[35,128]{1,0:T(8,128)S(1)}, u32[]{:S(2)}, u32[]{:S(2)}) collective-permute-start(f32[35,128]{1,0:T(8,128)S(1)} %add.61), channel_id=1, source_target_pairs={{0,16},{4,20},{8,24},{12,28},{16,0},{20,4},{24,8},{28,12},{1,17},{... | collective-permute-start | bytes 53768 | tf_op jit(solution)/shard_map/ppermute | solution.py:340
  78.1 2.4 %collective-permute-done.13 = f32[35,128]{1,0:T(8,128)S(1)} collective-permute-done((f32[35,128]{1,0:T(8,128)S(1)}, f32[35,128]{1,0:T(8,128)S(1)}, u32[]{:S(2)}, u32[]{:S(2)}) %collective-permute-start.13) | collective-permute-done | bytes 17952 | tf_op jit(solution)/shard_map/ppermute | solution.py:340
  80.5 2.9 %collective-permute-start.18 = (f32[32,128]{1,0:T(8,128)S(1)}, f32[32,128]{1,0:T(8,128)S(1)}, u32[]{:S(2)}, u32[]{:S(2)}) collective-permute-start(f32[32,128]{1,0:T(8,128)S(1)} %slice_add_fusion.refs_0_), channel_id=1, source_target_pairs={{0,2},{1,3},{2,0},{3,1},{4,6},{5,7},{6,4},{7,5},{8,10},{9,11},{10,... | collective-permute-start | bytes 49160 | tf_op jit(solution)/shard_map/ppermute | solution.py:383
  83.4 3.8 %collective-permute-start.17 = (f32[32,128]{1,0:T(8,128)S(1)}, f32[32,128]{1,0:T(8,128)S(1)}, u32[]{:S(2)}, u32[]{:S(2)}) collective-permute-start(f32[32,128]{1,0:T(8,128)S(1)} %slice_add_fusion.refs_0_), channel_id=1, source_target_pairs={{0,3},{1,0},{2,1},{3,2},{4,7},{5,4},{6,5},{7,6},{8,11},{9,8},{10,9... | collective-permute-start | bytes 49160 | tf_op jit(solution)/shard_map/ppermute | solution.py:383
  87.2 9.0 %collective-permute-done.18.refs_2_ = f32[32,128]{1,0:T(8,128)S(1)} collective-permute-done((f32[32,128]{1,0:T(8,128)S(1)}, f32[32,128]{1,0:T(8,128)S(1)}, u32[]{:S(2)}, u32[]{:S(2)}) %collective-permute-start.18) | collective-permute-done | bytes 16416 | tf_op jit(solution)/shard_map/ppermute | solution.py:383
  96.2 2.0 %shard_map.73 = (f32[72,16,128]{2,1,0:T(8,128)}, f32[72,16,128]{2,1,0:T(8,128)}) custom-call(s32[4]{0:T(128)S(1)} %pad_add_fusion.offsets_ref, f32[72,16,128]{2,1,0:T(8,128)S(1)} %copy-done.1, f32[32,128]{1,0:T(8,128)S(1)} %slice_add_fusion.refs_0_, f32[32,128]{1,0:T(8,128)S(1)} %collective-permute-done.17.refs_1_, ...), custom_call_target="tpu_custom_call" | custom-call | tf_op jit(solution)/shard_map/pallas_call | solution.py:326
  (51 shorter events, 11.8 us)
Async XLA Ops:
  0.6 14.2 %copy-start.5 = (f32[16,128]{1,0:T(8,128)S(1)}, f32[16,128]{1,0:T(8,128)}, u32[]{:S(2)}) copy-start(f32[16,128]{1,0:T(8,128)} %param.8) | copy-start | bytes 24580
  3.2 16.9 %collective-permute-start.1 = (f32[38,8,128]{2,1,0:T(8,128)S(1)}, f32[38,8,128]{2,1,0:T(8,128)S(1)}, u32[]{:S(2)}, u32[]{:S(2)}) collective-permute-start(f32[38,8,128]{2,1,0:T(8,128)S(1)} %get-tuple-element.35), channel_id=1, source_target_pairs={{0,2},{1,3},{2,0},{3,1},{4,6},{5,7},{6,4},{7,5},{8,10},{9,11},{10,... | collective-permute-start | bytes 466952 | tf_op jit(solution)/shard_map/ppermute | solution.py:383
  7.3 7.7 %collective-permute-start.2 = (f32[37,8,128]{2,1,0:T(8,128)S(1)}, f32[37,8,128]{2,1,0:T(8,128)S(1)}, u32[]{:S(2)}, u32[]{:S(2)}) collective-permute-start(f32[37,8,128]{2,1,0:T(8,128)S(1)} %get-tuple-element.36), channel_id=1, source_target_pairs={{0,3},{1,0},{2,1},{3,2},{4,7},{5,4},{6,5},{7,6},{8,11},{9,8},{10,9... | collective-permute-start | bytes 454664 | tf_op jit(solution)/shard_map/ppermute | solution.py:383
  8.7 11.5 %collective-permute-start = (f32[37,8,128]{2,1,0:T(8,128)S(1)}, f32[37,8,128]{2,1,0:T(8,128)S(1)}, u32[]{:S(2)}, u32[]{:S(2)}) collective-permute-start(f32[37,8,128]{2,1,0:T(8,128)S(1)} %get-tuple-element.34), channel_id=1, source_target_pairs={{0,1},{1,2},{2,3},{3,0},{4,5},{5,6},{6,7},{7,4},{8,9},{9,10},{10,1... | collective-permute-start | bytes 454664 | tf_op jit(solution)/shard_map/ppermute | solution.py:383
  11.1 22.8 %collective-permute-start.5 = (f32[39,8,128]{2,1,0:T(8,128)S(1)}, f32[39,8,128]{2,1,0:T(8,128)S(1)}, u32[]{:S(2)}, u32[]{:S(2)}) collective-permute-start(f32[39,8,128]{2,1,0:T(8,128)S(1)} %get-tuple-element.41), channel_id=1, source_target_pairs={{0,1},{1,2},{2,3},{3,0},{4,5},{5,6},{6,7},{7,4},{8,9},{9,10},{10,1... | collective-permute-start | bytes 479240 | tf_op jit(solution)/shard_map/ppermute | solution.py:383
  12.7 21.2 %collective-permute-start.6 = (f32[39,8,128]{2,1,0:T(8,128)S(1)}, f32[39,8,128]{2,1,0:T(8,128)S(1)}, u32[]{:S(2)}, u32[]{:S(2)}) collective-permute-start(f32[39,8,128]{2,1,0:T(8,128)S(1)} %get-tuple-element.42), channel_id=1, source_target_pairs={{0,2},{1,3},{2,0},{3,1},{4,6},{5,7},{6,4},{7,5},{8,10},{9,11},{10,... | collective-permute-start | bytes 479240 | tf_op jit(solution)/shard_map/ppermute | solution.py:383
  15.1 20.0 %collective-permute-start.7 = (f32[39,8,128]{2,1,0:T(8,128)S(1)}, f32[39,8,128]{2,1,0:T(8,128)S(1)}, u32[]{:S(2)}, u32[]{:S(2)}) collective-permute-start(f32[39,8,128]{2,1,0:T(8,128)S(1)} %get-tuple-element.43), channel_id=1, source_target_pairs={{0,3},{1,0},{2,1},{3,2},{4,7},{5,4},{6,5},{7,6},{8,11},{9,8},{10,9... | collective-permute-start | bytes 479240 | tf_op jit(solution)/shard_map/ppermute | solution.py:383
  21.4 15.1 %collective-permute-start.3 = (f32[308,128]{1,0:T(8,128)S(1)}, f32[308,128]{1,0:T(8,128)S(1)}, u32[]{:S(2)}, u32[]{:S(2)}) collective-permute-start(f32[308,128]{1,0:T(8,128)S(1)} %get-tuple-element.38), channel_id=1, source_target_pairs={{0,1},{1,2},{2,3},{3,7},{7,6},{6,5},{5,4},{4,8},{8,9},{9,10},{10,1... | collective-permute-start | bytes 473096 | tf_op jit(solution)/shard_map/ppermute | solution.py:415
  32.6 7.2 %collective-permute-start.4 = (f32[308,128]{1,0:T(8,128)S(1)}, f32[308,128]{1,0:T(8,128)S(1)}, u32[]{:S(2)}, u32[]{:S(2)}) collective-permute-start(f32[308,128]{1,0:T(8,128)S(1)} %get-tuple-element.39), channel_id=1, source_target_pairs={{1,0},{2,1},{3,2},{7,3},{6,7},{5,6},{4,5},{8,4},{9,8},{10,9},{11,1... | collective-permute-start | bytes 473096 | tf_op jit(solution)/shard_map/ppermute | solution.py:416
  44.5 51.7 %copy-start.1 = (f32[72,16,128]{2,1,0:T(8,128)S(1)}, f32[72,16,128]{2,1,0:T(8,128)}, u32[]{:S(2)}) copy-start(f32[72,16,128]{2,1,0:T(8,128)} %x_ref.1) | copy-start | bytes 1769476
  44.5 10.7 %collective-permute-start.8 = (f32[2,288,128]{2,1,0:T(8,128)}, f32[2,288,128]{2,1,0:T(8,128)S(1)}, u32[]{:S(2)}, u32[]{:S(2)}) collective-permute-start(f32[2,288,128]{2,1,0:T(8,128)} %get-tuple-element.45), channel_id=1, source_target_pairs={{0,1},{1,2},{2,3},{3,7},{7,6},{6,5},{5,4},{4,8},{8,9},{9,10},{10,1... | collective-permute-start | bytes 884744 | tf_op jit(solution)/shard_map/ppermute | solution.py:424
  48.5 12.6 %collective-permute-start.9 = (f32[2,288,128]{2,1,0:T(8,128)S(1)}, f32[2,288,128]{2,1,0:T(8,128)S(1)}, u32[]{:S(2)}, u32[]{:S(2)}) collective-permute-start(f32[2,288,128]{2,1,0:T(8,128)S(1)} %get-tuple-element.46), channel_id=1, source_target_pairs={{1,0},{2,1},{3,2},{7,3},{6,7},{5,6},{4,5},{8,4},{9,8},{10,9},{11,1... | collective-permute-start | bytes 884744 | tf_op jit(solution)/shard_map/ppermute | solution.py:425
  49.8 19.1 %collective-permute-start.14 = (f32[36,8,128]{2,1,0:T(8,128)}, f32[36,8,128]{2,1,0:T(8,128)S(1)}, u32[]{:S(2)}, u32[]{:S(2)}) collective-permute-start(f32[36,8,128]{2,1,0:T(8,128)} %get-tuple-element.55), channel_id=1, source_target_pairs={{0,3},{1,0},{2,1},{3,2},{4,7},{5,4},{6,5},{7,6},{8,11},{9,8},{10,9... | collective-permute-start | bytes 442376 | tf_op jit(solution)/shard_map/ppermute | solution.py:383
  52.6 16.4 %collective-permute-start.15 = (f32[36,8,128]{2,1,0:T(8,128)}, f32[36,8,128]{2,1,0:T(8,128)S(1)}, u32[]{:S(2)}, u32[]{:S(2)}) collective-permute-start(f32[36,8,128]{2,1,0:T(8,128)} %get-tuple-element.56), channel_id=1, source_target_pairs={{0,1},{1,2},{2,3},{3,0},{4,5},{5,6},{6,7},{7,4},{8,9},{9,10},{10,1... | collective-permute-start | bytes 442376 | tf_op jit(solution)/shard_map/ppermute | solution.py:383
  52.6 17.2 %collective-permute-start.10 = (f32[36,8,128]{2,1,0:T(8,128)S(1)}, f32[36,8,128]{2,1,0:T(8,128)S(1)}, u32[]{:S(2)}, u32[]{:S(2)}) collective-permute-start(f32[36,8,128]{2,1,0:T(8,128)S(1)} %get-tuple-element.49), channel_id=1, source_target_pairs={{0,2},{1,3},{2,0},{3,1},{4,6},{5,7},{6,4},{7,5},{8,10},{9,11},{10,... | collective-permute-start | bytes 442376 | tf_op jit(solution)/shard_map/ppermute | solution.py:383
  68.9 14.5 %collective-permute-start.16 = (f32[72,8,128]{2,1,0:T(8,128)S(1)}, f32[72,8,128]{2,1,0:T(8,128)S(1)}, u32[]{:S(2)}, u32[]{:S(2)}) collective-permute-start(f32[72,8,128]{2,1,0:T(8,128)S(1)} %get-tuple-element.57), channel_id=1, source_target_pairs={{0,1},{1,2},{2,3},{3,0},{4,5},{5,6},{6,7},{7,4},{8,9},{9,10},{10,1... | collective-permute-start | bytes 884744 | tf_op jit(solution)/shard_map/ppermute | solution.py:383
  69.8 3.0 %collective-permute-start.11 = (f32[35,128]{1,0:T(8,128)S(1)}, f32[35,128]{1,0:T(8,128)S(1)}, u32[]{:S(2)}, u32[]{:S(2)}) collective-permute-start(f32[35,128]{1,0:T(8,128)S(1)} %get-tuple-element.50), channel_id=1, source_target_pairs={{0,4},{4,0},{8,12},{12,8},{16,20},{20,16},{24,28},{28,24},{1,5},{5... | collective-permute-start | bytes 53768 | tf_op jit(solution)/shard_map/ppermute | solution.py:340
  69.8 26.4 %collective-permute-start.20 = (f32[72,8,128]{2,1,0:T(8,128)S(1)}, f32[72,8,128]{2,1,0:T(8,128)S(1)}, u32[]{:S(2)}, u32[]{:S(2)}) collective-permute-start(f32[72,8,128]{2,1,0:T(8,128)S(1)} %get-tuple-element.62), channel_id=1, source_target_pairs={{0,3},{1,0},{2,1},{3,2},{4,7},{5,4},{6,5},{7,6},{8,11},{9,8},{10,9... | collective-permute-start | bytes 884744 | tf_op jit(solution)/shard_map/ppermute | solution.py:383
  72.8 23.4 %collective-permute-start.21 = (f32[72,8,128]{2,1,0:T(8,128)S(1)}, f32[72,8,128]{2,1,0:T(8,128)S(1)}, u32[]{:S(2)}, u32[]{:S(2)}) collective-permute-start(f32[72,8,128]{2,1,0:T(8,128)S(1)} %get-tuple-element.63), channel_id=1, source_target_pairs={{0,2},{1,3},{2,0},{3,1},{4,6},{5,7},{6,4},{7,5},{8,10},{9,11},{10,... | collective-permute-start | bytes 884744 | tf_op jit(solution)/shard_map/ppermute | solution.py:383
  72.8 3.8 %collective-permute-start.12 = (f32[35,128]{1,0:T(8,128)S(1)}, f32[35,128]{1,0:T(8,128)S(1)}, u32[]{:S(2)}, u32[]{:S(2)}) collective-permute-start(f32[35,128]{1,0:T(8,128)S(1)} %add.60), channel_id=1, source_target_pairs={{0,8},{4,12},{8,0},{12,4},{16,24},{20,28},{24,16},{28,20},{1,9},{5... | collective-permute-start | bytes 53768 | tf_op jit(solution)/shard_map/ppermute | solution.py:340
  76.7 3.8 %collective-permute-start.13 = (f32[35,128]{1,0:T(8,128)S(1)}, f32[35,128]{1,0:T(8,128)S(1)}, u32[]{:S(2)}, u32[]{:S(2)}) collective-permute-start(f32[35,128]{1,0:T(8,128)S(1)} %add.61), channel_id=1, source_target_pairs={{0,16},{4,20},{8,24},{12,28},{16,0},{20,4},{24,8},{28,12},{1,17},{... | collective-permute-start | bytes 53768 | tf_op jit(solution)/shard_map/ppermute | solution.py:340
  80.5 15.7 %collective-permute-start.18 = (f32[32,128]{1,0:T(8,128)S(1)}, f32[32,128]{1,0:T(8,128)S(1)}, u32[]{:S(2)}, u32[]{:S(2)}) collective-permute-start(f32[32,128]{1,0:T(8,128)S(1)} %slice_add_fusion.refs_0_), channel_id=1, source_target_pairs={{0,2},{1,3},{2,0},{3,1},{4,6},{5,7},{6,4},{7,5},{8,10},{9,11},{10,... | collective-permute-start | bytes 49160 | tf_op jit(solution)/shard_map/ppermute | solution.py:383
  83.4 12.8 %collective-permute-start.19 = (f32[32,128]{1,0:T(8,128)S(1)}, f32[32,128]{1,0:T(8,128)S(1)}, u32[]{:S(2)}, u32[]{:S(2)}) collective-permute-start(f32[32,128]{1,0:T(8,128)S(1)} %slice_add_fusion.refs_0_), channel_id=1, source_target_pairs={{0,1},{1,2},{2,3},{3,0},{4,5},{5,6},{6,7},{7,4},{8,9},{9,10},{10,1... | collective-permute-start | bytes 49160 | tf_op jit(solution)/shard_map/ppermute | solution.py:383
  83.4 12.8 %collective-permute-start.17 = (f32[32,128]{1,0:T(8,128)S(1)}, f32[32,128]{1,0:T(8,128)S(1)}, u32[]{:S(2)}, u32[]{:S(2)}) collective-permute-start(f32[32,128]{1,0:T(8,128)S(1)} %slice_add_fusion.refs_0_), channel_id=1, source_target_pairs={{0,3},{1,0},{2,1},{3,2},{4,7},{5,4},{6,5},{7,6},{8,11},{9,8},{10,9... | collective-permute-start | bytes 49160 | tf_op jit(solution)/shard_map/ppermute | solution.py:383
  (4 other events, 17.0 us)
